TPU v7x, 128 devices: a whole 4x4x4 slice. The times are simulated.
128 devices in a mesh: fsdp: 16 (over x_lo, y, core), seq: 8 (over x_hi, z).
Axes of the slice: x: 4 (x_hi: 2, x_lo: 2; x = x_hi * 2 + x_lo), y: 4, z: 4, core: 2. Of those that a mesh axis runs over, the one named last changes fastest.
Arguments:
- latents: bfloat16 [32, 1024, 384], P('fsdp', 'seq'), may hold values from -6 to 6
- modulation: float32 [32, 2304], P('fsdp'), may hold values from -3 to 3
- w_qkv: bfloat16 [384, 1152], P(('fsdp', 'seq')), may hold values from -0.3125 to 0.3125
- b_query: bfloat16 [384], P(('fsdp', 'seq')), may hold values from -3 to 3
- b_value: bfloat16 [384], P(('fsdp', 'seq')), may hold values from -0.59765625 to 0.59765625
- w_out: bfloat16 [384, 384], P(('fsdp', 'seq')), may hold values from -2.5 to 2.5
- b_out: bfloat16 [384], P(('fsdp', 'seq')), may hold values from -2 to 2
- w_fc1: bfloat16 [384, 1536], P(('fsdp', 'seq')), may hold values from -0.3125 to 0.3125
- b_fc1: bfloat16 [1536], P(('fsdp', 'seq')), may hold values from -3 to 3
- w_fc2: bfloat16 [1536, 384], P(('fsdp', 'seq')), may hold values from -0.15625 to 0.15625
- b_fc2: bfloat16 [384], P(('fsdp', 'seq')), may hold values from -2 to 2
- cotangent: bfloat16 [32, 1024, 384], P('fsdp', 'seq'), may hold values from -6 to 6
Outputs:
- output: bfloat16 [32, 1024, 384], P('fsdp', 'seq')
- input_grad: bfloat16 [32, 1024, 384], P('fsdp', 'seq')
- modulation_grad: float32 [32, 2304], P('fsdp')
- grad_qkv: float32 [384, 1152], P(('fsdp', 'seq'))
- grad_query_bias: float32 [384], P(('fsdp', 'seq'))
- grad_value_bias: float32 [384], P(('fsdp', 'seq'))
- grad_out: float32 [384, 384], P(('fsdp', 'seq'))
- grad_out_bias: float32 [384], P(('fsdp', 'seq'))
- grad_fc1: float32 [384, 1536], P(('fsdp', 'seq'))
- grad_fc1_bias: float32 [1536], P(('fsdp', 'seq'))
- grad_fc2: float32 [1536, 384], P(('fsdp', 'seq'))
- grad_fc2_bias: float32 [384], P(('fsdp', 'seq'))
All inputs are finite; a program needn't handle non-finite values.
Results may differ from a plain program's by a relative error of at most 0.018.
Values may be sent and summed in bfloat16 or wider, within the bound.
No kernel may reach another device: no remote copies, remote signals or barrier semaphores. Data moves between devices by JAX's collectives and lax.ppermute only.
A program may use at most 64 MiB of HBM per device.

v0:
```python
import jax
import jax.numpy as jnp
from jax import lax
from jax.sharding import PartitionSpec as P

HEADS = 6
MICRO = 2


EPSILON = 1e-06


def layer_norm(values):
    center = values - jnp.mean(values, axis=-1, keepdims=True)
    inverse = lax.rsqrt(jnp.mean(center * center, axis=-1, keepdims=True) + EPSILON)
    return (center * inverse, inverse)


def norm_back(grad_normed, normed, inverse):
    first = jnp.mean(grad_normed, axis=-1, keepdims=True)
    second = jnp.mean(grad_normed * normed, axis=-1, keepdims=True)
    return inverse * (grad_normed - first - normed * second)


def left_t(left, right):
    return lax.dot_general(
        left, right, (((0,), (0,)), ((), ())), preferred_element_type=jnp.float32
    )


def right_t(left, right):
    return lax.dot_general(
        left, right, (((1,), (1,)), ((), ())), preferred_element_type=jnp.float32
    )


def gelu_tanh(values):
    return jax.nn.gelu(values, approximate=True)


def head_split(array, latent_count):
    return array.reshape(latent_count, -1, HEADS, array.shape[-1] // HEADS)


def attend_forward(inputs):
    query, keys, values = inputs
    scale = query.shape[-1] ** (-0.5)
    scores = jnp.einsum("qhd,khd->hqk", query, keys, preferred_element_type=jnp.float32) * scale
    top = jnp.max(scores, axis=-1, keepdims=True)
    exponent = jnp.exp(scores - top)
    total = jnp.sum(exponent, axis=-1, keepdims=True)
    probability = (exponent / total).astype(jnp.bfloat16)
    attended = jnp.einsum("hqk,khd->qhd", probability, values, preferred_element_type=jnp.float32)
    return (attended, (top + jnp.log(total))[..., 0])


def attend_backward(inputs):
    query, keys, values, logsum, grad_attended = inputs
    scale = query.shape[-1] ** (-0.5)
    scores = jnp.einsum("qhd,khd->hqk", query, keys, preferred_element_type=jnp.float32) * scale
    probability = jnp.exp(scores - logsum[..., None])
    grad_values = jnp.einsum(
        "hqk,qhd->khd",
        probability.astype(jnp.bfloat16),
        grad_attended,
        preferred_element_type=jnp.float32,
    )
    grad_probability = jnp.einsum(
        "qhd,khd->hqk", grad_attended, values, preferred_element_type=jnp.float32
    )
    weighted = jnp.sum(probability * grad_probability, axis=-1, keepdims=True)
    grad_scores = (probability * (grad_probability - weighted)).astype(jnp.bfloat16)
    grad_query = (
        jnp.einsum("hqk,khd->qhd", grad_scores, keys, preferred_element_type=jnp.float32) * scale
    ).astype(jnp.bfloat16)
    grad_keys = (
        jnp.einsum("hqk,qhd->khd", grad_scores, query, preferred_element_type=jnp.float32) * scale
    )
    return (grad_query, grad_keys, grad_values)


def body(
    latents,
    modulation,
    w_qkv,
    b_query,
    b_value,
    w_out,
    b_out,
    w_fc1,
    b_fc1,
    w_fc2,
    b_fc2,
    cotangent,
):
    shards = (w_qkv, b_query, b_value, w_out, b_out, w_fc1, b_fc1, w_fc2, b_fc2)
    count, tokens, width = latents.shape
    per_micro = count // MICRO
    rows = per_micro * tokens
    saved = []
    outputs = []
    for micro_index in range(MICRO):
        weights = (
            lax.all_gather(shards[0], ("fsdp", "seq"), axis=0, tiled=True),
            lax.all_gather(shards[1], ("fsdp", "seq"), axis=0, tiled=True),
            lax.all_gather(shards[2], ("fsdp", "seq"), axis=0, tiled=True),
            lax.all_gather(shards[3], ("fsdp", "seq"), axis=0, tiled=True),
            lax.all_gather(shards[4], ("fsdp", "seq"), axis=0, tiled=True),
            lax.all_gather(shards[5], ("fsdp", "seq"), axis=0, tiled=True),
            lax.all_gather(shards[6], ("fsdp", "seq"), axis=0, tiled=True),
            lax.all_gather(shards[7], ("fsdp", "seq"), axis=0, tiled=True),
            lax.all_gather(shards[8], ("fsdp", "seq"), axis=0, tiled=True),
        )
        (
            full_qkv,
            bias_query,
            bias_value,
            full_out,
            bias_out,
            full_fc1,
            bias_fc1,
            full_fc2,
            bias_fc2,
        ) = weights
        lower = micro_index * per_micro
        inputs = latents[lower : lower + per_micro].astype(jnp.float32)
        condition = modulation[lower : lower + per_micro][:, None, :]
        pieces = [condition[..., index * width : (index + 1) * width] for index in range(6)]
        normed, inverse = layer_norm(inputs)
        hidden = (normed * (1.0 + pieces[1]) + pieces[0]).astype(jnp.bfloat16).reshape(rows, width)
        projected = jnp.dot(hidden, full_qkv, preferred_element_type=jnp.float32)
        query = (
            (projected[:, :width] + bias_query)
            .astype(jnp.bfloat16)
            .reshape(per_micro, tokens, width)
        )
        keys = (
            projected[:, width : 2 * width].astype(jnp.bfloat16).reshape(per_micro, tokens, width)
        )
        values = (
            (projected[:, 2 * width :] + bias_value)
            .astype(jnp.bfloat16)
            .reshape(per_micro, tokens, width)
        )
        all_keys, all_values = (
            lax.all_gather(keys, "seq", axis=1, tiled=True),
            lax.all_gather(values, "seq", axis=1, tiled=True),
        )
        kept_query = head_split(query, per_micro)
        kept_keys = head_split(all_keys, per_micro)
        kept_values = head_split(all_values, per_micro)
        attended, logsum = lax.map(attend_forward, (kept_query, kept_keys, kept_values))
        attended = attended.reshape(rows, width).astype(jnp.bfloat16)
        branch = (
            jnp.dot(attended, full_out, preferred_element_type=jnp.float32) + bias_out
        ).reshape(per_micro, tokens, width)
        middle = inputs + pieces[2] * branch
        normed_two, inverse_two = layer_norm(middle)
        hidden_two = (
            (normed_two * (1.0 + pieces[4]) + pieces[3]).astype(jnp.bfloat16).reshape(rows, width)
        )
        inner = jnp.dot(hidden_two, full_fc1, preferred_element_type=jnp.float32) + bias_fc1
        active = gelu_tanh(inner).astype(jnp.bfloat16)
        branch_two = (
            jnp.dot(active, full_fc2, preferred_element_type=jnp.float32) + bias_fc2
        ).reshape(per_micro, tokens, width)
        outputs.append((middle + pieces[5] * branch_two).astype(jnp.bfloat16))
        saved.append(
            (
                pieces,
                normed,
                inverse,
                hidden,
                kept_query,
                kept_keys,
                kept_values,
                logsum,
                attended,
                branch,
                normed_two,
                inverse_two,
                hidden_two,
                inner,
                active,
                branch_two,
            )
        )
    accumulated = None
    grad_shards = None
    input_grads = []
    condition_grads = []
    for micro_index in range(MICRO):
        weights = (
            lax.all_gather(shards[0], ("fsdp", "seq"), axis=0, tiled=True),
            lax.all_gather(shards[1], ("fsdp", "seq"), axis=0, tiled=True),
            lax.all_gather(shards[2], ("fsdp", "seq"), axis=0, tiled=True),
            lax.all_gather(shards[3], ("fsdp", "seq"), axis=0, tiled=True),
            lax.all_gather(shards[4], ("fsdp", "seq"), axis=0, tiled=True),
            lax.all_gather(shards[5], ("fsdp", "seq"), axis=0, tiled=True),
            lax.all_gather(shards[6], ("fsdp", "seq"), axis=0, tiled=True),
            lax.all_gather(shards[7], ("fsdp", "seq"), axis=0, tiled=True),
            lax.all_gather(shards[8], ("fsdp", "seq"), axis=0, tiled=True),
        )
        (
            full_qkv,
            bias_query,
            bias_value,
            full_out,
            bias_out,
            full_fc1,
            bias_fc1,
            full_fc2,
            bias_fc2,
        ) = weights
        (
            pieces,
            normed,
            inverse,
            hidden,
            kept_query,
            kept_keys,
            kept_values,
            logsum,
            attended,
            branch,
            normed_two,
            inverse_two,
            hidden_two,
            inner,
            active,
            branch_two,
        ) = saved[micro_index]
        lower = micro_index * per_micro
        upstream = cotangent[lower : lower + per_micro].astype(jnp.float32)
        grad_gate_two = jnp.sum(upstream * branch_two, axis=1)
        grad_branch_two = (upstream * pieces[5]).astype(jnp.bfloat16).reshape(rows, width)
        grad_fc2 = left_t(active, grad_branch_two)
        grad_fc2_bias = jnp.sum(grad_branch_two.astype(jnp.float32), axis=0)
        grad_active = right_t(grad_branch_two, full_fc2)
        pullback = jax.vjp(gelu_tanh, inner)[1]
        grad_inner = pullback(grad_active)[0].astype(jnp.bfloat16)
        grad_fc1 = left_t(hidden_two, grad_inner)
        grad_fc1_bias = jnp.sum(grad_inner.astype(jnp.float32), axis=0)
        grad_hidden_two = right_t(grad_inner, full_fc1).reshape(per_micro, tokens, width)
        grad_scale_two = jnp.sum(grad_hidden_two * normed_two, axis=1)
        grad_shift_two = jnp.sum(grad_hidden_two, axis=1)
        grad_middle = upstream + norm_back(
            grad_hidden_two * (1.0 + pieces[4]), normed_two, inverse_two
        )
        grad_gate_one = jnp.sum(grad_middle * branch, axis=1)
        grad_branch = (grad_middle * pieces[2]).astype(jnp.bfloat16).reshape(rows, width)
        grad_out = left_t(attended, grad_branch)
        grad_out_bias = jnp.sum(grad_branch.astype(jnp.float32), axis=0)
        grad_attended = right_t(grad_branch, full_out).astype(jnp.bfloat16)
        grad_query, key_parts, value_parts = lax.map(
            attend_backward,
            (kept_query, kept_keys, kept_values, logsum, head_split(grad_attended, per_micro)),
        )
        length = kept_keys.shape[1]
        key_parts = key_parts.reshape(per_micro, length, width)
        value_parts = value_parts.reshape(per_micro, length, width)
        grad_keys, grad_values = (
            lax.psum_scatter(
                key_parts.astype(jnp.bfloat16), "seq", scatter_dimension=1, tiled=True
            ).astype(jnp.float32),
            lax.psum_scatter(
                value_parts.astype(jnp.bfloat16), "seq", scatter_dimension=1, tiled=True
            ).astype(jnp.float32),
        )
        grad_query = grad_query.reshape(rows, width)
        grad_keys = grad_keys.astype(jnp.bfloat16).reshape(rows, width)
        grad_values = grad_values.astype(jnp.bfloat16).reshape(rows, width)
        grad_projected = jnp.concatenate([grad_query, grad_keys, grad_values], axis=1)
        grad_qkv = left_t(hidden, grad_projected)
        grad_query_bias = jnp.sum(grad_query.astype(jnp.float32), axis=0)
        grad_value_bias = jnp.sum(grad_values.astype(jnp.float32), axis=0)
        grad_hidden = right_t(grad_projected, full_qkv).reshape(per_micro, tokens, width)
        grad_scale_one = jnp.sum(grad_hidden * normed, axis=1)
        grad_shift_one = jnp.sum(grad_hidden, axis=1)
        grad_inputs = grad_middle + norm_back(grad_hidden * (1.0 + pieces[1]), normed, inverse)
        input_grads.append(grad_inputs.astype(jnp.bfloat16))
        condition_grads.append(
            jnp.concatenate(
                [
                    grad_shift_one,
                    grad_scale_one,
                    grad_gate_one,
                    grad_shift_two,
                    grad_scale_two,
                    grad_gate_two,
                ],
                axis=1,
            )
        )
        local_grads = (
            grad_qkv,
            grad_query_bias,
            grad_value_bias,
            grad_out,
            grad_out_bias,
            grad_fc1,
            grad_fc1_bias,
            grad_fc2,
            grad_fc2_bias,
        )
        accumulated = (
            local_grads if accumulated is None else jax.tree.map(jnp.add, accumulated, local_grads)
        )
    grad_shards = lax.psum_scatter(accumulated, ("fsdp", "seq"), scatter_dimension=0, tiled=True)
    modulation_grad = lax.psum(jnp.concatenate(condition_grads, axis=0), "seq")
    output = jnp.concatenate(outputs, axis=0)
    input_grad = jnp.concatenate(input_grads, axis=0)
    return (
        output,
        input_grad,
        modulation_grad,
        grad_shards[0],
        grad_shards[1],
        grad_shards[2],
        grad_shards[3],
        grad_shards[4],
        grad_shards[5],
        grad_shards[6],
        grad_shards[7],
        grad_shards[8],
    )


def solution(mesh):
    in_specs = (
        P("fsdp", "seq", None),
        P("fsdp", None),
        P(("fsdp", "seq"), None),
        P(("fsdp", "seq")),
        P(("fsdp", "seq")),
        P(("fsdp", "seq"), None),
        P(("fsdp", "seq")),
        P(("fsdp", "seq"), None),
        P(("fsdp", "seq")),
        P(("fsdp", "seq"), None),
        P(("fsdp", "seq")),
        P("fsdp", "seq", None),
    )
    out_specs = (
        P("fsdp", "seq", None),
        P("fsdp", "seq", None),
        P("fsdp", None),
        P(("fsdp", "seq"), None),
        P(("fsdp", "seq")),
        P(("fsdp", "seq")),
        P(("fsdp", "seq"), None),
        P(("fsdp", "seq")),
        P(("fsdp", "seq"), None),
        P(("fsdp", "seq")),
        P(("fsdp", "seq"), None),
        P(("fsdp", "seq")),
    )
    return jax.shard_map(body, mesh=mesh, in_specs=in_specs, out_specs=out_specs, check_vma=False)
```

profile of v0, /device:TPU:8, one launch (start us, length us, event | category | flops | bytes accessed | tf_op | source)
XLA Modules:
  0.0 1753.1 jit_solution(16370230416431234148)
XLA Ops:
  12.3 293.1 %all-gather.4 = bf16[128,3,1152]{2,1,0:T(4,128)(2,1)S(1)} all-gather(bf16[1,3,1152]{2,1,0:T(4,128)(2,1)} %bitcast.280), channel_id=1, replica_groups=mesh['fsdp'=16,'seq'=8] {'fsdp','seq'}, dimensions={0}, use_global_device_ids=true | all-gather | bytes 891648 | tf_op jit(solution)/shard_map/all_gather | solution.py:104
  307.4 91.3 %all-reduce.17 = (bf16[1536]{0:T(1024)(128)(2,1)S(1)}, bf16[384]{0:T(512)(128)(2,1)S(1)}, bf16[384]{0:T(512)(128)(2,1)S(1)}, bf16[384]{0:T(512)(128)(2,1)S(1)}, bf16[384]{0:T(512)(128)(2,1)}) all-reduce(bf16[1536]{0:T(1024)(128)(2,1)S(1)} %dynamic-update-slice.3, ...), channel_id=1, replica_groups=mesh['fsdp'=16,'seq'=8] {'fsdp','seq'}, use_global_device_ids=true, to_apply=%add.3 | all-reduce | flops 3072 | bytes 12288
  400.1 35.7 %all-gather.1 = bf16[1024,384]{1,0:T(8,128)(2,1)S(1)} all-gather(bf16[128,384]{1,0:T(8,128)(2,1)S(1)} %slice.190), channel_id=3, replica_groups=mesh['fsdp'=16,'seq'=8] {'seq'}, dimensions={0}, use_global_device_ids=true | all-gather | bytes 884736 | tf_op jit(solution)/shard_map/all_gather | solution.py:146
  437.1 35.7 %all-gather = bf16[1024,384]{1,0:T(8,128)(2,1)S(1)} all-gather(bf16[128,384]{1,0:T(8,128)(2,1)S(1)} %get-tuple-element.163), channel_id=2, replica_groups=mesh['fsdp'=16,'seq'=8] {'seq'}, dimensions={0}, use_global_device_ids=true | all-gather | bytes 884736 | tf_op jit(solution)/shard_map/all_gather | solution.py:147
  474.1 283.4 %all-gather.5 = bf16[128,3,384]{2,1,0:T(4,128)(2,1)S(1)} all-gather(bf16[1,3,384]{2,1,0:T(4,128)(2,1)S(1)} %bitcast.281), channel_id=1, replica_groups=mesh['fsdp'=16,'seq'=8] {'fsdp','seq'}, dimensions={0}, use_global_device_ids=true | all-gather | bytes 297216 | tf_op jit(solution)/shard_map/all_gather | solution.py:107
  787.3 4.8 copy.56
  796.4 5.0 copy.58
  816.1 77.1 %reduce-scatter.15.cloned.1.call-done = bf16[128,384]{1,0:T(8,128)(2,1)} async-done(((bf16[1024,384]{1,0:T(8,128)(2,1)}), bf16[128,384]{1,0:T(8,128)(2,1)}) %reduce-scatter.15.cloned.1.call-update) | async-done | bytes 98320
  894.4 73.2 %reduce-scatter.17.cloned.1.call-done = bf16[128,384]{1,0:T(8,128)(2,1)} async-done(((bf16[1024,384]{1,0:T(8,128)(2,1)}), bf16[128,384]{1,0:T(8,128)(2,1)}) %reduce-scatter.17.cloned.1.call-update) | async-done | bytes 98320
  970.3 35.9 %all-gather.3 = bf16[1024,384]{1,0:T(8,128)(2,1)S(1)} all-gather(bf16[128,384]{1,0:T(8,128)(2,1)S(1)} %slice.189), channel_id=5, replica_groups=mesh['fsdp'=16,'seq'=8] {'seq'}, dimensions={0}, use_global_device_ids=true | all-gather | bytes 884736 | tf_op jit(solution)/shard_map/all_gather | solution.py:146
  1007.6 35.6 %all-gather.2 = bf16[1024,384]{1,0:T(8,128)(2,1)S(1)} all-gather(bf16[128,384]{1,0:T(8,128)(2,1)S(1)} %get-tuple-element.161), channel_id=4, replica_groups=mesh['fsdp'=16,'seq'=8] {'seq'}, dimensions={0}, use_global_device_ids=true | all-gather | bytes 884736 | tf_op jit(solution)/shard_map/all_gather | solution.py:147
  1054.2 316.5 %fusion = f32[16,384]{1,0:T(8,128)} fusion(f32[1536,384]{1,0:T(8,128)} %convolution_add_fusion.1), kind=kCustom, calls=%all-reduce-scatter | all-reduce-scatter fusion | flops 786433 | bytes 2383872
  1397.9 4.8 copy.62
  1424.7 6.8 collective-permute-start.12
  1431.6 8.5 collective-permute-start.13
  1440.1 8.2 collective-permute-start.14
  1448.3 7.3 collective-permute-start.15
  1455.6 15.9 collective-permute-start.16
  1474.9 6.4 collective-permute-start.18
  1538.9 8.0 concatenate.28
  1548.1 32.4 %reduce-scatter.19.cloned.1.call-done = bf16[128,384]{1,0:T(8,128)(2,1)} async-done(((bf16[1024,384]{1,0:T(8,128)(2,1)}), bf16[128,384]{1,0:T(8,128)(2,1)}) %reduce-scatter.19.cloned.1.call-update) | async-done | bytes 98320
  1585.0 63.4 %all-reduce.15 = (f32[384]{0:T(512)S(1)}, f32[384]{0:T(512)S(1)}, f32[384]{0:T(512)S(1)}, f32[1536]{0:T(1024)S(1)}, f32[384]{0:T(512)S(1)}) all-reduce(f32[384]{0:T(512)S(1)} %copy-done.102, f32[384]{0:T(512)S(1)} %add.338, f32[384]{0:T(512)S(1)} %copy-done.103, ...), channel_id=11, replica_groups=mesh['fsdp'=16,'seq'=8] {'fsdp','seq'}, use_global_device_ids=true, to_apply=%region_42.43.clone | all-reduce | flops 3072 | bytes 24576
  1652.3 40.5 %psum.7 = f32[2,2304]{1,0:T(2,128)} all-reduce(f32[2,2304]{1,0:T(2,128)S(1)} %pad_maximum_fusion.8), channel_id=1, replica_groups=mesh['fsdp'=16,'seq'=8] {'seq'}, use_global_device_ids=true, to_apply=%region_38.39 | all-reduce | flops 4608 | bytes 36864 | tf_op jit(solution)/shard_map/psum | solution.py:310
  1693.5 48.0 %all-reduce.20.cloned.1.call-done = (f32[384,1152]{1,0:T(8,128)}, f32[384,384]{1,0:T(8,128)}, f32[384,1536]{1,0:T(8,128)}) async-done(((f32[384,1152]{1,0:T(8,128)}, f32[384,384]{1,0:T(8,128)}, f32[384,1536]{1,0:T(8,128)}), (f32[384,1152]{1,0:T(8,128)}, f32[384,384]{1,0:T(8,128)}, f32[384,1536]{1,0:T(8,128)})) %all-reduce.20.cloned.1.call-update) | async-done | bytes 4718608
  (486 shorter events, 198.7 us)
Async XLA Ops:
  7.2 755.9 %all-gather.11.cloned.1.call-start = ((), (), s32[]{:S(2)}) async-start(), calls=%async_computation.4 | async-start | bytes 1585152 | tf_op jit(solution)/shard_map/all_gather | solution.py:109
  8.0 761.8 %all-gather.13.cloned.1.call-start = ((), (), s32[]{:S(2)}) async-start(), calls=%async_computation.5 | async-start | bytes 1585152 | tf_op jit(solution)/shard_map/all_gather | solution.py:111
  8.7 884.5 %reduce-scatter.15.cloned.1.call-start = ((), (), s32[]{:S(2)}) async-start(), calls=%async_computation.6 | async-start | bytes 884736
  794.6 173.0 %reduce-scatter.17.cloned.1.call-start = ((), (), s32[]{:S(2)}) async-start(), calls=%async_computation.7 | async-start | bytes 884736
  804.0 743.0 %reduce-scatter.21.cloned.1.call-start = ((), (), s32[]{:S(2)}) async-start(), calls=%async_computation.9 | async-start | bytes 884736
  1372.1 59.5 %collective-permute-start = (f32[16,384]{1,0:T(8,128)}, f32[16,384]{1,0:T(8,128)}, u32[]{:S(2)}, u32[]{:S(2)}) collective-permute-start(f32[16,384]{1,0:T(8,128)} %fusion), channel_id=1, source_target_pairs={{0,1},{1,2},{2,3},{3,4},{4,5},{5,6},{6,7},{7,8},{8,9},{9,10},{10,1... | collective-permute-start | bytes 73736
  1375.7 64.4 %collective-permute-start.1 = (f32[16,384]{1,0:T(8,128)}, f32[16,384]{1,0:T(8,128)}, u32[]{:S(2)}, u32[]{:S(2)}) collective-permute-start(f32[16,384]{1,0:T(8,128)} %fusion), channel_id=1, source_target_pairs={{0,2},{1,3},{2,4},{3,5},{4,6},{5,7},{6,8},{7,9},{8,10},{9,11},{10,... | collective-permute-start | bytes 73736
  1377.6 70.7 %collective-permute-start.10 = (f32[16,384]{1,0:T(8,128)}, f32[16,384]{1,0:T(8,128)}, u32[]{:S(2)}, u32[]{:S(2)}) collective-permute-start(f32[16,384]{1,0:T(8,128)} %fusion), channel_id=1, source_target_pairs={{0,11},{1,12},{2,13},{3,14},{4,15},{5,16},{6,17},{7,18},{8,19},{9,... | collective-permute-start | bytes 73736
  1380.0 75.6 %collective-permute-start.11 = (f32[16,384]{1,0:T(8,128)}, f32[16,384]{1,0:T(8,128)}, u32[]{:S(2)}, u32[]{:S(2)}) collective-permute-start(f32[16,384]{1,0:T(8,128)} %fusion), channel_id=1, source_target_pairs={{0,12},{1,13},{2,14},{3,15},{4,16},{5,17},{6,18},{7,19},{8,20},{9,... | collective-permute-start | bytes 73736
  1385.7 39.0 %collective-permute-start.31 = (f32[12,384]{1,0:T(8,128)}, f32[12,384]{1,0:T(8,128)}, u32[]{:S(2)}, u32[]{:S(2)}) collective-permute-start(f32[12,384]{1,0:T(8,128)} %slice.116), channel_id=1, source_target_pairs={{0,32},{1,33},{2,34},{3,35},{4,36},{5,37},{6,38},{7,39},{8,40},{9,... | collective-permute-start | bytes 55304
  1405.2 175.3 %reduce-scatter.19.cloned.1.call-start = ((), (), s32[]{:S(2)}) async-start(), calls=%async_computation.8 | async-start | bytes 884736
  1416.8 324.7 %all-reduce.20.cloned.1.call-start = ((), (), s32[]{:S(2)}) async-start(), calls=%async_computation.10 | async-start | bytes 9437184
  1424.7 46.8 %collective-permute-start.12 = (f32[16,384]{1,0:T(8,128)S(1)}, f32[16,384]{1,0:T(8,128)S(1)}, u32[]{:S(2)}, u32[]{:S(2)}) collective-permute-start(f32[16,384]{1,0:T(8,128)S(1)} %copy-done.60), channel_id=1, source_target_pairs={{0,13},{1,14},{2,15},{3,16},{4,17},{5,18},{6,19},{7,20},{8,21},{9,... | collective-permute-start | bytes 73736
  1431.6 43.3 %collective-permute-start.13 = (f32[16,384]{1,0:T(8,128)S(1)}, f32[16,384]{1,0:T(8,128)S(1)}, u32[]{:S(2)}, u32[]{:S(2)}) collective-permute-start(f32[16,384]{1,0:T(8,128)S(1)} %copy-done.60), channel_id=1, source_target_pairs={{0,14},{1,15},{2,16},{3,17},{4,18},{5,19},{6,20},{7,21},{8,22},{9,... | collective-permute-start | bytes 73736
  1440.1 41.3 %collective-permute-start.14 = (f32[16,384]{1,0:T(8,128)S(1)}, f32[16,384]{1,0:T(8,128)S(1)}, u32[]{:S(2)}, u32[]{:S(2)}) collective-permute-start(f32[16,384]{1,0:T(8,128)S(1)} %copy-done.60), channel_id=1, source_target_pairs={{0,15},{1,16},{2,17},{3,18},{4,19},{5,20},{6,21},{7,22},{8,23},{9,... | collective-permute-start | bytes 73736
  1448.3 35.3 %collective-permute-start.15 = (f32[16,384]{1,0:T(8,128)S(1)}, f32[16,384]{1,0:T(8,128)S(1)}, u32[]{:S(2)}, u32[]{:S(2)}) collective-permute-start(f32[16,384]{1,0:T(8,128)S(1)} %copy-done.60), channel_id=1, source_target_pairs={{0,16},{1,17},{2,18},{3,19},{4,20},{5,21},{6,22},{7,23},{8,24},{9,... | collective-permute-start | bytes 73736
  1455.6 31.1 %collective-permute-start.16 = (f32[16,384]{1,0:T(8,128)S(1)}, f32[16,384]{1,0:T(8,128)S(1)}, u32[]{:S(2)}, u32[]{:S(2)}) collective-permute-start(f32[16,384]{1,0:T(8,128)S(1)} %copy-done.60), channel_id=1, source_target_pairs={{0,17},{1,18},{2,19},{3,20},{4,21},{5,22},{6,23},{7,24},{8,25},{9,... | collective-permute-start | bytes 73736
  1471.5 17.5 collective-permute-start.17
  1474.9 16.6 collective-permute-start.18
  1498.1 14.7 collective-permute-start.26
  1500.0 14.4 collective-permute-start.27
  1504.8 15.3 collective-permute-start.29
  1508.2 16.2 collective-permute-start.3
  1516.3 15.5 collective-permute-start.5
  (147 other events, 8732.7 us)
Sparse Core Ops, SparseCore 0:
  9.8 300.1 all-gather.10
  311.6 297.8 all-gather.12
  794.7 98.4 reduce-scatter.14
  897.0 70.5 reduce-scatter.16
  1405.3 100.5 reduce-scatter.20
  1509.7 70.7 reduce-scatter.18
  1585.9 155.6 all-reduce.19
where the time goes:
time: 1760 us; the launch traced here: 1750 us
  blocking collectives  1230 us (70%)
  waiting for transfers between devices  239 us (14%)
  starting transfers between devices  119 us (7%)
  local copies, waits for them, and re-layouts  71.4 us (4%)
  matrix products  56.9 us (3%)
  other arithmetic  18.9 us (1%)
    unnamed x3, blocking collectives  471 us
    all_gather x1, blocking collectives, body(): lax.all_gather(shards[0], ('fsdp', 'seq'), axis=0, tiled=True)  293 us
    all_gather x1, blocking collectives, body(): lax.all_gather(shards[3], ('fsdp', 'seq'), axis=0, tiled=True)  283 us
    unnamed x44, waiting for transfers between devices  239 us
    unnamed x37, starting transfers between devices  119 us
    all_gather x2, blocking collectives, body(): lax.all_gather(keys, 'seq', axis=1, tiled=True)  71.7 us
    all_gather x2, blocking collectives, body(): lax.all_gather(values, 'seq', axis=1, tiled=True)  71.4 us
    unnamed x315, local copies, waits for them, and re-layouts  62.8 us
  transfers between devices with their start and end apart: 39, of which 6 were waited for; matrix products, arithmetic and copies ran while one was open for 5% of the time, Pallas kernels for 0%

commit v1 on v0

v1 whole, which is shorter than its diff:
```python
import jax
import jax.numpy as jnp
import numpy as np
from jax import lax
from jax.experimental import pallas as pl
from jax.experimental.pallas import tpu as pltpu
from jax.sharding import Mesh
from jax.sharding import PartitionSpec as P

D = 384
HEADS = 6
FF = 1536
EPSILON = 1e-06
WIDE = 1792
LEFT = 1152
SPLIT = 640
FSDP = ("xl", "y", "core")
SEQ = ("xh", "z")
CHIPS = ("xl", "y", "xh", "z")
X = ("xl", "xh")
BF = jnp.bfloat16
F32 = jnp.float32


def dot(left, right, dims=((1,), (0,))):
    return lax.dot_general(left, right, (dims, ((), ())), preferred_element_type=F32)


def dot_nt(left, right):
    return dot(left, right, ((1,), (1,)))


def dot_tn(left, right):
    return dot(left, right, ((0,), (0,)))


def normalise(values):
    center = values - jnp.mean(values, axis=-1, keepdims=True)
    inverse = lax.rsqrt(jnp.mean(center * center, axis=-1, keepdims=True) + EPSILON)
    return center * inverse, inverse


def norm_back(grad, normed, inverse):
    first = jnp.mean(grad, axis=-1, keepdims=True)
    second = jnp.mean(grad * normed, axis=-1, keepdims=True)
    return inverse * (grad - first - normed * second)


def column_sum(values):
    return jnp.sum(values, axis=0, keepdims=True)


def pick(columns, width):
    place = lax.broadcasted_iota(jnp.int32, (columns.shape[0], width), 1)
    return jnp.where(place == columns, 1.0, 0.0).astype(BF)


def main_kernel(
    near_ref,
    far_ref,
    tokens_ref,
    upstream_ref,
    modulation_ref,
    take_ref,
    give_ref,
    output_ref,
    middle_grad_ref,
    hidden_grad_ref,
    vectors_ref,
    keep_ref,
    send_ref,
    w_qkv,
    w_fc1,
    w_fc2,
    w_out,
    hidden_scr,
    normed_scr,
    keys_scr,
    values_scr,
    keys_t,
    values_t,
    probability_scr,
    attended_t,
    slope_scr,
    grad_a,
    grad_b,
    grad_c,
    key_grads,
    value_grads,
    query_t,
    rows_scr,
):
    half = near_ref.shape[0]

    def unpack(index, start, stop):
        chosen = pick(take_ref[:, index : index + 1], 2 * half)
        return dot(chosen[:, :half], near_ref[:, start:stop]) + dot(
            chosen[:, half:], far_ref[:, start:stop]
        )

    first = unpack(0, 0, WIDE).astype(BF)
    w_fc1[...] = first[:, :FF]
    w_out[:, :256] = first[:, FF:]
    second = unpack(1, 0, WIDE)
    for part in range(4):
        w_fc2[part * D : (part + 1) * D, :] = second[:, part * D : (part + 1) * D].astype(BF)
    w_out[:, 256:] = second[:, FF : FF + 128].astype(BF)
    biases = second[:, FF + 128 :].T
    third = unpack(2, 0, LEFT)
    w_qkv[:, :SPLIT] = (third[:, :SPLIT] + unpack(3, LEFT, WIDE)).astype(BF)
    w_qkv[:, SPLIT:] = (third[:, SPLIT:] + unpack(4, LEFT, LEFT + 512)).astype(BF)
    b_query, b_value, b_out, b_fc2 = (biases[i : i + 1, :] for i in range(4))
    b_fc1 = jnp.concatenate([biases[4 + i : 5 + i, :] for i in range(4)], axis=1)

    shift_one, scale_one, gate_one, shift_two, scale_two, gate_two = (
        modulation_ref[i : i + 1, :] for i in range(6)
    )
    own = upstream_ref.shape[0]
    tokens = tokens_ref[...].astype(F32)
    normed, _ = normalise(tokens)
    normed_scr[...] = normed
    hidden_scr[...] = (normed * (1.0 + scale_one) + shift_one).astype(BF)
    query = (dot(hidden_scr[:own, :], w_qkv[:, :D]) + b_query).astype(BF)
    keys_scr[...] = dot(hidden_scr[...], w_qkv[:, D : 2 * D]).astype(BF)
    values_scr[...] = (dot(hidden_scr[...], w_qkv[:, 2 * D :]) + b_value).astype(BF)
    keys_t[...] = keys_scr[...].T
    values_t[...] = values_scr[...].T
    lane = lax.broadcasted_iota(jnp.int32, (own, 128), 1)

    def one_head(pair, head):
        return jnp.where((lane >= 64) == (head % 2 == 1), pair, jnp.zeros_like(pair))

    queries = []
    for head in range(HEADS):
        tile = slice(head // 2 * 128, head // 2 * 128 + 128)
        scaled = one_head(query[:, tile] * jnp.asarray(0.125, BF), head)
        queries.append(scaled)
        scores = dot_nt(keys_scr[:, tile], scaled)
        exponent = jnp.exp(scores - jnp.max(scores, axis=0, keepdims=True))
        probability = (exponent * (1.0 / column_sum(exponent))).astype(BF)
        probability_scr[head] = probability
        attended_t[head * 64 : head * 64 + 64, :] = dot(
            values_t[head * 64 : head * 64 + 64, :], probability
        )
    attended = attended_t[...].T.astype(BF)
    branch_one = dot(attended, w_out[...]) + b_out
    middle = tokens[:own] + gate_one * branch_one
    normed_two, inverse_two = normalise(middle)
    hidden_two = (normed_two * (1.0 + scale_two) + shift_two).astype(BF)
    inner = dot(hidden_two, w_fc1[...]) + b_fc1
    root = np.sqrt(2.0 / np.pi).astype(np.float32)
    curve = jnp.tanh(root * (inner + 0.044715 * (inner * inner * inner)))
    slope_scr[...] = 0.5 * (1.0 + curve) + 0.5 * inner * (1.0 - curve * curve) * (
        root * (1.0 + 3.0 * 0.044715 * (inner * inner))
    )
    active = (0.5 * inner * (1.0 + curve)).astype(BF)
    branch_two = dot(active, w_fc2[...]) + b_fc2
    output_ref[...] = (middle + gate_two * branch_two).astype(BF)

    upstream = upstream_ref[...].astype(F32)
    rows_scr[...] = jnp.zeros_like(rows_scr)
    vectors_ref[...] = jnp.zeros_like(vectors_ref)
    vectors_ref[5:6, :] = column_sum(upstream * branch_two)
    grad_two = (upstream * gate_two).astype(BF)
    rows_scr[3:4, :] = column_sum(grad_two.astype(F32))
    for part in range(4):
        cut = slice(part * D, (part + 1) * D)
        grad_b[:, cut] = dot_tn(active[:, cut], grad_two).astype(BF)
    grad_inner = (dot_nt(grad_two, w_fc2[...]) * slope_scr[...]).astype(BF)
    grad_a[:, :FF] = dot_tn(hidden_two, grad_inner).astype(BF)
    inner_sum = column_sum(grad_inner.astype(F32))
    for part in range(4):
        rows_scr[4 + part : 5 + part, :] = inner_sum[:, part * D : (part + 1) * D]
    grad_hidden_two = dot_nt(grad_inner, w_fc1[...])
    vectors_ref[4:5, :] = column_sum(grad_hidden_two * normed_two)
    vectors_ref[3:4, :] = column_sum(grad_hidden_two)
    grad_middle = upstream + norm_back(
        grad_hidden_two * (1.0 + scale_two), normed_two, inverse_two
    )
    middle_grad_ref[...] = grad_middle
    vectors_ref[2:3, :] = column_sum(grad_middle * branch_one)
    grad_one = (grad_middle * gate_one).astype(BF)
    grad_out = dot_tn(attended, grad_one).astype(BF)
    grad_a[:, FF:] = grad_out[:, :256]
    grad_b[:, FF : FF + 128] = grad_out[:, 256:]
    rows_scr[2:3, :] = column_sum(grad_one.astype(F32))
    grad_attended = dot_nt(grad_one, w_out[...]).astype(BF)
    products = grad_attended.astype(F32).T * attended_t[...]

    for pair in range(HEADS // 2):
        tile = slice(pair * 128, pair * 128 + 128)
        key_sum = None
        value_sum = None
        for head in (2 * pair, 2 * pair + 1):
            cut = slice(head * 64, head * 64 + 64)
            probability = probability_scr[head]
            grad_head = one_head(grad_attended[:, tile], head)
            weighted = column_sum(products[cut, :])
            grad_probability = dot_nt(values_scr[:, tile], grad_head)
            grad_scores = (probability.astype(F32) * (grad_probability - weighted)).astype(BF)
            value_part = dot(probability, grad_head)
            key_part = dot(grad_scores, queries[head])
            value_sum = value_part if value_sum is None else value_sum + value_part
            key_sum = key_part if key_sum is None else key_sum + key_part
            query_t[cut, :] = dot(keys_t[cut, :], grad_scores) * 0.125
        key_grads[:, tile] = key_sum.astype(BF)
        value_grads[:, tile] = value_sum.astype(BF)
    grad_query = query_t[...].T.astype(BF)
    rows_scr[0:1, :] = column_sum(grad_query.astype(F32))
    rows_scr[1:2, :] = column_sum(value_grads[...].astype(F32))
    grad_c[:, :D] = dot_tn(hidden_scr[:own, :], grad_query).astype(BF)
    grad_c[:, D : 2 * D] = dot_tn(hidden_scr[...], key_grads[...]).astype(BF)
    grad_c[:, 2 * D : 3 * D] = dot_tn(hidden_scr[...], value_grads[...]).astype(BF)
    grad_c[:, 3 * D :] = jnp.zeros((D, 128), BF)
    grad_b[:, FF + 128 :] = rows_scr[...].T.astype(BF)

    others = dot_nt(key_grads[...], w_qkv[:, D : 2 * D]) + dot_nt(
        value_grads[...], w_qkv[:, 2 * D :]
    )
    mine = others[:own] + dot_nt(grad_query, w_qkv[:, :D])
    hidden_grad_ref[:own, :] = mine.astype(BF)
    hidden_grad_ref[own:, :] = others[own:].astype(BF)
    vectors_ref[0:1, :] = column_sum(mine) + column_sum(others[own:])
    vectors_ref[1:2, :] = column_sum(mine * normed_scr[:own, :]) + column_sum(
        others[own:] * normed_scr[own:, :]
    )

    for side, target in enumerate((keep_ref, send_ref)):
        for band in range(2):
            rows = slice(band * 192, band * 192 + 192)
            place = [
                pick(give_ref[:, 5 * side + i : 5 * side + i + 1], 192) for i in range(5)
            ]
            area = slice(band * 256, band * 256 + 256)
            both = dot(place[0], grad_a[rows, :]) + dot(place[1], grad_b[rows, :])
            target[area, :LEFT] = (both[:, :LEFT] + dot(place[2], grad_c[rows, :LEFT])).astype(BF)
            target[area, LEFT:] = (
                both[:, LEFT:]
                + dot(place[3], grad_c[rows, :SPLIT])
                + dot(place[4], grad_c[rows, SPLIT:])
            ).astype(BF)


def final_kernel(tokens_ref, modulation_ref, middle_ref, own_ref, a_ref, b_ref, c_ref, out_ref):
    grad = (
        own_ref[...].astype(F32)
        + a_ref[...].astype(F32)
        + b_ref[...].astype(F32)
        + c_ref[...].astype(F32)
    )
    normed, inverse = normalise(tokens_ref[...].astype(F32))
    out_ref[...] = (
        middle_ref[...] + norm_back(grad * (1.0 + modulation_ref[1:2, :]), normed, inverse)
    ).astype(BF)


def shift(array, axis, step, size):
    return lax.ppermute(array, axis, [(i, (i + step) % size) for i in range(size)])


def shift_x(array, step):
    moves = []
    for index in range(4):
        place = (index % 2) * 2 + index // 2
        there = (place + step) % 4
        moves.append((index, (there % 2) * 2 + there // 2))
    return lax.ppermute(array, X, moves)


def ring(array, axis):
    return [array] + [shift(array, axis, -k, 4) for k in range(1, 4)]


def gather_weights(payload):
    column = jnp.stack(ring(payload, "z"))
    plane = jnp.stack(ring(column, "y"))
    before, after = shift_x(plane, 1), shift_x(plane, -1)
    cut = plane.shape[0] // 2
    opposite = jnp.concatenate([shift_x(before[:cut], 1), shift_x(after[cut:], -1)])
    near = jnp.stack([plane, after, opposite, before])
    far = shift(near, "core", 1, 2)
    return near.reshape(-1, WIDE), far.reshape(-1, WIDE)


def take_columns():
    device = np.arange(128)
    seq, fsdp = device % 8, device // 8
    z, x_hi = seq % 4, seq // 4
    core, y, x_lo = fsdp % 2, fsdp // 2 % 4, fsdp // 8
    x = 2 * x_hi + x_lo
    here = 2 * lax.axis_index("xh") + lax.axis_index("xl")
    slot = (core - lax.axis_index("core")) % 2
    slot = slot * 4 + (x - here) % 4
    slot = slot * 4 + (y - lax.axis_index("y")) % 4
    slot = slot * 4 + (z - lax.axis_index("z")) % 4
    base = jnp.repeat(slot * 8, 3)[:, None]
    j = np.tile(np.arange(3), 128)
    inner = np.stack(
        [j, 3 + j, np.where(j < 2, 6 + j, -2048), np.where(j == 2, 6, -2048), np.where(j == 2, 7, -2048)],
        axis=1,
    )
    return jnp.pad((base + inner).astype(jnp.int32), ((0, 0), (0, 3)), constant_values=-1)


def give_columns():
    row = np.arange(256)
    y, seq, q = row // 64, row // 8 % 8, row % 8
    places = []
    for side in range(2):
        core = (lax.axis_index("core") + side) % 2
        base = (y * 2 + core) * 24 + seq * 3
        for low, high, offset in ((0, 3, 0), (3, 6, -3), (6, 8, -6), (6, 7, -4), (7, 8, -5)):
            places.append(jnp.where((q >= low) & (q < high), base + q + offset, -1))
    return jnp.pad(jnp.stack(places, axis=1).astype(jnp.int32), ((0, 0), (0, 6)), constant_values=-1)


def halves(array):
    upper = lax.axis_index("xh") == 1
    return jnp.where(upper, array[1], array[0]), jnp.where(upper, array[0], array[1])


def rejoin(own, other):
    upper = lax.axis_index("xh") == 1
    return jnp.stack([jnp.where(upper, other, own), jnp.where(upper, own, other)])


def body(latents, modulation, w_qkv, b_query, b_value, w_out, b_out, w_fc1, b_fc1, w_fc2, b_fc2, cotangent):
    tokens = latents.shape[1]
    fc1 = w_fc1.reshape(3, D, 4).transpose(0, 2, 1).reshape(3, FF)
    fc2 = w_fc2.reshape(3, FF)
    biases = jnp.concatenate(
        [b[:, None] for b in (b_query, b_value, b_out, b_fc2)] + [b_fc1.reshape(3, 4), jnp.zeros((3, 120), BF)],
        axis=1,
    )
    rows = jnp.concatenate(
        [
            jnp.concatenate([fc1, w_out[:, :256]], axis=1),
            jnp.concatenate([fc2, w_out[:, 256:], biases], axis=1),
            jnp.concatenate([w_qkv[0:1], w_qkv[2:3, :SPLIT]], axis=1),
            jnp.concatenate([w_qkv[1:2], w_qkv[2:3, SPLIT:], jnp.zeros((1, 128), BF)], axis=1),
        ],
        axis=0,
    )
    near, far = gather_weights(rows)

    own_tokens, partner_tokens = halves(latents)
    own_upstream, partner_upstream = halves(cotangent)
    swapped = shift(jnp.stack([partner_tokens, partner_upstream]), "xh", 1, 2)
    query_tokens = jnp.concatenate([own_tokens, swapped[0]])
    upstream = jnp.concatenate([own_upstream, swapped[1]])
    all_tokens = jnp.concatenate(ring(query_tokens, "z"))
    condition = halves(modulation)[0].reshape(6, D)

    own = 2 * tokens
    length = 4 * own
    vmem = lambda *shape, dtype=BF: pltpu.VMEM(shape, dtype)
    output, middle_grad, hidden_grad, vectors, keep, send = pl.pallas_call(
        main_kernel,
        out_shape=(
            jax.ShapeDtypeStruct((own, D), BF),
            jax.ShapeDtypeStruct((own, D), F32),
            jax.ShapeDtypeStruct((length, D), BF),
            jax.ShapeDtypeStruct((8, D), F32),
            jax.ShapeDtypeStruct((512, WIDE), BF),
            jax.ShapeDtypeStruct((512, WIDE), BF),
        ),
        scratch_shapes=[
            vmem(D, 3 * D),
            vmem(D, FF),
            vmem(FF, D),
            vmem(D, D),
            vmem(length, D),
            vmem(length, D, dtype=F32),
            vmem(length, D),
            vmem(length, D),
            vmem(D, length),
            vmem(D, length),
            vmem(HEADS, length, own),
            vmem(D, own, dtype=F32),
            vmem(own, FF, dtype=F32),
            vmem(D, WIDE),
            vmem(D, WIDE),
            vmem(D, LEFT + 128),
            vmem(length, D),
            vmem(length, D),
            vmem(D, own, dtype=F32),
            vmem(128, D, dtype=F32),
        ],
        compiler_params=pltpu.CompilerParams(vmem_limit_bytes=56 * 1024 * 1024),
    )(near, far, all_tokens, upstream, condition, take_columns(), give_columns())

    mixed = keep + shift(send, "core", 1, 2)
    pieces = lax.all_to_all(mixed, CHIPS, 0, 0, tiled=True)
    total = jnp.sum(pieces.reshape(64, 8, WIDE).astype(F32), axis=0)

    parts = hidden_grad.reshape(4, own, D)
    arrived = [shift(parts[k], "z", k, 4) for k in range(1, 4)]
    input_grad = pl.pallas_call(
        final_kernel, out_shape=jax.ShapeDtypeStruct((own, D), BF)
    )(query_tokens, condition, middle_grad, parts[0], *arrived)
    output_back = shift(output[tokens:], "xh", 1, 2)
    grad_back = shift(input_grad[tokens:], "xh", 1, 2)
    sums = vectors
    for k in range(1, 4):
        sums = sums + shift(vectors, "z", k, 4)
    sums = sums[:6].reshape(6 * D)
    modulation_grad = rejoin(sums, shift(sums, "xh", 1, 2))

    grad_fc1 = total[:3, :FF].reshape(3, 4, D).transpose(0, 2, 1).reshape(3, FF)
    grad_fc2 = total[3:6, :FF].reshape(12, D)
    grad_out = jnp.concatenate([total[:3, FF:], total[3:6, FF : FF + 128]], axis=1)
    grad_bias = total[3:6, FF + 128 :]
    last = jnp.concatenate([total[6:7, LEFT:], total[7:8, LEFT : LEFT + 512]], axis=1)
    grad_qkv = jnp.concatenate([total[6:8, :LEFT], last], axis=0)
    return (
        rejoin(output[:tokens], output_back),
        rejoin(input_grad[:tokens], grad_back),
        modulation_grad,
        grad_qkv,
        grad_bias[:, 0],
        grad_bias[:, 1],
        grad_out,
        grad_bias[:, 2],
        grad_fc1,
        grad_bias[:, 4:8].reshape(12),
        grad_fc2,
        grad_bias[:, 3],
    )


def solution(mesh):
    chips = Mesh(mesh.devices.reshape(2, 4, 2, 2, 4), ("xl", "y", "core", "xh", "z"))
    rows = P(FSDP + SEQ, None)
    line = P(FSDP + SEQ)
    tokens = P(FSDP, SEQ, None)
    condition = P(FSDP, None)
    in_specs = (tokens, condition, rows, line, line, rows, line, rows, line, rows, line, tokens)
    out_specs = (tokens, tokens, condition, rows, line, line, rows, line, rows, line, rows, line)
    return jax.shard_map(body, mesh=chips, in_specs=in_specs, out_specs=out_specs, check_vma=False)
```

time: 1760 us -> 171 us (0.10)
  blocking collectives: 1230 us -> 0 us
  waiting for transfers between devices: 239 us -> 58.9 us
  starting transfers between devices: 119 us -> 46.2 us
  matrix products: 56.9 us -> 0 us
  local copies, waits for them, and re-layouts: 71.4 us -> 21.3 us
  Pallas kernels: 0 us -> 30 us
    all_gather x6 -> x0, blocking collectives: 720 us -> none  [the longest x1 293 us: body(): lax.all_gather(shards[0], ('fsdp', 'seq'), axis=0, tiled=True)]
    unnamed x3 -> x0, blocking collectives: 471 us -> none
    unnamed x44 -> x0, waiting for transfers between devices: 239 us -> none
    unnamed x37 -> x0, starting transfers between devices: 119 us -> none
    unnamed x315 -> x50, local copies, waits for them, and re-layouts: 62.8 us -> 2.99 us
    ppermute x0 -> x25, waiting for transfers between devices: none -> 58.9 us  [the longest x21 44.2 us: shift(): lax.ppermute(array, axis, [(i, (i + step) % size) for i in range(size)])]
    dot_general x36 -> x0, matrix products: 56.9 us -> none  [the longest x8 18 us: left_t(): lax.dot_general(left, right, (((0,), (0,)), ((), ())), preferred_element_...]
    psum x1 -> x0, blocking collectives: 40.5 us -> none  [body(): modulation_grad = lax.psum(jnp.concatenate(condition_grads, axis=0), 'seq')]
  transfers between devices with their start and end apart: 39 -> 26, of which waited for: 6 -> 16; matrix products, arithmetic and copies ran while one was open for 5% -> 7% of each run, Pallas kernels for 0% -> 1%
where the time goes in v1:
time: 171 us; the launch traced here: 168 us
  waiting for transfers between devices  58.9 us (34%)
  starting transfers between devices  46.2 us (27%)
  Pallas kernels  30 us (18%)
  local copies, waits for them, and re-layouts  21.3 us (12%)
  other arithmetic  10.5 us (6%)
    ppermute x21, waiting for transfers between devices, shift(): lax.ppermute(array, axis, [(i, (i + step) % size) for i in range(size)])  44.2 us
    ppermute x21, starting transfers between devices, shift(): lax.ppermute(array, axis, [(i, (i + step) % size) for i in range(size)])  32.8 us
    pallas_call x1, Pallas kernels, body(): pl.pallas_call(main_kernel, out_shape=(jax.ShapeDtypeStruct((own, D), BF)...  27.6 us
    ppermute x4, waiting for transfers between devices, shift_x(): return lax.ppermute(array, X, moves)  14.6 us
    all_to_all x1, starting transfers between devices, body(): pieces = lax.all_to_all(mixed, CHIPS, 0, 0, tiled=True)  7.24 us
    ppermute x4, starting transfers between devices, shift_x(): return lax.ppermute(array, X, moves)  6.14 us
  transfers between devices with their start and end apart: 26, of which 16 were waited for; matrix products, arithmetic and copies ran while one was open for 7% of the time, Pallas kernels for 1%

profile of v1, /device:TPU:8, one launch (start us, length us, event | category | flops | bytes accessed | tf_op | source)
XLA Modules:
  0.0 168.1 jit_solution(16874427348851877184)
XLA Ops:
  12.4 3.6 %collective-permute-start.1 = (bf16[8,1792]{1,0:T(8,128)(2,1)S(1)}, bf16[8,1792]{1,0:T(8,128)(2,1)S(1)}, u32[]{:S(2)}, u32[]{:S(2)}) collective-permute-start(bf16[8,1792]{1,0:T(8,128)(2,1)S(1)} %maximum_maximum_fusion), channel_id=1, source_target_pairs={{0,2},{1,3},{2,0},{3,1},{4,6},{5,7},{6,4},{7,5},{8,10},{9,11},{10,... | collective-permute-start | bytes 86024 | tf_op jit(solution)/shard_map/ppermute | solution.py:258
  19.9 2.4 %collective-permute-start.4 = (bf16[4,8,1792]{2,1,0:T(8,128)(2,1)S(1)}, bf16[4,8,1792]{2,1,0:T(8,128)(2,1)S(1)}, u32[]{:S(2)}, u32[]{:S(2)}) collective-permute-start(bf16[4,8,1792]{2,1,0:T(8,128)(2,1)S(1)} %get-tuple-element.45), channel_id=1, source_target_pairs={{0,32},{16,48},{32,0},{48,16},{1,33},{17,49},{33,1},{49,17},{2,34}... | collective-permute-start | bytes 344072 | tf_op jit(solution)/shard_map/ppermute | solution.py:258
  24.3 2.0 %collective-permute-done.4 = bf16[4,8,1792]{2,1,0:T(8,128)(2,1)S(1)} collective-permute-done((bf16[4,8,1792]{2,1,0:T(8,128)(2,1)S(1)}, bf16[4,8,1792]{2,1,0:T(8,128)(2,1)S(1)}, u32[]{:S(2)}, u32[]{:S(2)}) %collective-permute-start.4) | collective-permute-done | bytes 114720 | tf_op jit(solution)/shard_map/ppermute | solution.py:258
  28.5 2.8 %collective-permute-start.6 = (bf16[4,4,8,1792]{3,2,1,0:T(8,128)(2,1)S(1)}, bf16[4,4,8,1792]{3,2,1,0:T(8,128)(2,1)S(1)}, u32[]{:S(2)}, u32[]{:S(2)}) collective-permute-start(bf16[4,4,8,1792]{3,2,1,0:T(8,128)(2,1)S(1)} %get-tuple-element.35), channel_id=1, source_target_pairs={{0,68},{4,64},{64,0},{68,4},{1,69},{5,65},{65,1},{69,5},{2,70},{6,... | collective-permute-start | bytes 1376264 | tf_op jit(solution)/shard_map/ppermute | solution.py:267
  31.4 7.5 %collective-permute-done.6 = bf16[4,4,8,1792]{3,2,1,0:T(8,128)(2,1)S(1)} collective-permute-done((bf16[4,4,8,1792]{3,2,1,0:T(8,128)(2,1)S(1)}, bf16[4,4,8,1792]{3,2,1,0:T(8,128)(2,1)S(1)}, u32[]{:S(2)}, u32[]{:S(2)}) %collective-permute-start.6) | collective-permute-done | bytes 458784 | tf_op jit(solution)/shard_map/ppermute | solution.py:267
  38.9 3.2 %collective-permute-start.9 = (bf16[2,4,8,1792]{3,2,1,0:T(8,128)(2,1)S(1)}, bf16[2,4,8,1792]{3,2,1,0:T(8,128)(2,1)S(1)}, u32[]{:S(2)}, u32[]{:S(2)}) collective-permute-start(bf16[2,4,8,1792]{3,2,1,0:T(8,128)(2,1)S(1)} %slice.163), channel_id=1, source_target_pairs={{0,68},{4,64},{64,0},{68,4},{1,69},{5,65},{65,1},{69,5},{2,70},{6,... | collective-permute-start | bytes 688136 | tf_op jit(solution)/shard_map/ppermute | solution.py:267
  44.5 2.9 %collective-permute-done.9 = bf16[2,4,8,1792]{3,2,1,0:T(8,128)(2,1)S(1)} collective-permute-done((bf16[2,4,8,1792]{3,2,1,0:T(8,128)(2,1)S(1)}, bf16[2,4,8,1792]{3,2,1,0:T(8,128)(2,1)S(1)}, u32[]{:S(2)}, u32[]{:S(2)}) %collective-permute-start.9) | collective-permute-done | bytes 229408 | tf_op jit(solution)/shard_map/ppermute | solution.py:267
  47.4 4.2 %collective-permute-done.8 = bf16[2,4,8,1792]{3,2,1,0:T(8,128)(2,1)S(1)} collective-permute-done((bf16[2,4,8,1792]{3,2,1,0:T(8,128)(2,1)S(1)}, bf16[2,4,8,1792]{3,2,1,0:T(8,128)(2,1)S(1)}, u32[]{:S(2)}, u32[]{:S(2)}) %collective-permute-start.8) | collective-permute-done | bytes 229408 | tf_op jit(solution)/shard_map/ppermute | solution.py:267
  57.3 3.5 %collective-permute-start.13 = (bf16[256,384]{1,0:T(8,128)(2,1)S(1)}, bf16[256,384]{1,0:T(8,128)(2,1)S(1)}, u32[]{:S(2)}, u32[]{:S(2)}) collective-permute-start(bf16[256,384]{1,0:T(8,128)(2,1)S(1)} %pad_maximum_fusion.3.tokens_ref), channel_id=1, source_target_pairs={{0,2},{1,3},{2,0},{3,1},{4,6},{5,7},{6,4},{7,5},{8,10},{9,11},{10,... | collective-permute-start | bytes 589832 | tf_op jit(solution)/shard_map/ppermute | solution.py:258
  63.0 7.1 %collective-permute-done.12 = bf16[256,384]{1,0:T(8,128)(2,1)S(1)} collective-permute-done((bf16[256,384]{1,0:T(8,128)(2,1)S(1)}, bf16[256,384]{1,0:T(8,128)(2,1)S(1)}, u32[]{:S(2)}, u32[]{:S(2)}) %collective-permute-start.12) | collective-permute-done | bytes 196640 | tf_op jit(solution)/shard_map/ppermute | solution.py:258
  71.3 27.6 %shard_map.391 = (bf16[256,384]{1,0:T(8,128)(2,1)}, f32[256,384]{1,0:T(8,128)}, bf16[1024,384]{1,0:T(8,128)(2,1)}, f32[8,384]{1,0:T(8,128)}, bf16[512,1792]{1,0:T(8,128)(2,1)}, /*index=5*/bf16[512,1792]{1,0:T(8,128)(2,1)}) custom-call(bf16[512,1792]{1,0:T(8,128)(2,1)} %bitcast.56, bf16[512,1792]{1,0:T(8,128)(2,1)} %bitcast.18.far_ref, ...), custom_call_target="tpu_custom_call" | custom-call | tf_op jit(solution)/shard_map/pallas_call | solution.py:357
  98.9 4.0 %collective-permute-done.24 = bf16[512,1792]{1,0:T(8,128)(2,1)S(1)} collective-permute-done((bf16[512,1792]{1,0:T(8,128)(2,1)}, bf16[512,1792]{1,0:T(8,128)(2,1)S(1)}, u32[]{:S(2)}, u32[]{:S(2)}) %collective-permute-start.24) | collective-permute-done | bytes 1835040 | tf_op jit(solution)/shard_map/ppermute | solution.py:258
  102.9 3.0 %add_bitcast_fusion = bf16[64,8,1792]{2,1,0:T(8,128)(2,1)} fusion(bf16[512,1792]{1,0:T(8,128)(2,1)} %get-tuple-element.22, bf16[512,1792]{1,0:T(8,128)(2,1)S(1)} %collective-permute-done.24), kind=kLoop, calls=%fused_computation.2 | loop fusion | flops 917504 | bytes 5505024 | tf_op jit(solution)/shard_map/all_to_all | solution.py:393
  105.9 7.2 %all-to-all-start = ((bf16[64,8,1792]{2,1,0:T(8,128)(2,1)}), bf16[64,8,1792]{2,1,0:T(8,128)(2,1)S(1)}, u32[]{:S(2)}, u32[]{:S(2)}) async-start(bf16[64,8,1792]{2,1,0:T(8,128)(2,1)} %add_bitcast_fusion), calls=%async_computation | async-start | bytes 3670016 | tf_op jit(solution)/shard_map/all_to_all | solution.py:393
  113.2 2.7 %collective-permute-start.22 = (f32[8,384]{1,0:T(8,128)S(1)}, f32[8,384]{1,0:T(8,128)S(1)}, u32[]{:S(2)}, u32[]{:S(2)}) collective-permute-start(f32[8,384]{1,0:T(8,128)S(1)} %copy-done.11), channel_id=1, source_target_pairs={{0,3},{1,0},{2,1},{3,2},{4,7},{5,4},{6,5},{7,6},{8,11},{9,8},{10,9... | collective-permute-start | bytes 36872 | tf_op jit(solution)/shard_map/ppermute | solution.py:258
  117.7 3.0 %collective-permute-start.15 = (bf16[128,384]{1,0:T(8,128)(2,1)S(1)}, bf16[128,384]{1,0:T(8,128)(2,1)S(1)}, u32[]{:S(2)}, u32[]{:S(2)}) collective-permute-start(bf16[128,384]{1,0:T(8,128)(2,1)S(1)} %slice.141), channel_id=1, source_target_pairs={{0,4},{4,0},{1,5},{5,1},{2,6},{6,2},{3,7},{7,3},{8,12},{12,8},{9,1... | collective-permute-start | bytes 294920 | tf_op jit(solution)/shard_map/ppermute | solution.py:258
  120.7 2.2 %collective-permute-done.22 = f32[8,384]{1,0:T(8,128)S(1)} collective-permute-done((f32[8,384]{1,0:T(8,128)S(1)}, f32[8,384]{1,0:T(8,128)S(1)}, u32[]{:S(2)}, u32[]{:S(2)}) %collective-permute-start.22) | collective-permute-done | bytes 12320 | tf_op jit(solution)/shard_map/ppermute | solution.py:258
  122.9 13.4 %collective-permute-done.21 = f32[8,384]{1,0:T(8,128)S(1)} collective-permute-done((f32[8,384]{1,0:T(8,128)S(1)}, f32[8,384]{1,0:T(8,128)S(1)}, u32[]{:S(2)}, u32[]{:S(2)}) %collective-permute-start.21) | collective-permute-done | bytes 12320 | tf_op jit(solution)/shard_map/ppermute | solution.py:258
  136.3 2.5 %collective-permute-start.23 = (f32[2304]{0:T(1024)S(1)}, f32[2304]{0:T(1024)S(1)}, u32[]{:S(2)}, u32[]{:S(2)}) collective-permute-start(f32[2304]{0:T(1024)S(1)} %reshape.86), channel_id=1, source_target_pairs={{0,4},{4,0},{1,5},{5,1},{2,6},{6,2},{3,7},{7,3},{8,12},{12,8},{9,1... | collective-permute-start | bytes 27656 | tf_op jit(solution)/shard_map/ppermute | solution.py:258
  139.6 2.8 %collective-permute-start.18 = (bf16[256,384]{1,0:T(8,128)(2,1)S(1)}, bf16[256,384]{1,0:T(8,128)(2,1)S(1)}, u32[]{:S(2)}, u32[]{:S(2)}) collective-permute-start(bf16[256,384]{1,0:T(8,128)(2,1)S(1)} %get-tuple-element.30), channel_id=1, source_target_pairs={{0,3},{1,0},{2,1},{3,2},{4,7},{5,4},{6,5},{7,6},{8,11},{9,8},{10,9... | collective-permute-start | bytes 589832 | tf_op jit(solution)/shard_map/ppermute | solution.py:258
  144.0 4.0 %collective-permute-done.18.c_ref = bf16[256,384]{1,0:T(8,128)(2,1)S(1)} collective-permute-done((bf16[256,384]{1,0:T(8,128)(2,1)S(1)}, bf16[256,384]{1,0:T(8,128)(2,1)S(1)}, u32[]{:S(2)}, u32[]{:S(2)}) %collective-permute-start.18) | collective-permute-done | bytes 196640 | tf_op jit(solution)/shard_map/ppermute | solution.py:258
  152.1 2.4 %shard_map.392 = bf16[256,384]{1,0:T(8,128)(2,1)} custom-call(bf16[256,384]{1,0:T(8,128)(2,1)} %copy-done.2, f32[6,384]{1,0:T(8,128)} %select_n.138.modulation_ref, f32[256,384]{1,0:T(8,128)} %get-tuple-element.19.middle_ref, bf16[256,384]{1,0:T(8,128)(2,1)} %get-tuple-element.33.own_ref, bf16[256,384]{1,0:T(8,128)(2,1)} %copy-done.7, ...), custom_call_target="tpu_custom_call" | custom-call | tf_op jit(solution)/shard_map/pallas_call | solution.py:398
  155.4 2.3 %collective-permute-start.19 = (bf16[128,384]{1,0:T(8,128)(2,1)S(1)}, bf16[128,384]{1,0:T(8,128)(2,1)S(1)}, u32[]{:S(2)}, u32[]{:S(2)}) collective-permute-start(bf16[128,384]{1,0:T(8,128)(2,1)S(1)} %slice.166), channel_id=1, source_target_pairs={{0,4},{4,0},{1,5},{5,1},{2,6},{6,2},{3,7},{7,3},{8,12},{12,8},{9,1... | collective-permute-start | bytes 294920 | tf_op jit(solution)/shard_map/ppermute | solution.py:258
  158.5 3.2 %collective-permute-done.19 = bf16[128,384]{1,0:T(8,128)(2,1)S(1)} collective-permute-done((bf16[128,384]{1,0:T(8,128)(2,1)S(1)}, bf16[128,384]{1,0:T(8,128)(2,1)S(1)}, u32[]{:S(2)}, u32[]{:S(2)}) %collective-permute-start.19) | collective-permute-done | bytes 98336 | tf_op jit(solution)/shard_map/ppermute | solution.py:258
  (151 shorter events, 47.1 us)
Async XLA Ops:
  10.4 6.6 %collective-permute-start.2 = (bf16[8,1792]{1,0:T(8,128)(2,1)S(1)}, bf16[8,1792]{1,0:T(8,128)(2,1)S(1)}, u32[]{:S(2)}, u32[]{:S(2)}) collective-permute-start(bf16[8,1792]{1,0:T(8,128)(2,1)S(1)} %maximum_maximum_fusion), channel_id=1, source_target_pairs={{0,1},{1,2},{2,3},{3,0},{4,5},{5,6},{6,7},{7,4},{8,9},{9,10},{10,1... | collective-permute-start | bytes 86024 | tf_op jit(solution)/shard_map/ppermute | solution.py:258
  12.4 5.7 %collective-permute-start.1 = (bf16[8,1792]{1,0:T(8,128)(2,1)S(1)}, bf16[8,1792]{1,0:T(8,128)(2,1)S(1)}, u32[]{:S(2)}, u32[]{:S(2)}) collective-permute-start(bf16[8,1792]{1,0:T(8,128)(2,1)S(1)} %maximum_maximum_fusion), channel_id=1, source_target_pairs={{0,2},{1,3},{2,0},{3,1},{4,6},{5,7},{6,4},{7,5},{8,10},{9,11},{10,... | collective-permute-start | bytes 86024 | tf_op jit(solution)/shard_map/ppermute | solution.py:258
  19.9 6.4 %collective-permute-start.4 = (bf16[4,8,1792]{2,1,0:T(8,128)(2,1)S(1)}, bf16[4,8,1792]{2,1,0:T(8,128)(2,1)S(1)}, u32[]{:S(2)}, u32[]{:S(2)}) collective-permute-start(bf16[4,8,1792]{2,1,0:T(8,128)(2,1)S(1)} %get-tuple-element.45), channel_id=1, source_target_pairs={{0,32},{16,48},{32,0},{48,16},{1,33},{17,49},{33,1},{49,17},{2,34}... | collective-permute-start | bytes 344072 | tf_op jit(solution)/shard_map/ppermute | solution.py:258
  22.3 5.2 %collective-permute-start.3 = (bf16[4,8,1792]{2,1,0:T(8,128)(2,1)S(1)}, bf16[4,8,1792]{2,1,0:T(8,128)(2,1)S(1)}, u32[]{:S(2)}, u32[]{:S(2)}) collective-permute-start(bf16[4,8,1792]{2,1,0:T(8,128)(2,1)S(1)} %get-tuple-element.45), channel_id=1, source_target_pairs={{0,48},{16,0},{32,16},{48,32},{1,49},{17,1},{33,17},{49,33},{2,50}... | collective-permute-start | bytes 344072 | tf_op jit(solution)/shard_map/ppermute | solution.py:258
  23.6 4.8 %collective-permute-start.5 = (bf16[4,8,1792]{2,1,0:T(8,128)(2,1)S(1)}, bf16[4,8,1792]{2,1,0:T(8,128)(2,1)S(1)}, u32[]{:S(2)}, u32[]{:S(2)}) collective-permute-start(bf16[4,8,1792]{2,1,0:T(8,128)(2,1)S(1)} %get-tuple-element.45), channel_id=1, source_target_pairs={{0,16},{16,32},{32,48},{48,0},{1,17},{17,33},{33,49},{49,1},{2,18}... | collective-permute-start | bytes 344072 | tf_op jit(solution)/shard_map/ppermute | solution.py:258
  28.5 10.4 %collective-permute-start.6 = (bf16[4,4,8,1792]{3,2,1,0:T(8,128)(2,1)S(1)}, bf16[4,4,8,1792]{3,2,1,0:T(8,128)(2,1)S(1)}, u32[]{:S(2)}, u32[]{:S(2)}) collective-permute-start(bf16[4,4,8,1792]{3,2,1,0:T(8,128)(2,1)S(1)} %get-tuple-element.35), channel_id=1, source_target_pairs={{0,68},{4,64},{64,0},{68,4},{1,69},{5,65},{65,1},{69,5},{2,70},{6,... | collective-permute-start | bytes 1376264 | tf_op jit(solution)/shard_map/ppermute | solution.py:267
  31.3 10.8 %collective-permute-start.7 = (bf16[4,4,8,1792]{3,2,1,0:T(8,128)(2,1)S(1)}, bf16[4,4,8,1792]{3,2,1,0:T(8,128)(2,1)S(1)}, u32[]{:S(2)}, u32[]{:S(2)}) collective-permute-start(bf16[4,4,8,1792]{3,2,1,0:T(8,128)(2,1)S(1)} %get-tuple-element.35), channel_id=1, source_target_pairs={{0,64},{4,68},{64,4},{68,0},{1,65},{5,69},{65,5},{69,1},{2,66},{6,... | collective-permute-start | bytes 1376264 | tf_op jit(solution)/shard_map/ppermute | solution.py:267
  38.9 8.5 %collective-permute-start.9 = (bf16[2,4,8,1792]{3,2,1,0:T(8,128)(2,1)S(1)}, bf16[2,4,8,1792]{3,2,1,0:T(8,128)(2,1)S(1)}, u32[]{:S(2)}, u32[]{:S(2)}) collective-permute-start(bf16[2,4,8,1792]{3,2,1,0:T(8,128)(2,1)S(1)} %slice.163), channel_id=1, source_target_pairs={{0,68},{4,64},{64,0},{68,4},{1,69},{5,65},{65,1},{69,5},{2,70},{6,... | collective-permute-start | bytes 688136 | tf_op jit(solution)/shard_map/ppermute | solution.py:267
  42.2 9.4 %collective-permute-start.8 = (bf16[2,4,8,1792]{3,2,1,0:T(8,128)(2,1)S(1)}, bf16[2,4,8,1792]{3,2,1,0:T(8,128)(2,1)S(1)}, u32[]{:S(2)}, u32[]{:S(2)}) collective-permute-start(bf16[2,4,8,1792]{3,2,1,0:T(8,128)(2,1)S(1)} %slice.162), channel_id=1, source_target_pairs={{0,64},{4,68},{64,4},{68,0},{1,65},{5,69},{65,5},{69,1},{2,66},{6,... | collective-permute-start | bytes 688136 | tf_op jit(solution)/shard_map/ppermute | solution.py:267
  43.0 13.2 %collective-permute-start.11 = (bf16[2,128,384]{2,1,0:T(8,128)(2,1)}, bf16[2,128,384]{2,1,0:T(8,128)(2,1)}, u32[]{:S(2)}, u32[]{:S(2)}) collective-permute-start(bf16[2,128,384]{2,1,0:T(8,128)(2,1)} %pad_maximum_fusion.2), channel_id=1, source_target_pairs={{0,4},{4,0},{1,5},{5,1},{2,6},{6,2},{3,7},{7,3},{8,12},{12,8},{9,1... | collective-permute-start | bytes 589832 | tf_op jit(solution)/shard_map/ppermute | solution.py:258
  52.0 18.3 %collective-permute-start.10 = (bf16[4,4,4,8,1792]{4,3,2,1,0:T(8,128)(2,1)S(1)}, bf16[4,4,4,8,1792]{4,3,2,1,0:T(8,128)(2,1)}, u32[]{:S(2)}, u32[]{:S(2)}) collective-permute-start(bf16[4,4,4,8,1792]{4,3,2,1,0:T(8,128)(2,1)S(1)} %pad_maximum_fusion), channel_id=1, source_target_pairs={{0,8},{8,0},{1,9},{9,1},{2,10},{10,2},{3,11},{11,3},{4,12},{12,4},... | collective-permute-start | bytes 5505032 | tf_op jit(solution)/shard_map/ppermute | solution.py:258
  57.2 13.1 %collective-permute-start.14 = (bf16[256,384]{1,0:T(8,128)(2,1)S(1)}, bf16[256,384]{1,0:T(8,128)(2,1)S(1)}, u32[]{:S(2)}, u32[]{:S(2)}) collective-permute-start(bf16[256,384]{1,0:T(8,128)(2,1)S(1)} %pad_maximum_fusion.3.tokens_ref), channel_id=1, source_target_pairs={{0,1},{1,2},{2,3},{3,0},{4,5},{5,6},{6,7},{7,4},{8,9},{9,10},{10,1... | collective-permute-start | bytes 589832 | tf_op jit(solution)/shard_map/ppermute | solution.py:258
  57.3 12.9 %collective-permute-start.13 = (bf16[256,384]{1,0:T(8,128)(2,1)S(1)}, bf16[256,384]{1,0:T(8,128)(2,1)S(1)}, u32[]{:S(2)}, u32[]{:S(2)}) collective-permute-start(bf16[256,384]{1,0:T(8,128)(2,1)S(1)} %pad_maximum_fusion.3.tokens_ref), channel_id=1, source_target_pairs={{0,2},{1,3},{2,0},{3,1},{4,6},{5,7},{6,4},{7,5},{8,10},{9,11},{10,... | collective-permute-start | bytes 589832 | tf_op jit(solution)/shard_map/ppermute | solution.py:258
  60.8 9.3 %collective-permute-start.12 = (bf16[256,384]{1,0:T(8,128)(2,1)S(1)}, bf16[256,384]{1,0:T(8,128)(2,1)S(1)}, u32[]{:S(2)}, u32[]{:S(2)}) collective-permute-start(bf16[256,384]{1,0:T(8,128)(2,1)S(1)} %pad_maximum_fusion.3.tokens_ref), channel_id=1, source_target_pairs={{0,3},{1,0},{2,1},{3,2},{4,7},{5,4},{6,5},{7,6},{8,11},{9,8},{10,9... | collective-permute-start | bytes 589832 | tf_op jit(solution)/shard_map/ppermute | solution.py:258
  105.9 57.3 %all-to-all-start = ((bf16[64,8,1792]{2,1,0:T(8,128)(2,1)}), bf16[64,8,1792]{2,1,0:T(8,128)(2,1)S(1)}, u32[]{:S(2)}, u32[]{:S(2)}) async-start(bf16[64,8,1792]{2,1,0:T(8,128)(2,1)} %add_bitcast_fusion), calls=%async_computation | async-start | bytes 3670016 | tf_op jit(solution)/shard_map/all_to_all | solution.py:393
  113.2 9.7 %collective-permute-start.22 = (f32[8,384]{1,0:T(8,128)S(1)}, f32[8,384]{1,0:T(8,128)S(1)}, u32[]{:S(2)}, u32[]{:S(2)}) collective-permute-start(f32[8,384]{1,0:T(8,128)S(1)} %copy-done.11), channel_id=1, source_target_pairs={{0,3},{1,0},{2,1},{3,2},{4,7},{5,4},{6,5},{7,6},{8,11},{9,8},{10,9... | collective-permute-start | bytes 36872 | tf_op jit(solution)/shard_map/ppermute | solution.py:258
  115.9 20.4 %collective-permute-start.21 = (f32[8,384]{1,0:T(8,128)S(1)}, f32[8,384]{1,0:T(8,128)S(1)}, u32[]{:S(2)}, u32[]{:S(2)}) collective-permute-start(f32[8,384]{1,0:T(8,128)S(1)} %copy-done.11), channel_id=1, source_target_pairs={{0,2},{1,3},{2,0},{3,1},{4,6},{5,7},{6,4},{7,5},{8,10},{9,11},{10,... | collective-permute-start | bytes 36872 | tf_op jit(solution)/shard_map/ppermute | solution.py:258
  116.8 19.5 %collective-permute-start.20 = (f32[8,384]{1,0:T(8,128)S(1)}, f32[8,384]{1,0:T(8,128)S(1)}, u32[]{:S(2)}, u32[]{:S(2)}) collective-permute-start(f32[8,384]{1,0:T(8,128)S(1)} %copy-done.11), channel_id=1, source_target_pairs={{0,1},{1,2},{2,3},{3,0},{4,5},{5,6},{6,7},{7,4},{8,9},{9,10},{10,1... | collective-permute-start | bytes 36872 | tf_op jit(solution)/shard_map/ppermute | solution.py:258
  117.7 26.3 %collective-permute-start.15 = (bf16[128,384]{1,0:T(8,128)(2,1)S(1)}, bf16[128,384]{1,0:T(8,128)(2,1)S(1)}, u32[]{:S(2)}, u32[]{:S(2)}) collective-permute-start(bf16[128,384]{1,0:T(8,128)(2,1)S(1)} %slice.141), channel_id=1, source_target_pairs={{0,4},{4,0},{1,5},{5,1},{2,6},{6,2},{3,7},{7,3},{8,12},{12,8},{9,1... | collective-permute-start | bytes 294920 | tf_op jit(solution)/shard_map/ppermute | solution.py:258
  136.3 7.0 %collective-permute-start.23 = (f32[2304]{0:T(1024)S(1)}, f32[2304]{0:T(1024)S(1)}, u32[]{:S(2)}, u32[]{:S(2)}) collective-permute-start(f32[2304]{0:T(1024)S(1)} %reshape.86), channel_id=1, source_target_pairs={{0,4},{4,0},{1,5},{5,1},{2,6},{6,2},{3,7},{7,3},{8,12},{12,8},{9,1... | collective-permute-start | bytes 27656 | tf_op jit(solution)/shard_map/ppermute | solution.py:258
  139.6 8.4 %collective-permute-start.18 = (bf16[256,384]{1,0:T(8,128)(2,1)S(1)}, bf16[256,384]{1,0:T(8,128)(2,1)S(1)}, u32[]{:S(2)}, u32[]{:S(2)}) collective-permute-start(bf16[256,384]{1,0:T(8,128)(2,1)S(1)} %get-tuple-element.30), channel_id=1, source_target_pairs={{0,3},{1,0},{2,1},{3,2},{4,7},{5,4},{6,5},{7,6},{8,11},{9,8},{10,9... | collective-permute-start | bytes 589832 | tf_op jit(solution)/shard_map/ppermute | solution.py:258
  142.4 7.3 %collective-permute-start.17 = (bf16[256,384]{1,0:T(8,128)(2,1)S(1)}, bf16[256,384]{1,0:T(8,128)(2,1)S(1)}, u32[]{:S(2)}, u32[]{:S(2)}) collective-permute-start(bf16[256,384]{1,0:T(8,128)(2,1)S(1)} %get-tuple-element.31), channel_id=1, source_target_pairs={{0,2},{1,3},{2,0},{3,1},{4,6},{5,7},{6,4},{7,5},{8,10},{9,11},{10,... | collective-permute-start | bytes 589832 | tf_op jit(solution)/shard_map/ppermute | solution.py:258
  142.4 9.0 %collective-permute-start.16 = (bf16[256,384]{1,0:T(8,128)(2,1)S(1)}, bf16[256,384]{1,0:T(8,128)(2,1)S(1)}, u32[]{:S(2)}, u32[]{:S(2)}) collective-permute-start(bf16[256,384]{1,0:T(8,128)(2,1)S(1)} %get-tuple-element.32), channel_id=1, source_target_pairs={{0,1},{1,2},{2,3},{3,0},{4,5},{5,6},{6,7},{7,4},{8,9},{9,10},{10,1... | collective-permute-start | bytes 589832 | tf_op jit(solution)/shard_map/ppermute | solution.py:258
  155.4 6.2 %collective-permute-start.19 = (bf16[128,384]{1,0:T(8,128)(2,1)S(1)}, bf16[128,384]{1,0:T(8,128)(2,1)S(1)}, u32[]{:S(2)}, u32[]{:S(2)}) collective-permute-start(bf16[128,384]{1,0:T(8,128)(2,1)S(1)} %slice.166), channel_id=1, source_target_pairs={{0,4},{4,0},{1,5},{5,1},{2,6},{6,2},{3,7},{7,3},{8,12},{12,8},{9,1... | collective-permute-start | bytes 294920 | tf_op jit(solution)/shard_map/ppermute | solution.py:258
  (25 other events, 299.8 us)

commit v2 on v1

v2 whole, which is shorter than its diff:
```python
import jax
import jax.numpy as jnp
import numpy as np
from jax import lax
from jax.experimental import pallas as pl
from jax.experimental.pallas import tpu as pltpu
from jax.sharding import Mesh
from jax.sharding import PartitionSpec as P

D = 384
HEADS = 6
FF = 1536
EPSILON = 1e-06
FIRST = 512
SECOND = 1408
TAIL = 640
FSDP = ("xl", "y", "core")
SEQ = ("xh", "z")
CHIPS = ("xl", "y", "xh", "z")
X = ("xl", "xh")
BF = jnp.bfloat16
F32 = jnp.float32
VMEM_LIMIT = 36 * 1024 * 1024


def dot(left, right, dims=((1,), (0,))):
    return lax.dot_general(left, right, (dims, ((), ())), preferred_element_type=F32)


def dot_nt(left, right):
    return dot(left, right, ((1,), (1,)))


def dot_tn(left, right):
    return dot(left, right, ((0,), (0,)))


def normalise(values):
    center = values - jnp.mean(values, axis=-1, keepdims=True)
    inverse = lax.rsqrt(jnp.mean(center * center, axis=-1, keepdims=True) + EPSILON)
    return center * inverse, inverse


def norm_back(grad, normed, inverse):
    first = jnp.mean(grad, axis=-1, keepdims=True)
    second = jnp.mean(grad * normed, axis=-1, keepdims=True)
    return inverse * (grad - first - normed * second)


def column_sum(values):
    return jnp.sum(values, axis=0, keepdims=True)


def iota(shape, axis):
    return lax.broadcasted_iota(jnp.int32, shape, axis)


def pick(columns, width):
    return jnp.where(iota((columns.shape[0], width), 1) == columns, 1.0, 0.0).astype(BF)


def one_head(pair, head):
    lane = iota(pair.shape, 1)
    return jnp.where((lane >= 64) == (head % 2 == 1), pair, jnp.zeros_like(pair))


def take_columns(ids_ref):
    row = iota((D, 1), 0)
    device = (row * 43691) >> 17
    j = row - 3 * device
    x = 2 * ((device >> 2) & 1) + (device >> 6)
    here = 2 * ids_ref[3] + ids_ref[0]
    slot = ((device >> 3) + ids_ref[2]) & 1
    slot = slot * 4 + ((x - here) & 3)
    slot = slot * 4 + (((device >> 4) - ids_ref[1]) & 3)
    slot = slot * 4 + ((device - ids_ref[4]) & 3)
    return j, slot * 8


def unpacker(ids_ref, near_ref, far_ref, offset):
    j, base = take_columns(ids_ref)
    half = near_ref.shape[0]
    places = (
        base + j,
        base + 3 + j,
        jnp.where(j < 2, base + 6 + j, -1),
        jnp.where(j == 2, base + 6, -1),
    )

    def unpack(index, start, stop):
        chosen = pick(places[index], 2 * half)
        lanes = slice(offset + start, offset + stop)
        return dot(chosen[:, :half], near_ref[:, lanes]) + dot(chosen[:, half:], far_ref[:, lanes])

    return unpack


def give(ids_ref, targets, whole, third):
    width = targets[0].shape[1]
    more = third.shape[1]
    row = iota((256, 1), 0)
    q = row & 7
    for side, target in enumerate(targets):
        core = (ids_ref[2] + side) & 1
        base = ((row >> 6) * 2 + core) * 24 + ((row >> 3) & 7) * 3
        place = [
            pick(jnp.where((q >= low) & (q < high), base + q + offset, -1), 192)
            for low, high, offset in ((0, 3, 0), (3, 6, -3), (6, 8, -6), (6, 7, -4))
        ]
        for band in range(2):
            rows = slice(band * 192, band * 192 + 192)
            area = slice(band * 256, band * 256 + 256)
            both = dot(place[0], whole[rows, :width]) + dot(place[1], whole[rows, width:])
            target[area, :more] = (both[:, :more] + dot(place[2], third[rows, :])).astype(BF)
            target[area, more : 2 * more] = (
                both[:, more : 2 * more] + dot(place[3], third[rows, :])
            ).astype(BF)
            if 2 * more < width:
                target[area, 2 * more :] = both[:, 2 * more :].astype(BF)


def interleave():
    row = iota((512, 1), 0)
    return pick((row & 3) * 128 + (row >> 2), 512)


def pack_kernel(
    ids_ref,
    biases_ref,
    latents_ref,
    cotangent_ref,
    modulation_ref,
    w_qkv_ref,
    w_out_ref,
    w_fc1_ref,
    w_fc2_ref,
    payload_ref,
    own_ref,
    send_ref,
    condition_ref,
    scratch,
):
    upper = ids_ref[3]
    own_ref[0] = latents_ref[upper]
    own_ref[1] = cotangent_ref[upper]
    send_ref[0] = latents_ref[1 - upper]
    send_ref[1] = cotangent_ref[1 - upper]
    modulation = jnp.where(upper == 1, modulation_ref[1:2, :], modulation_ref[0:1, :])
    condition_ref[...] = jnp.zeros_like(condition_ref)
    for part in range(6):
        condition_ref[part : part + 1, :] = modulation[:, part * D : (part + 1) * D]
    scratch[...] = jnp.zeros_like(scratch)
    scratch[0:3, : 3 * D] = w_qkv_ref[...].astype(F32)
    row, lane = iota((8, 128), 0), iota((8, 128), 1)
    tile = jnp.zeros((8, 128), F32)
    for j in range(3):
        for column in range(8):
            index = 3 * column + j if column < 4 else 12 + 4 * j + column - 4
            tile = jnp.where((row == j) & (lane == column), biases_ref[0:1, index : index + 1], tile)
    scratch[:, 3 * D : 3 * D + 128] = tile
    start = 3 * D + 128
    swap = interleave()
    for block in range(3):
        moved = dot(w_fc1_ref[:, block * 512 : block * 512 + 512], swap)
        for part in range(4):
            lanes = start + part * D + block * 128
            scratch[0:3, lanes : lanes + 128] = moved[:, part * 128 : part * 128 + 128]
    start = start + FF
    rows = w_fc2_ref[...].astype(F32)
    for j in range(3):
        for part in range(4):
            line = 4 * j + part
            scratch[j : j + 1, start + part * D : start + part * D + D] = rows[line : line + 1, :]
    start = start + FF
    scratch[0:3, start : start + D] = w_out_ref[...].astype(F32)

    def place(width, begin, more):
        result = jnp.zeros((8, width), F32)
        group = scratch[:, begin : begin + width]
        result = result + jnp.where(iota((8, width), 0) < 3, group, 0.0)
        group = scratch[:, begin + width : begin + 2 * width]
        scratch_rows = [group[j : j + 1, :] for j in range(3)]
        for j in range(3):
            result = jnp.where(iota((8, width), 0) == 3 + j, scratch_rows[j], result)
        group = scratch[:, begin + 2 * width : begin + 2 * width + more]
        empty = jnp.zeros((1, width - 2 * more), F32)
        ends = [empty] if width > 2 * more else []
        six = jnp.concatenate([group[0:1], group[2:3]] + ends, axis=1)
        seven = jnp.concatenate([group[1:2], jnp.zeros((1, more), F32)] + ends, axis=1)
        result = jnp.where(iota((8, width), 0) == 6, six, result)
        result = jnp.where(iota((8, width), 0) == 7, seven, result)
        return result.astype(BF)

    payload_ref[:, :FIRST] = place(FIRST, 0, 256)
    payload_ref[:, FIRST:] = place(SECOND, 3 * D + 128, TAIL)


def attention_part(
    ids_ref,
    near_ref,
    far_ref,
    token_0,
    token_1,
    token_2,
    token_3,
    condition_ref,
    w_qkv_ref,
    hidden_ref,
    query_ref,
    keys_ref,
    values_ref,
    keys_t,
    probability_ref,
    biases_ref,
    attended_t,
    values_t,
):
    unpack = unpacker(ids_ref, near_ref, far_ref, 0)
    w_qkv_ref[:, :FIRST] = unpack(0, 0, FIRST).astype(BF)
    w_qkv_ref[:, FIRST : 2 * FIRST] = unpack(1, 0, FIRST).astype(BF)
    last = unpack(2, 0, 256) + unpack(3, 256, 512)
    w_qkv_ref[:, 2 * FIRST :] = last[:, :128].astype(BF)
    biases = last[:, 128:].T[:8, :]
    biases_ref[...] = biases
    shift_one, scale_one = condition_ref[0:1, :], condition_ref[1:2, :]
    own = token_0.shape[0]
    for index, token_ref in enumerate((token_0, token_1, token_2, token_3)):
        normed, _ = normalise(token_ref[...].astype(F32))
        hidden = (normed * (1.0 + scale_one) + shift_one).astype(BF)
        rows = slice(index * own, index * own + own)
        hidden_ref[rows, :] = hidden
        keys = dot(hidden, w_qkv_ref[:, D : 2 * D])
        values = dot(hidden, w_qkv_ref[:, 2 * D :]) + biases[1:2, :]
        keys_ref[rows, :] = keys.astype(BF)
        values_ref[rows, :] = values.astype(BF)
        keys_t[:, rows] = keys.astype(BF).T
        values_t[:, rows] = values.astype(BF).T
    query = (dot(hidden_ref[:own, :], w_qkv_ref[:, :D]) + biases[0:1, :]).astype(BF)
    query = query * jnp.asarray(0.125, BF)
    query_ref[...] = query
    for head in range(HEADS):
        tile = slice(head // 2 * 128, head // 2 * 128 + 128)
        cut = slice(head * 64, head * 64 + 64)
        scores = dot_nt(keys_ref[:, tile], one_head(query[:, tile], head))
        exponent = jnp.exp(scores - jnp.max(scores, axis=0, keepdims=True))
        probability = (exponent * (1.0 / column_sum(exponent))).astype(BF)
        probability_ref[head] = probability
        attended_t[cut, :] = dot(values_t[cut, :], probability)


def forward_part(
    ids_ref,
    near_ref,
    far_ref,
    tokens_ref,
    upstream_a,
    upstream_b,
    condition_ref,
    output_a,
    output_b,
    middle_grad_ref,
    attended_grad_ref,
    weighted_ref,
    vectors_ref,
    rows_ref,
    keep_ref,
    send_ref,
    biases_ref,
    attended_t,
    w_fc1,
    w_fc2,
    w_out,
    slope_scr,
    whole,
    third,
):
    unpack = unpacker(ids_ref, near_ref, far_ref, FIRST)
    w_fc1[:, :SECOND] = unpack(0, 0, SECOND).astype(BF)
    group = unpack(1, 0, SECOND).astype(BF)
    w_fc1[:, SECOND:] = group[:, :128]
    last = (unpack(2, 0, TAIL) + unpack(3, TAIL, 2 * TAIL)).astype(BF)
    for part in range(3):
        w_fc2[part * D : (part + 1) * D, :] = group[:, 128 + part * D : 128 + (part + 1) * D]
    w_fc2[3 * D :, :128] = group[:, 128 + 3 * D :]
    w_fc2[3 * D :, 128:] = last[:, :256]
    w_out[...] = last[:, 256:]
    b_out, b_fc2 = biases_ref[2:3, :], biases_ref[3:4, :]
    b_fc1 = jnp.concatenate([biases_ref[4 + i : 5 + i, :] for i in range(4)], axis=1)
    gate_one, shift_two, scale_two, gate_two = (condition_ref[i : i + 1, :] for i in range(2, 6))

    attended = attended_t[...].T.astype(BF)
    branch_one = dot(attended, w_out[...]) + b_out
    middle = tokens_ref[...].astype(F32) + gate_one * branch_one
    normed_two, inverse_two = normalise(middle)
    hidden_two = (normed_two * (1.0 + scale_two) + shift_two).astype(BF)
    inner = dot(hidden_two, w_fc1[...]) + b_fc1
    root = np.sqrt(2.0 / np.pi).astype(np.float32)
    square = inner * inner
    curve = jnp.tanh(root * (inner + 0.044715 * (square * inner)))
    slope_scr[...] = 0.5 * (1.0 + curve) + 0.5 * inner * (1.0 - curve * curve) * (
        root * (1.0 + 3.0 * 0.044715 * square)
    )
    active = (0.5 * inner * (1.0 + curve)).astype(BF)
    branch_two = dot(active, w_fc2[...]) + b_fc2
    output = (middle + gate_two * branch_two).astype(BF)
    side = output_a.shape[0]
    output_a[...] = output[:side]
    output_b[...] = output[side:]

    upstream = jnp.concatenate([upstream_a[...], upstream_b[...]], axis=0).astype(F32)
    rows_ref[...] = jnp.zeros_like(rows_ref)
    vectors_ref[...] = jnp.zeros_like(vectors_ref)
    vectors_ref[5:6, :] = column_sum(upstream * branch_two)
    grad_two = (upstream * gate_two).astype(BF)
    rows_ref[3:4, :] = column_sum(grad_two.astype(F32))
    second = dot_tn(active, grad_two).astype(BF)
    for part in range(3):
        whole[:, FF + part * D : FF + (part + 1) * D] = second[part * D : (part + 1) * D, :]
    whole[:, FF + 3 * D :] = second[3 * D :, :128]
    third[:, :256] = second[3 * D :, 128:]
    grad_inner = (dot_nt(grad_two, w_fc2[...]) * slope_scr[...]).astype(BF)
    whole[:, :FF] = dot_tn(hidden_two, grad_inner).astype(BF)
    inner_sum = column_sum(grad_inner.astype(F32))
    for part in range(4):
        rows_ref[4 + part : 5 + part, :] = inner_sum[:, part * D : (part + 1) * D]
    grad_hidden_two = dot_nt(grad_inner, w_fc1[...])
    vectors_ref[4:5, :] = column_sum(grad_hidden_two * normed_two)
    vectors_ref[3:4, :] = column_sum(grad_hidden_two)
    grad_middle = upstream + norm_back(
        grad_hidden_two * (1.0 + scale_two), normed_two, inverse_two
    )
    middle_grad_ref[...] = grad_middle
    vectors_ref[2:3, :] = column_sum(grad_middle * branch_one)
    grad_one = (grad_middle * gate_one).astype(BF)
    third[:, 256:] = dot_tn(attended, grad_one).astype(BF)
    rows_ref[2:3, :] = column_sum(grad_one.astype(F32))
    grad_attended = dot_nt(grad_one, w_out[...]).astype(BF)
    attended_grad_ref[...] = grad_attended
    products = grad_attended.astype(F32).T * attended_t[...]
    weighted_ref[...] = jnp.zeros_like(weighted_ref)
    for head in range(HEADS):
        weighted_ref[head : head + 1, :] = column_sum(products[head * 64 : head * 64 + 64, :])
    give(ids_ref, (keep_ref, send_ref), whole, third)


def front_kernel(
    ids_ref, near_ref, far_ref, token_0, token_1, token_2, token_3, upstream_a, upstream_b, condition_ref,
    w_qkv_ref, hidden_ref, query_ref, keys_ref, values_ref, keys_t, probability_ref,
    output_a, output_b, middle_grad_ref, attended_grad_ref, weighted_ref, vectors_ref, rows_ref,
    keep_ref, send_ref,
    values_t, biases_ref, attended_t, w_fc1, w_fc2, w_out, slope_scr, whole, third,
):
    attention_part(
        ids_ref, near_ref, far_ref, token_0, token_1, token_2, token_3, condition_ref,
        w_qkv_ref, hidden_ref, query_ref, keys_ref, values_ref, keys_t, probability_ref,
        biases_ref, attended_t, values_t,
    )
    forward_part(
        ids_ref, near_ref, far_ref, token_0, upstream_a, upstream_b, condition_ref,
        output_a, output_b, middle_grad_ref, attended_grad_ref, weighted_ref, vectors_ref, rows_ref,
        keep_ref, send_ref, biases_ref, attended_t, w_fc1, w_fc2, w_out, slope_scr, whole, third,
    )


def backward_kernel(
    token_0, token_1, token_2, token_3, condition_ref,
    w_qkv_ref, query_ref, keys_ref, values_ref, keys_t, probability_ref,
    attended_grad_ref, weighted_ref, vectors_in,
    own_ref, piece_1, piece_2, piece_3, vectors_ref, grad_query_ref, key_grads, value_grads,
    query_t,
):
    own = token_0.shape[0]
    for pair in range(HEADS // 2):
        tile = slice(pair * 128, pair * 128 + 128)
        key_sum = None
        value_sum = None
        for head in (2 * pair, 2 * pair + 1):
            cut = slice(head * 64, head * 64 + 64)
            probability = probability_ref[head]
            grad_head = one_head(attended_grad_ref[:, tile], head)
            grad_probability = dot_nt(values_ref[:, tile], grad_head)
            grad_scores = (
                probability.astype(F32) * (grad_probability - weighted_ref[head : head + 1, :])
            ).astype(BF)
            value_part = dot(probability, grad_head)
            key_part = dot(grad_scores, one_head(query_ref[:, tile], head))
            value_sum = value_part if value_sum is None else value_sum + value_part
            key_sum = key_part if key_sum is None else key_sum + key_part
            query_t[cut, :] = dot(keys_t[cut, :], grad_scores) * 0.125
        key_grads[:, tile] = key_sum.astype(BF)
        value_grads[:, tile] = value_sum.astype(BF)
    grad_query = query_t[...].T.astype(BF)
    grad_query_ref[...] = grad_query
    shift_sum, scale_sum = None, None
    pieces = (own_ref, piece_1, piece_2, piece_3)
    for index, token_ref in enumerate((token_0, token_1, token_2, token_3)):
        rows = slice(index * own, index * own + own)
        grad = dot_nt(key_grads[rows, :], w_qkv_ref[:, D : 2 * D]) + dot_nt(
            value_grads[rows, :], w_qkv_ref[:, 2 * D :]
        )
        if index == 0:
            grad = grad + dot_nt(grad_query, w_qkv_ref[:, :D])
        normed, _ = normalise(token_ref[...].astype(F32))
        shifts, scales = column_sum(grad), column_sum(grad * normed)
        shift_sum = shifts if shift_sum is None else shift_sum + shifts
        scale_sum = scales if scale_sum is None else scale_sum + scales
        pieces[index][:own, :] = grad.astype(pieces[index].dtype)
    vectors_ref[...] = vectors_in[...]
    vectors_ref[0:1, :] = shift_sum
    vectors_ref[1:2, :] = scale_sum
    for piece in pieces[1:]:
        piece[own:, :] = two_parts(vectors_ref[...])


def weight_kernel(
    ids_ref, hidden_ref, grad_query_ref, key_grads, value_grads, rows_ref,
    keep_ref, send_ref,
    whole, third, tall,
):
    own = grad_query_ref.shape[0]
    tall[...] = jnp.zeros_like(tall)
    tall[0:8, :] = rows_ref[...]
    tall[0:1, :] = column_sum(grad_query_ref[...].astype(F32))
    tall[1:2, :] = column_sum(value_grads[...].astype(F32))
    whole[:, :D] = dot_tn(hidden_ref[:own, :], grad_query_ref[...]).astype(BF)
    whole[:, D : 2 * D] = dot_tn(hidden_ref[...], key_grads[...]).astype(BF)
    value_weight = dot_tn(hidden_ref[...], value_grads[...]).astype(BF)
    whole[:, 2 * D :] = value_weight[:, :256]
    third[:, :128] = value_weight[:, 256:]
    third[:, 128:] = tall[...].T.astype(BF)
    give(ids_ref, (keep_ref, send_ref), whole, third)


def two_parts(vectors):
    high = vectors.astype(BF).astype(F32)
    return jnp.concatenate([high, vectors - high], axis=0).astype(BF)


def one_part(parts):
    parts = parts.astype(F32)
    return parts[:8] + parts[8:]


def final_kernel(
    tokens_ref, condition_ref, middle_ref, own_ref, a_ref, b_ref, c_ref, vectors_ref, output_ref,
    half_ref, send_ref, sums_ref,
):
    own = own_ref.shape[0]
    side = own // 2
    grad = own_ref[...]
    sums = vectors_ref[...]
    for piece in (a_ref, b_ref, c_ref):
        grad = grad + piece[:own, :].astype(F32)
        sums = sums + one_part(piece[own:, :])
    normed, inverse = normalise(tokens_ref[...].astype(F32))
    result = (
        middle_ref[...] + norm_back(grad * (1.0 + condition_ref[1:2, :]), normed, inverse)
    ).astype(BF)
    half_ref[...] = result[:side]
    send_ref[:side, :] = result[side:]
    send_ref[side : 2 * side, :] = output_ref[...]
    send_ref[2 * side :, :] = two_parts(sums)
    sums_ref[...] = sums


def join_kernel(
    ids_ref, output_ref, grad_ref, other_ref, sums_ref,
    output_out, grad_out, modulation_out,
):
    upper = ids_ref[3]
    side = output_ref.shape[0]
    output_out[upper] = output_ref[...]
    output_out[1 - upper] = other_ref[side : 2 * side, :]
    grad_out[upper] = grad_ref[...]
    grad_out[1 - upper] = other_ref[:side, :]
    mine, other = sums_ref[...], one_part(other_ref[2 * side :, :])
    low = jnp.where(upper == 1, other, mine)
    high = jnp.where(upper == 1, mine, other)
    for part in range(6):
        cut = slice(part * D, part * D + D)
        modulation_out[0:1, cut] = low[part : part + 1, :]
        modulation_out[1:2, cut] = high[part : part + 1, :]


def sum_kernel(pieces_ref, qkv_ref, bias_ref, fc1_ref, fc2_ref, out_ref):
    total = pieces_ref[0].astype(F32)
    for index in range(1, pieces_ref.shape[0]):
        total = total + pieces_ref[index].astype(F32)
    small, total = total[:, :FIRST], total[:, FIRST:]
    qkv_ref[:, :FIRST] = small[0:3]
    qkv_ref[:, FIRST : 2 * FIRST] = small[3:6]
    last = jnp.concatenate([small[6:8, :256], small[6:7, 256:]], axis=0)
    qkv_ref[:, 2 * FIRST :] = last[:, :128]
    bias_ref[...] = last[:, 128:]
    swap = interleave()
    one, two = total[0:3], total[3:6]
    last = jnp.concatenate([total[6:8, :TAIL], total[6:7, TAIL : 2 * TAIL]], axis=0)
    fc1 = jnp.concatenate([one, two[:, :128]], axis=1)
    for block in range(3):
        rest = jnp.concatenate(
            [fc1[:, i * D + block * 128 : i * D + block * 128 + 128] for i in range(4)], axis=1
        )
        moved = None
        for _ in range(3):
            part = rest.astype(BF)
            rest = rest - part.astype(F32)
            step = dot_nt(part, swap)
            moved = step if moved is None else moved + step
        fc1_ref[:, block * 512 : block * 512 + 512] = moved
    fc2 = jnp.concatenate([two[:, 128:], last[:, :256]], axis=1)
    for j in range(3):
        for part in range(4):
            line = 4 * j + part
            fc2_ref[line : line + 1, :] = fc2[j : j + 1, part * D : part * D + D]
    out_ref[...] = last[:, 256:]


def shift(array, axis, step, size):
    return lax.ppermute(array, axis, [(i, (i + step) % size) for i in range(size)])


def shift_x(array, step):
    moves = []
    for index in range(4):
        place = (index % 2) * 2 + index // 2
        there = (place + step) % 4
        moves.append((index, (there % 2) * 2 + there // 2))
    return lax.ppermute(array, X, moves)


def ring(array, axis):
    return [array] + [shift(array, axis, -k, 4) for k in range(1, 4)]


def sds(*shape, dtype=BF):
    return jax.ShapeDtypeStruct(shape, dtype)


def vmem(*shape, dtype=BF):
    return pltpu.VMEM(shape, dtype)


def hold(array):
    return pltpu.with_memory_space_constraint(array, pltpu.VMEM)


def far(array):
    return pltpu.with_memory_space_constraint(array, pltpu.HBM)


def call(kernel, out_shape, scratch, ids, *operands):
    specs = [] if ids is None else [pl.BlockSpec(memory_space=pltpu.SMEM)]
    given = operands if ids is None else (ids, *operands)
    specs += [pl.BlockSpec(memory_space=pltpu.VMEM)] * (len(given) - len(specs))
    return pl.pallas_call(
        kernel,
        out_shape=out_shape,
        in_specs=specs,
        out_specs=tuple(pl.BlockSpec(memory_space=pltpu.VMEM) for _ in out_shape),
        scratch_shapes=scratch,
        compiler_params=pltpu.CompilerParams(vmem_limit_bytes=VMEM_LIMIT),
    )(*given)


def body(latents, modulation, w_qkv, b_query, b_value, w_out, b_out, w_fc1, b_fc1, w_fc2, b_fc2, cotangent):
    side = latents.shape[1]
    own = 2 * side
    length = 4 * own
    ids = jnp.stack([lax.axis_index(a) for a in ("xl", "y", "core", "xh", "z")]).astype(jnp.int32)
    biases = sum(
        jnp.pad(b.astype(F32)[None], ((0, 0), (first, 128 - first - b.shape[0])))
        for b, first in ((b_query, 0), (b_value, 3), (b_out, 6), (b_fc2, 9), (b_fc1, 12))
    )
    payload, own_pair, send_pair, condition = call(
        pack_kernel,
        (sds(8, FIRST + SECOND), sds(2, side, D), sds(2, side, D), sds(8, D, dtype=F32)),
        [vmem(8, 3 * D + 128 + 2 * FF + D, dtype=F32)],
        ids, biases, *(far(a) for a in (latents, cotangent, modulation, w_qkv, w_out, w_fc1, w_fc2)),
    )

    swapped = shift(send_pair, "xh", 1, 2)
    column = jnp.stack(ring(payload, "z"))
    plane = jnp.stack(ring(column, "y"))
    plane, swapped = lax.optimization_barrier((plane, swapped))
    tokens = jnp.concatenate([own_pair[0], swapped[0]])
    all_tokens = ring(tokens, "z")
    before, after = shift_x(plane, 1), shift_x(plane, -1)
    half = plane.shape[0] // 2
    opposite = jnp.concatenate([shift_x(before[:half], 1), shift_x(after[half:], -1)])
    near = jnp.stack([plane, after, opposite, before]).reshape(-1, FIRST + SECOND)
    near, all_tokens = lax.optimization_barrier((near, all_tokens))
    other = shift(near, "core", 1, 2)

    (
        w_all, hidden, query, keys, values, keys_t, probability,
        output_a, output_b, middle_grad, attended_grad, weighted, vectors, bias_sums, keep_two, send_two,
    ) = call(
        front_kernel,
        (
            vmem(D, 3 * D),
            vmem(length, D),
            vmem(own, D),
            vmem(length, D),
            vmem(length, D),
            vmem(D, length),
            vmem(HEADS, length, own),
            sds(side, D),
            sds(side, D),
            vmem(own, D, dtype=F32),
            vmem(own, D),
            vmem(8, own, dtype=F32),
            vmem(8, D, dtype=F32),
            vmem(8, D, dtype=F32),
            vmem(512, SECOND),
            vmem(512, SECOND),
        ),
        [
            vmem(D, length),
            vmem(8, D, dtype=F32),
            vmem(D, own, dtype=F32),
            vmem(D, FF),
            vmem(FF, D),
            vmem(D, D),
            vmem(own, FF, dtype=F32),
            vmem(D, 2 * SECOND),
            vmem(D, TAIL),
        ],
        ids, hold(near), hold(other), *(hold(t) for t in all_tokens), own_pair[1], swapped[1], condition,
    )
    other_two = shift(send_two, "core", 1, 2)

    hidden_own, piece_1, piece_2, piece_3, vectors, grad_query, key_grads, value_grads = call(
        backward_kernel,
        (
            vmem(own, D, dtype=F32),
            vmem(own + 16, D),
            vmem(own + 16, D),
            vmem(own + 16, D),
            vmem(8, D, dtype=F32),
            vmem(own, D),
            vmem(length, D),
            vmem(length, D),
        ),
        [vmem(D, own, dtype=F32)],
        None, *(hold(t) for t in all_tokens), condition,
        *(
            hold(a)
            for a in (w_all, query, keys, values, keys_t, probability, attended_grad, weighted, vectors)
        ),
    )
    arrived = [shift(p, "z", k, 4) for k, p in ((1, piece_1), (2, piece_2), (3, piece_3))]
    keep_one, send_one = call(
        weight_kernel,
        (vmem(512, FIRST), vmem(512, FIRST)),
        [vmem(D, 2 * FIRST), vmem(D, 256), vmem(128, D, dtype=F32)],
        ids, *(hold(a) for a in (hidden, grad_query, key_grads, value_grads, bias_sums)),
    )
    other_one = shift(send_one, "core", 1, 2)
    mixed = jnp.concatenate([keep_one + other_one, keep_two + other_two], axis=1)
    grad_a, grad_b, sums = call(
        final_kernel,
        (sds(side, D), vmem(2 * side + 16, D), vmem(8, D, dtype=F32)),
        [],
        None, hold(tokens), condition, hold(middle_grad), hold(hidden_own),
        *(hold(a) for a in arrived), hold(vectors), output_b,
    )
    mixed, grad_b = lax.optimization_barrier((mixed, grad_b))
    pieces = lax.all_to_all(mixed.reshape(64, 8, FIRST + SECOND), CHIPS, 0, 0, tiled=True)
    grad_back = shift(grad_b, "xh", 1, 2)
    output, input_grad, modulation_grad = call(
        join_kernel,
        (sds(2, side, D), sds(2, side, D), sds(2, 6 * D, dtype=F32)),
        [],
        ids, output_a, grad_a, hold(grad_back), hold(sums),
    )
    grad_qkv, grad_bias, grad_fc1, grad_fc2, grad_out = call(
        sum_kernel,
        (
            sds(3, 3 * D, dtype=F32),
            sds(3, 128, dtype=F32),
            sds(3, FF, dtype=F32),
            sds(12, D, dtype=F32),
            sds(3, D, dtype=F32),
        ),
        [],
        None, hold(pieces),
    )
    return (
        output,
        input_grad,
        modulation_grad,
        grad_qkv,
        grad_bias[:, 0],
        grad_bias[:, 1],
        grad_out,
        grad_bias[:, 2],
        grad_fc1,
        grad_bias[:, 4:8].reshape(12),
        grad_fc2,
        grad_bias[:, 3],
    )


def solution(mesh):
    chips = Mesh(mesh.devices.reshape(2, 4, 2, 2, 4), ("xl", "y", "core", "xh", "z"))
    rows = P(FSDP + SEQ, None)
    line = P(FSDP + SEQ)
    tokens = P(FSDP, SEQ, None)
    condition = P(FSDP, None)
    in_specs = (tokens, condition, rows, line, line, rows, line, rows, line, rows, line, tokens)
    out_specs = (tokens, tokens, condition, rows, line, line, rows, line, rows, line, rows, line)
    return jax.shard_map(body, mesh=chips, in_specs=in_specs, out_specs=out_specs, check_vma=False)
```

time: 171 us -> 143 us (0.84); the launches traced: 168 us -> 142 us
  local copies, waits for them, and re-layouts: 21.3 us -> 1.56 us
  other arithmetic: 10.5 us -> 3.19 us
  starting transfers between devices: 46.2 us -> 42.1 us
  waiting for transfers between devices: 58.9 us -> 62.6 us
  Pallas kernels: 30 us -> 32 us
    ppermute x21 -> x17, waiting for transfers between devices: 44.2 us -> 53.9 us  [shift(): lax.ppermute(array, axis, [(i, (i + step) % size) for i in range(size)])]
    ppermute x21 -> x17, starting transfers between devices: 32.8 us -> 26.1 us  [shift(): lax.ppermute(array, axis, [(i, (i + step) % size) for i in range(size)])]
    ppermute x4, waiting for transfers between devices: 14.6 us -> 8.65 us  [shift_x(): return lax.ppermute(array, X, moves)]
    slice x16 -> x2, local copies, waits for them, and re-layouts: 5.32 us -> 0.04 us  [the longest x1 0.02 us: body(): after[half:]]
    reshape x8 -> x0, local copies, waits for them, and re-layouts: 4.67 us -> none  [the longest x1 1.34 us: body(): fc1 = w_fc1.reshape(3, D, 4).transpose(0, 2, 1).reshape(3, FF)]
    another operation x10 -> x4, other arithmetic: 4.05 us -> 0.45 us  [the longest x2 0.35 us: body(): jnp.stack([plane, after, opposite, before]).reshape(-1, FIRST + SECOND)]
    broadcast_in_dim x7 -> x0, local copies, waits for them, and re-layouts: 3.1 us -> none  [the longest x4 3.02 us: body(): b[:, None]]
    all_to_all x1 -> x0, other arithmetic: 3.04 us -> none  [body(): pieces = lax.all_to_all(mixed, CHIPS, 0, 0, tiled=True)]
  transfers between devices with their start and end apart: 26 -> 22, of which waited for: 16 -> 14; matrix products, arithmetic and copies ran while one was open for 7% -> 0% of each run, Pallas kernels for 1% -> 6%
where the time goes in v2:
time: 143 us; the launch traced here: 142 us
  waiting for transfers between devices  62.6 us (44%)
  starting transfers between devices  42.1 us (29%)
  Pallas kernels  32 us (22%)
  other arithmetic  3.19 us (2%)
  local copies, waits for them, and re-layouts  1.56 us (1%)
    ppermute x17, waiting for transfers between devices, shift(): lax.ppermute(array, axis, [(i, (i + step) % size) for i in range(size)])  53.9 us
    pallas_call x7, Pallas kernels, call(): pl.pallas_call(kernel, out_shape=out_shape, in_specs=specs, out_specs=tup...  32 us
    ppermute x17, starting transfers between devices, shift(): lax.ppermute(array, axis, [(i, (i + step) % size) for i in range(size)])  26.1 us
    all_to_all x1, starting transfers between devices, body(): lax.all_to_all(mixed.reshape(64, 8, FIRST + SECOND), CHIPS, 0, 0, tiled=T...  9.45 us
    ppermute x4, waiting for transfers between devices, shift_x(): return lax.ppermute(array, X, moves)  8.65 us
    ppermute x4, starting transfers between devices, shift_x(): return lax.ppermute(array, X, moves)  6.61 us
  transfers between devices with their start and end apart: 22, of which 14 were waited for; matrix products, arithmetic and copies ran while one was open for 0% of the time, Pallas kernels for 6%

profile of v2, /device:TPU:8, one launch (start us, length us, event | category | flops | bytes accessed | tf_op | source)
XLA Modules:
  0.0 142.3 jit_solution(9376686658214167368)
XLA Ops:
  3.0 2.0 %collective-permute-start.2 = (bf16[8,1920]{1,0:T(8,128)(2,1)S(1)}, bf16[8,1920]{1,0:T(8,128)(2,1)S(1)}, u32[]{:S(2)}, u32[]{:S(2)}) collective-permute-start(bf16[8,1920]{1,0:T(8,128)(2,1)S(1)} %get-tuple-element.62), channel_id=1, source_target_pairs={{0,1},{1,2},{2,3},{3,0},{4,5},{5,6},{6,7},{7,4},{8,9},{9,10},{10,1... | collective-permute-start | bytes 92168 | tf_op jit(solution)/shard_map/ppermute | solution.py:519
  5.0 3.6 %collective-permute-start.1 = (bf16[8,1920]{1,0:T(8,128)(2,1)S(1)}, bf16[8,1920]{1,0:T(8,128)(2,1)S(1)}, u32[]{:S(2)}, u32[]{:S(2)}) collective-permute-start(bf16[8,1920]{1,0:T(8,128)(2,1)S(1)} %get-tuple-element.62), channel_id=1, source_target_pairs={{0,2},{1,3},{2,0},{3,1},{4,6},{5,7},{6,4},{7,5},{8,10},{9,11},{10,... | collective-permute-start | bytes 92168 | tf_op jit(solution)/shard_map/ppermute | solution.py:519
  10.8 1.7 %collective-permute-done = bf16[8,1920]{1,0:T(8,128)(2,1)S(1)} collective-permute-done((bf16[8,1920]{1,0:T(8,128)(2,1)S(1)}, bf16[8,1920]{1,0:T(8,128)(2,1)S(1)}, u32[]{:S(2)}, u32[]{:S(2)}) %collective-permute-start) | collective-permute-done | bytes 30752 | tf_op jit(solution)/shard_map/ppermute | solution.py:519
  12.5 2.4 %collective-permute-start.4 = (bf16[4,8,1920]{2,1,0:T(8,128)(2,1)S(1)}, bf16[4,8,1920]{2,1,0:T(8,128)(2,1)S(1)}, u32[]{:S(2)}, u32[]{:S(2)}) collective-permute-start(bf16[4,8,1920]{2,1,0:T(8,128)(2,1)S(1)} %get-tuple-element.121), channel_id=1, source_target_pairs={{0,32},{16,48},{32,0},{48,16},{1,33},{17,49},{33,1},{49,17},{2,34}... | collective-permute-start | bytes 368648 | tf_op jit(solution)/shard_map/ppermute | solution.py:519
  16.9 3.0 %collective-permute-start.6 = (bf16[2,128,384]{2,1,0:T(8,128)(2,1)S(1)}, bf16[2,128,384]{2,1,0:T(8,128)(2,1)S(1)}, u32[]{:S(2)}, u32[]{:S(2)}) collective-permute-start(bf16[2,128,384]{2,1,0:T(8,128)(2,1)S(1)} %get-tuple-element.63), channel_id=1, source_target_pairs={{0,4},{4,0},{1,5},{5,1},{2,6},{6,2},{3,7},{7,3},{8,12},{12,8},{9,1... | collective-permute-start | bytes 589832 | tf_op jit(solution)/shard_map/ppermute | solution.py:519
  21.2 2.9 %collective-permute-done.6 = bf16[2,128,384]{2,1,0:T(8,128)(2,1)S(1)} collective-permute-done((bf16[2,128,384]{2,1,0:T(8,128)(2,1)S(1)}, bf16[2,128,384]{2,1,0:T(8,128)(2,1)S(1)}, u32[]{:S(2)}, u32[]{:S(2)}) %collective-permute-start.6) | collective-permute-done | bytes 196640 | tf_op jit(solution)/shard_map/ppermute | solution.py:519
  25.6 1.8 %collective-permute-start.7 = (bf16[4,4,8,1920]{3,2,1,0:T(8,128)(2,1)S(1)}, bf16[4,4,8,1920]{3,2,1,0:T(8,128)(2,1)S(1)}, u32[]{:S(2)}, u32[]{:S(2)}) collective-permute-start(bf16[4,4,8,1920]{3,2,1,0:T(8,128)(2,1)S(1)} %pad_maximum_fusion.2), channel_id=1, source_target_pairs={{0,68},{4,64},{64,0},{68,4},{1,69},{5,65},{65,1},{69,5},{2,70},{6,... | collective-permute-start | bytes 1474568 | tf_op jit(solution)/shard_map/ppermute | solution.py:528
  27.4 8.0 %collective-permute-done.8 = bf16[4,4,8,1920]{3,2,1,0:T(8,128)(2,1)S(1)} collective-permute-done((bf16[4,4,8,1920]{3,2,1,0:T(8,128)(2,1)S(1)}, bf16[4,4,8,1920]{3,2,1,0:T(8,128)(2,1)S(1)}, u32[]{:S(2)}, u32[]{:S(2)}) %collective-permute-start.8) | collective-permute-done | bytes 491552 | tf_op jit(solution)/shard_map/ppermute | solution.py:528
  35.4 1.5 %collective-permute-start.9 = (bf16[2,4,8,1920]{3,2,1,0:T(8,128)(2,1)S(1)}, bf16[2,4,8,1920]{3,2,1,0:T(8,128)(2,1)S(1)}, u32[]{:S(2)}, u32[]{:S(2)}) collective-permute-start(bf16[2,4,8,1920]{3,2,1,0:T(8,128)(2,1)S(1)} %slice.44), channel_id=1, source_target_pairs={{0,64},{4,68},{64,4},{68,0},{1,65},{5,69},{65,5},{69,1},{2,66},{6,... | collective-permute-start | bytes 737288 | tf_op jit(solution)/shard_map/ppermute | solution.py:528
  37.0 1.8 %collective-permute-start.10 = (bf16[2,4,8,1920]{3,2,1,0:T(8,128)(2,1)S(1)}, bf16[2,4,8,1920]{3,2,1,0:T(8,128)(2,1)S(1)}, u32[]{:S(2)}, u32[]{:S(2)}) collective-permute-start(bf16[2,4,8,1920]{3,2,1,0:T(8,128)(2,1)S(1)} %slice.45), channel_id=1, source_target_pairs={{0,68},{4,64},{64,0},{68,4},{1,69},{5,65},{65,1},{69,5},{2,70},{6,... | collective-permute-start | bytes 737288 | tf_op jit(solution)/shard_map/ppermute | solution.py:528
  39.0 3.4 %collective-permute-start.12 = (bf16[256,384]{1,0:T(8,128)(2,1)S(1)}, bf16[256,384]{1,0:T(8,128)(2,1)S(1)}, u32[]{:S(2)}, u32[]{:S(2)}) collective-permute-start(bf16[256,384]{1,0:T(8,128)(2,1)S(1)} %pad_maximum_fusion.3.token_0.tokens_ref), channel_id=1, source_target_pairs={{0,2},{1,3},{2,0},{3,1},{4,6},{5,7},{6,4},{7,5},{8,10},{9,11},{10,... | collective-permute-start | bytes 589832 | tf_op jit(solution)/shard_map/ppermute | solution.py:519
  44.1 1.8 %collective-permute-done.13.token_3 = bf16[256,384]{1,0:T(8,128)(2,1)S(1)} collective-permute-done((bf16[256,384]{1,0:T(8,128)(2,1)S(1)}, bf16[256,384]{1,0:T(8,128)(2,1)S(1)}, u32[]{:S(2)}, u32[]{:S(2)}) %collective-permute-start.13) | collective-permute-done | bytes 196640 | tf_op jit(solution)/shard_map/ppermute | solution.py:519
  45.8 2.2 %collective-permute-done.12.token_2 = bf16[256,384]{1,0:T(8,128)(2,1)S(1)} collective-permute-done((bf16[256,384]{1,0:T(8,128)(2,1)S(1)}, bf16[256,384]{1,0:T(8,128)(2,1)S(1)}, u32[]{:S(2)}, u32[]{:S(2)}) %collective-permute-start.12) | collective-permute-done | bytes 196640 | tf_op jit(solution)/shard_map/ppermute | solution.py:519
  48.8 4.0 %collective-permute-done.14.far_ref = bf16[512,1920]{1,0:T(8,128)(2,1)S(1)} collective-permute-done((bf16[512,1920]{1,0:T(8,128)(2,1)S(1)}, bf16[512,1920]{1,0:T(8,128)(2,1)S(1)}, u32[]{:S(2)}, u32[]{:S(2)}) %collective-permute-start.14) | collective-permute-done | bytes 1966112 | tf_op jit(solution)/shard_map/ppermute | solution.py:519
  52.8 19.5 %shard_map.212 = (bf16[384,1152]{1,0:T(8,128)(2,1)S(1)}, bf16[1024,384]{1,0:T(8,128)(2,1)S(1)}, bf16[256,384]{1,0:T(8,128)(2,1)S(1)}, bf16[1024,384]{1,0:T(8,128...) custom-call(s32[5]{0:T(128)S(1)} %stack.68.ids_ref, ...), custom_call_target="tpu_custom_call" | custom-call | tf_op jit(solution)/shard_map/pallas_call | solution.py:555
  72.5 4.7 %shard_map.213 = (f32[256,384]{1,0:T(8,128)S(1)}, bf16[272,384]{1,0:T(8,128)(2,1)S(1)}, bf16[272,384]{1,0:T(8,128)(2,1)S(1)}, bf16[272,384]{1,0:T(8,128)(2,1)S(1...) custom-call(bf16[256,384]{1,0:T(8,128)(2,1)S(1)} %pad_maximum_fusion, ...), custom_call_target="tpu_custom_call" | custom-call | tf_op jit(solution)/shard_map/pallas_call | solution.py:555
  77.2 2.6 %shard_map.215 = (bf16[512,512]{1,0:T(8,128)(2,1)S(1)}, bf16[512,512]{1,0:T(8,128)(2,1)S(1)}) custom-call(s32[5]{0:T(128)S(1)} %stack.68.ids_ref, bf16[1024,384]{1,0:T(8,128)(2,1)S(1)} %get-tuple-element.91.hidden_ref, bf16[256,384]{1,0:T(8,128)(2,1)S(1)} %get-tuple-element.92.grad_query_ref, bf16[1024,384]{1,0:T(8,128)(2,1)S(1)} %get-tuple-element.93.key_grads, ...), custom_call_target="tpu_custom_call" | custom-call | tf_op jit(solution)/shard_map/pallas_call | solution.py:555
  81.2 3.2 %collective-permute-start.16 = (bf16[272,384]{1,0:T(8,128)(2,1)S(1)}, bf16[272,384]{1,0:T(8,128)(2,1)S(1)}, u32[]{:S(2)}, u32[]{:S(2)}) collective-permute-start(bf16[272,384]{1,0:T(8,128)(2,1)S(1)} %get-tuple-element.86), channel_id=1, source_target_pairs={{0,2},{1,3},{2,0},{3,1},{4,6},{5,7},{6,4},{7,5},{8,10},{9,11},{10,... | collective-permute-start | bytes 626696 | tf_op jit(solution)/shard_map/ppermute | solution.py:519
  84.4 4.3 %collective-permute-done.15.a_ref = bf16[272,384]{1,0:T(8,128)(2,1)S(1)} collective-permute-done((bf16[272,384]{1,0:T(8,128)(2,1)S(1)}, bf16[272,384]{1,0:T(8,128)(2,1)S(1)}, u32[]{:S(2)}, u32[]{:S(2)}) %collective-permute-start.15) | collective-permute-done | bytes 208928 | tf_op jit(solution)/shard_map/ppermute | solution.py:519
  88.7 5.4 %collective-permute-done.16.b_ref = bf16[272,384]{1,0:T(8,128)(2,1)S(1)} collective-permute-done((bf16[272,384]{1,0:T(8,128)(2,1)S(1)}, bf16[272,384]{1,0:T(8,128)(2,1)S(1)}, u32[]{:S(2)}, u32[]{:S(2)}) %collective-permute-start.16) | collective-permute-done | bytes 208928 | tf_op jit(solution)/shard_map/ppermute | solution.py:519
  96.4 9.4 %all-to-all-start = ((bf16[64,8,1920]{2,1,0:T(8,128)(2,1)}), bf16[64,8,1920]{2,1,0:T(8,128)(2,1)S(1)}, u32[]{:S(2)}, u32[]{:S(2)}) async-start(bf16[64,8,1920]{2,1,0:T(8,128)(2,1)} %bitcast.37), calls=%async_computation | async-start | bytes 3932160 | tf_op jit(solution)/shard_map/all_to_all | solution.py:668
  105.8 3.0 %collective-permute-start.20 = (bf16[272,384]{1,0:T(8,128)(2,1)S(1)}, bf16[272,384]{1,0:T(8,128)(2,1)S(1)}, u32[]{:S(2)}, u32[]{:S(2)}) collective-permute-start(bf16[272,384]{1,0:T(8,128)(2,1)S(1)} %get-tuple-element.101), channel_id=1, source_target_pairs={{0,4},{4,0},{1,5},{5,1},{2,6},{6,2},{3,7},{7,3},{8,12},{12,8},{9,1... | collective-permute-start | bytes 626696 | tf_op jit(solution)/shard_map/ppermute | solution.py:519
  108.9 28.6 %collective-permute-done.20.other_ref = bf16[272,384]{1,0:T(8,128)(2,1)S(1)} collective-permute-done((bf16[272,384]{1,0:T(8,128)(2,1)S(1)}, bf16[272,384]{1,0:T(8,128)(2,1)S(1)}, u32[]{:S(2)}, u32[]{:S(2)}) %collective-permute-start.20) | collective-permute-done | bytes 208928 | tf_op jit(solution)/shard_map/ppermute | solution.py:519
  138.8 2.1 %shard_map.217 = (f32[3,1152]{1,0:T(4,128)}, f32[3,128]{1,0:T(4,128)S(1)}, f32[3,1536]{1,0:T(4,128)}, f32[12,384]{1,0:T(8,128)}, f32[3,384]{1,0:T(4,128)}) custom-call(bf16[64,8,1920]{2,1,0:T(8,128)(2,1)S(1)} %all-to-all-done.pieces_ref), custom_call_target="tpu_custom_call" | custom-call | tf_op jit(solution)/shard_map/pallas_call | solution.py:555
  (44 shorter events, 18.5 us)
Async XLA Ops:
  3.0 6.6 %collective-permute-start.2 = (bf16[8,1920]{1,0:T(8,128)(2,1)S(1)}, bf16[8,1920]{1,0:T(8,128)(2,1)S(1)}, u32[]{:S(2)}, u32[]{:S(2)}) collective-permute-start(bf16[8,1920]{1,0:T(8,128)(2,1)S(1)} %get-tuple-element.62), channel_id=1, source_target_pairs={{0,1},{1,2},{2,3},{3,0},{4,5},{5,6},{6,7},{7,4},{8,9},{9,10},{10,1... | collective-permute-start | bytes 92168 | tf_op jit(solution)/shard_map/ppermute | solution.py:519
  5.0 5.8 %collective-permute-start.1 = (bf16[8,1920]{1,0:T(8,128)(2,1)S(1)}, bf16[8,1920]{1,0:T(8,128)(2,1)S(1)}, u32[]{:S(2)}, u32[]{:S(2)}) collective-permute-start(bf16[8,1920]{1,0:T(8,128)(2,1)S(1)} %get-tuple-element.62), channel_id=1, source_target_pairs={{0,2},{1,3},{2,0},{3,1},{4,6},{5,7},{6,4},{7,5},{8,10},{9,11},{10,... | collective-permute-start | bytes 92168 | tf_op jit(solution)/shard_map/ppermute | solution.py:519
  8.6 3.9 %collective-permute-start = (bf16[8,1920]{1,0:T(8,128)(2,1)S(1)}, bf16[8,1920]{1,0:T(8,128)(2,1)S(1)}, u32[]{:S(2)}, u32[]{:S(2)}) collective-permute-start(bf16[8,1920]{1,0:T(8,128)(2,1)S(1)} %get-tuple-element.62), channel_id=1, source_target_pairs={{0,3},{1,0},{2,1},{3,2},{4,7},{5,4},{6,5},{7,6},{8,11},{9,8},{10,9... | collective-permute-start | bytes 92168 | tf_op jit(solution)/shard_map/ppermute | solution.py:519
  12.5 7.4 %collective-permute-start.4 = (bf16[4,8,1920]{2,1,0:T(8,128)(2,1)S(1)}, bf16[4,8,1920]{2,1,0:T(8,128)(2,1)S(1)}, u32[]{:S(2)}, u32[]{:S(2)}) collective-permute-start(bf16[4,8,1920]{2,1,0:T(8,128)(2,1)S(1)} %get-tuple-element.121), channel_id=1, source_target_pairs={{0,32},{16,48},{32,0},{48,16},{1,33},{17,49},{33,1},{49,17},{2,34}... | collective-permute-start | bytes 368648 | tf_op jit(solution)/shard_map/ppermute | solution.py:519
  14.9 5.5 %collective-permute-start.3 = (bf16[4,8,1920]{2,1,0:T(8,128)(2,1)S(1)}, bf16[4,8,1920]{2,1,0:T(8,128)(2,1)S(1)}, u32[]{:S(2)}, u32[]{:S(2)}) collective-permute-start(bf16[4,8,1920]{2,1,0:T(8,128)(2,1)S(1)} %get-tuple-element.121), channel_id=1, source_target_pairs={{0,48},{16,0},{32,16},{48,32},{1,49},{17,1},{33,17},{49,33},{2,50}... | collective-permute-start | bytes 368648 | tf_op jit(solution)/shard_map/ppermute | solution.py:519
  16.2 4.9 %collective-permute-start.5 = (bf16[4,8,1920]{2,1,0:T(8,128)(2,1)S(1)}, bf16[4,8,1920]{2,1,0:T(8,128)(2,1)S(1)}, u32[]{:S(2)}, u32[]{:S(2)}) collective-permute-start(bf16[4,8,1920]{2,1,0:T(8,128)(2,1)S(1)} %get-tuple-element.121), channel_id=1, source_target_pairs={{0,16},{16,32},{32,48},{48,0},{1,17},{17,33},{33,49},{49,1},{2,18}... | collective-permute-start | bytes 368648 | tf_op jit(solution)/shard_map/ppermute | solution.py:519
  16.9 7.2 %collective-permute-start.6 = (bf16[2,128,384]{2,1,0:T(8,128)(2,1)S(1)}, bf16[2,128,384]{2,1,0:T(8,128)(2,1)S(1)}, u32[]{:S(2)}, u32[]{:S(2)}) collective-permute-start(bf16[2,128,384]{2,1,0:T(8,128)(2,1)S(1)} %get-tuple-element.63), channel_id=1, source_target_pairs={{0,4},{4,0},{1,5},{5,1},{2,6},{6,2},{3,7},{7,3},{8,12},{12,8},{9,1... | collective-permute-start | bytes 589832 | tf_op jit(solution)/shard_map/ppermute | solution.py:519
  24.1 11.3 %collective-permute-start.8 = (bf16[4,4,8,1920]{3,2,1,0:T(8,128)(2,1)S(1)}, bf16[4,4,8,1920]{3,2,1,0:T(8,128)(2,1)S(1)}, u32[]{:S(2)}, u32[]{:S(2)}) collective-permute-start(bf16[4,4,8,1920]{3,2,1,0:T(8,128)(2,1)S(1)} %pad_maximum_fusion.2), channel_id=1, source_target_pairs={{0,64},{4,68},{64,4},{68,0},{1,65},{5,69},{65,5},{69,1},{2,66},{6,... | collective-permute-start | bytes 1474568 | tf_op jit(solution)/shard_map/ppermute | solution.py:528
  25.6 11.4 %collective-permute-start.7 = (bf16[4,4,8,1920]{3,2,1,0:T(8,128)(2,1)S(1)}, bf16[4,4,8,1920]{3,2,1,0:T(8,128)(2,1)S(1)}, u32[]{:S(2)}, u32[]{:S(2)}) collective-permute-start(bf16[4,4,8,1920]{3,2,1,0:T(8,128)(2,1)S(1)} %pad_maximum_fusion.2), channel_id=1, source_target_pairs={{0,68},{4,64},{64,0},{68,4},{1,69},{5,65},{65,1},{69,5},{2,70},{6,... | collective-permute-start | bytes 1474568 | tf_op jit(solution)/shard_map/ppermute | solution.py:528
  35.4 7.7 %collective-permute-start.9 = (bf16[2,4,8,1920]{3,2,1,0:T(8,128)(2,1)S(1)}, bf16[2,4,8,1920]{3,2,1,0:T(8,128)(2,1)S(1)}, u32[]{:S(2)}, u32[]{:S(2)}) collective-permute-start(bf16[2,4,8,1920]{3,2,1,0:T(8,128)(2,1)S(1)} %slice.44), channel_id=1, source_target_pairs={{0,64},{4,68},{64,4},{68,0},{1,65},{5,69},{65,5},{69,1},{2,66},{6,... | collective-permute-start | bytes 737288 | tf_op jit(solution)/shard_map/ppermute | solution.py:528
  37.0 6.7 %collective-permute-start.10 = (bf16[2,4,8,1920]{3,2,1,0:T(8,128)(2,1)S(1)}, bf16[2,4,8,1920]{3,2,1,0:T(8,128)(2,1)S(1)}, u32[]{:S(2)}, u32[]{:S(2)}) collective-permute-start(bf16[2,4,8,1920]{3,2,1,0:T(8,128)(2,1)S(1)} %slice.45), channel_id=1, source_target_pairs={{0,68},{4,64},{64,0},{68,4},{1,69},{5,65},{65,1},{69,5},{2,70},{6,... | collective-permute-start | bytes 737288 | tf_op jit(solution)/shard_map/ppermute | solution.py:528
  38.9 7.0 %collective-permute-start.13 = (bf16[256,384]{1,0:T(8,128)(2,1)S(1)}, bf16[256,384]{1,0:T(8,128)(2,1)S(1)}, u32[]{:S(2)}, u32[]{:S(2)}) collective-permute-start(bf16[256,384]{1,0:T(8,128)(2,1)S(1)} %pad_maximum_fusion.3.token_0.tokens_ref), channel_id=1, source_target_pairs={{0,1},{1,2},{2,3},{3,0},{4,5},{5,6},{6,7},{7,4},{8,9},{9,10},{10,1... | collective-permute-start | bytes 589832 | tf_op jit(solution)/shard_map/ppermute | solution.py:519
  39.0 9.1 %collective-permute-start.12 = (bf16[256,384]{1,0:T(8,128)(2,1)S(1)}, bf16[256,384]{1,0:T(8,128)(2,1)S(1)}, u32[]{:S(2)}, u32[]{:S(2)}) collective-permute-start(bf16[256,384]{1,0:T(8,128)(2,1)S(1)} %pad_maximum_fusion.3.token_0.tokens_ref), channel_id=1, source_target_pairs={{0,2},{1,3},{2,0},{3,1},{4,6},{5,7},{6,4},{7,5},{8,10},{9,11},{10,... | collective-permute-start | bytes 589832 | tf_op jit(solution)/shard_map/ppermute | solution.py:519
  42.3 6.5 %collective-permute-start.11 = (bf16[256,384]{1,0:T(8,128)(2,1)S(1)}, bf16[256,384]{1,0:T(8,128)(2,1)S(1)}, u32[]{:S(2)}, u32[]{:S(2)}) collective-permute-start(bf16[256,384]{1,0:T(8,128)(2,1)S(1)} %pad_maximum_fusion.3.token_0.tokens_ref), channel_id=1, source_target_pairs={{0,3},{1,0},{2,1},{3,2},{4,7},{5,4},{6,5},{7,6},{8,11},{9,8},{10,9... | collective-permute-start | bytes 589832 | tf_op jit(solution)/shard_map/ppermute | solution.py:519
  48.8 4.0 %collective-permute-start.14 = (bf16[512,1920]{1,0:T(8,128)(2,1)S(1)}, bf16[512,1920]{1,0:T(8,128)(2,1)S(1)}, u32[]{:S(2)}, u32[]{:S(2)}) collective-permute-start(bf16[512,1920]{1,0:T(8,128)(2,1)S(1)} %bitcast.34), channel_id=1, source_target_pairs={{0,8},{8,0},{1,9},{9,1},{2,10},{10,2},{3,11},{11,3},{4,12},{12,4},... | collective-permute-start | bytes 5898248 | tf_op jit(solution)/shard_map/ppermute | solution.py:519
  72.3 22.3 %collective-permute-start.19 = (bf16[512,1408]{1,0:T(8,128)(2,1)S(1)}, bf16[512,1408]{1,0:T(8,128)(2,1)S(1)}, u32[]{:S(2)}, u32[]{:S(2)}) collective-permute-start(bf16[512,1408]{1,0:T(8,128)(2,1)S(1)} %get-tuple-element.99), channel_id=1, source_target_pairs={{0,8},{8,0},{1,9},{9,1},{2,10},{10,2},{3,11},{11,3},{4,12},{12,4},... | collective-permute-start | bytes 4325384 | tf_op jit(solution)/shard_map/ppermute | solution.py:519
  79.8 14.6 %collective-permute-start.18 = (bf16[512,512]{1,0:T(8,128)(2,1)S(1)}, bf16[512,512]{1,0:T(8,128)(2,1)S(1)}, u32[]{:S(2)}, u32[]{:S(2)}) collective-permute-start(bf16[512,512]{1,0:T(8,128)(2,1)S(1)} %get-tuple-element.97), channel_id=1, source_target_pairs={{0,8},{8,0},{1,9},{9,1},{2,10},{10,2},{3,11},{11,3},{4,12},{12,4},... | collective-permute-start | bytes 1572872 | tf_op jit(solution)/shard_map/ppermute | solution.py:519
  80.3 8.4 %collective-permute-start.15 = (bf16[272,384]{1,0:T(8,128)(2,1)S(1)}, bf16[272,384]{1,0:T(8,128)(2,1)S(1)}, u32[]{:S(2)}, u32[]{:S(2)}) collective-permute-start(bf16[272,384]{1,0:T(8,128)(2,1)S(1)} %get-tuple-element.85), channel_id=1, source_target_pairs={{0,1},{1,2},{2,3},{3,0},{4,5},{5,6},{6,7},{7,4},{8,9},{9,10},{10,1... | collective-permute-start | bytes 626696 | tf_op jit(solution)/shard_map/ppermute | solution.py:519
  81.2 12.9 %collective-permute-start.16 = (bf16[272,384]{1,0:T(8,128)(2,1)S(1)}, bf16[272,384]{1,0:T(8,128)(2,1)S(1)}, u32[]{:S(2)}, u32[]{:S(2)}) collective-permute-start(bf16[272,384]{1,0:T(8,128)(2,1)S(1)} %get-tuple-element.86), channel_id=1, source_target_pairs={{0,2},{1,3},{2,0},{3,1},{4,6},{5,7},{6,4},{7,5},{8,10},{9,11},{10,... | collective-permute-start | bytes 626696 | tf_op jit(solution)/shard_map/ppermute | solution.py:519
  84.4 9.6 %collective-permute-start.17 = (bf16[272,384]{1,0:T(8,128)(2,1)S(1)}, bf16[272,384]{1,0:T(8,128)(2,1)S(1)}, u32[]{:S(2)}, u32[]{:S(2)}) collective-permute-start(bf16[272,384]{1,0:T(8,128)(2,1)S(1)} %get-tuple-element.87), channel_id=1, source_target_pairs={{0,3},{1,0},{2,1},{3,2},{4,7},{5,4},{6,5},{7,6},{8,11},{9,8},{10,9... | collective-permute-start | bytes 626696 | tf_op jit(solution)/shard_map/ppermute | solution.py:519
  96.4 42.4 %all-to-all-start = ((bf16[64,8,1920]{2,1,0:T(8,128)(2,1)}), bf16[64,8,1920]{2,1,0:T(8,128)(2,1)S(1)}, u32[]{:S(2)}, u32[]{:S(2)}) async-start(bf16[64,8,1920]{2,1,0:T(8,128)(2,1)} %bitcast.37), calls=%async_computation | async-start | bytes 3932160 | tf_op jit(solution)/shard_map/all_to_all | solution.py:668
  105.8 31.7 %collective-permute-start.20 = (bf16[272,384]{1,0:T(8,128)(2,1)S(1)}, bf16[272,384]{1,0:T(8,128)(2,1)S(1)}, u32[]{:S(2)}, u32[]{:S(2)}) collective-permute-start(bf16[272,384]{1,0:T(8,128)(2,1)S(1)} %get-tuple-element.101), channel_id=1, source_target_pairs={{0,4},{4,0},{1,5},{5,1},{2,6},{6,2},{3,7},{7,3},{8,12},{12,8},{9,1... | collective-permute-start | bytes 626696 | tf_op jit(solution)/shard_map/ppermute | solution.py:519

commit v3 on v2

--- a/solution.py
+++ b/solution.py
@@ -20,7 +20,6 @@
 X = ("xl", "xh")
 BF = jnp.bfloat16
 F32 = jnp.float32
-VMEM_LIMIT = 36 * 1024 * 1024
 
 
 def dot(left, right, dims=((1,), (0,))):
@@ -64,33 +63,39 @@
     return jnp.where((lane >= 64) == (head % 2 == 1), pair, jnp.zeros_like(pair))
 
 
-def take_columns(ids_ref):
-    row = iota((D, 1), 0)
+def unpacker(ids_ref, near_ref, far_ref, offset):
+    row = iota((96, 1), 0)
     device = (row * 43691) >> 17
     j = row - 3 * device
-    x = 2 * ((device >> 2) & 1) + (device >> 6)
+    run = (device >> 4) * 4 + (((device >> 3) & 1) ^ ids_ref[2]) * 2 + ((device >> 2) & 1)
+    z = (device & 3) ^ ids_ref[4]
+    base = run * 32 + (z ^ (z >> 1)) * 8
+    places = [
+        pick(columns, 256)
+        for columns in (
+            jnp.concatenate([base + j, base + 3 + j], axis=0),
+            jnp.concatenate([jnp.where(j < 2, base + 6 + j, -1), jnp.where(j == 2, base + 6, -1)], axis=0),
+        )
+    ]
     here = 2 * ids_ref[3] + ids_ref[0]
-    slot = ((device >> 3) + ids_ref[2]) & 1
-    slot = slot * 4 + ((x - here) & 3)
-    slot = slot * 4 + (((device >> 4) - ids_ref[1]) & 3)
-    slot = slot * 4 + ((device - ids_ref[4]) & 3)
-    return j, slot * 8
-
-
-def unpacker(ids_ref, near_ref, far_ref, offset):
-    j, base = take_columns(ids_ref)
-    half = near_ref.shape[0]
-    places = (
-        base + j,
-        base + 3 + j,
-        jnp.where(j < 2, base + 6 + j, -1),
-        jnp.where(j == 2, base + 6, -1),
-    )
-
-    def unpack(index, start, stop):
-        chosen = pick(places[index], 2 * half)
-        lanes = slice(offset + start, offset + stop)
-        return dot(chosen[:, :half], near_ref[:, lanes]) + dot(chosen[:, half:], far_ref[:, lanes])
+
+    def band(number, lanes):
+        runs = []
+        for low in range(2):
+            y = (2 * (number & 1) + low - ids_ref[1]) & 3
+            for ref in (near_ref, far_ref):
+                for upper in range(2):
+                    x = (2 * upper + (number >> 1) - here) & 3
+                    first = pl.multiple_of((x * 4 + y) * 32, 32)
+                    runs.append(ref[pl.ds(first, 32), lanes])
+        return jnp.concatenate(runs, axis=0)
+
+    def unpack(number, width, more):
+        rows = band(number, slice(offset, offset + width))
+        both = dot(places[0], rows).astype(BF)
+        ends = dot(places[1], rows[:, : 2 * more])
+        last = (ends[:96, :more] + ends[96:, more:]).astype(BF)
+        return both[:96], both[96:], last
 
     return unpack
 
@@ -135,14 +140,11 @@
     w_fc1_ref,
     w_fc2_ref,
     payload_ref,
-    own_ref,
     send_ref,
     condition_ref,
     scratch,
 ):
     upper = ids_ref[3]
-    own_ref[0] = latents_ref[upper]
-    own_ref[1] = cotangent_ref[upper]
     send_ref[0] = latents_ref[1 - upper]
     send_ref[1] = cotangent_ref[1 - upper]
     modulation = jnp.where(upper == 1, modulation_ref[1:2, :], modulation_ref[0:1, :])
@@ -201,8 +203,7 @@
     far_ref,
     token_0,
     token_1,
-    token_2,
-    token_3,
+    token_23,
     condition_ref,
     w_qkv_ref,
     hidden_ref,
@@ -216,15 +217,19 @@
     values_t,
 ):
     unpack = unpacker(ids_ref, near_ref, far_ref, 0)
-    w_qkv_ref[:, :FIRST] = unpack(0, 0, FIRST).astype(BF)
-    w_qkv_ref[:, FIRST : 2 * FIRST] = unpack(1, 0, FIRST).astype(BF)
-    last = unpack(2, 0, 256) + unpack(3, 256, 512)
-    w_qkv_ref[:, 2 * FIRST :] = last[:, :128].astype(BF)
-    biases = last[:, 128:].T[:8, :]
+    columns = []
+    for number in range(4):
+        rows = slice(number * 96, number * 96 + 96)
+        one, two, last = unpack(number, FIRST, 256)
+        w_qkv_ref[rows, :FIRST] = one
+        w_qkv_ref[rows, FIRST : 2 * FIRST] = two
+        w_qkv_ref[rows, 2 * FIRST :] = last[:, :128]
+        columns.append(last[:, 128:].astype(F32))
+    biases = jnp.concatenate(columns, axis=0).T[:8, :]
     biases_ref[...] = biases
     shift_one, scale_one = condition_ref[0:1, :], condition_ref[1:2, :]
     own = token_0.shape[0]
-    for index, token_ref in enumerate((token_0, token_1, token_2, token_3)):
+    for index, token_ref in enumerate((token_0, token_1, token_23.at[0], token_23.at[1])):
         normed, _ = normalise(token_ref[...].astype(F32))
         hidden = (normed * (1.0 + scale_one) + shift_one).astype(BF)
         rows = slice(index * own, index * own + own)
@@ -253,8 +258,8 @@
     near_ref,
     far_ref,
     tokens_ref,
-    upstream_a,
-    upstream_b,
+    swapped_ref,
+    cotangent_ref,
     condition_ref,
     output_a,
     output_b,
@@ -275,15 +280,19 @@
     third,
 ):
     unpack = unpacker(ids_ref, near_ref, far_ref, FIRST)
-    w_fc1[:, :SECOND] = unpack(0, 0, SECOND).astype(BF)
-    group = unpack(1, 0, SECOND).astype(BF)
-    w_fc1[:, SECOND:] = group[:, :128]
-    last = (unpack(2, 0, TAIL) + unpack(3, TAIL, 2 * TAIL)).astype(BF)
-    for part in range(3):
-        w_fc2[part * D : (part + 1) * D, :] = group[:, 128 + part * D : 128 + (part + 1) * D]
-    w_fc2[3 * D :, :128] = group[:, 128 + 3 * D :]
-    w_fc2[3 * D :, 128:] = last[:, :256]
-    w_out[...] = last[:, 256:]
+    for number in range(4):
+        rows = slice(number * 96, number * 96 + 96)
+        one, two, last = unpack(number, SECOND, TAIL)
+        w_fc1[rows, :SECOND] = one
+        w_fc1[rows, SECOND:] = two[:, :128]
+        for part in range(4):
+            area = slice(part * D + number * 96, part * D + number * 96 + 96)
+            if part < 3:
+                w_fc2[area, :] = two[:, 128 + part * D : 128 + (part + 1) * D]
+            else:
+                w_fc2[area, :128] = two[:, 128 + part * D :]
+                w_fc2[area, 128:] = last[:, :256]
+        w_out[rows, :] = last[:, 256:]
     b_out, b_fc2 = biases_ref[2:3, :], biases_ref[3:4, :]
     b_fc1 = jnp.concatenate([biases_ref[4 + i : 5 + i, :] for i in range(4)], axis=1)
     gate_one, shift_two, scale_two, gate_two = (condition_ref[i : i + 1, :] for i in range(2, 6))
@@ -307,7 +316,7 @@
     output_a[...] = output[:side]
     output_b[...] = output[side:]
 
-    upstream = jnp.concatenate([upstream_a[...], upstream_b[...]], axis=0).astype(F32)
+    upstream = jnp.concatenate([cotangent_ref[ids_ref[3]], swapped_ref[1]], axis=0).astype(F32)
     rows_ref[...] = jnp.zeros_like(rows_ref)
     vectors_ref[...] = jnp.zeros_like(vectors_ref)
     vectors_ref[5:6, :] = column_sum(upstream * branch_two)
@@ -344,30 +353,30 @@
 
 
 def front_kernel(
-    ids_ref, near_ref, far_ref, token_0, token_1, token_2, token_3, upstream_a, upstream_b, condition_ref,
+    ids_ref, near_ref, far_ref, token_0, token_1, token_23, swapped_ref, cotangent_ref, condition_ref,
     w_qkv_ref, hidden_ref, query_ref, keys_ref, values_ref, keys_t, probability_ref,
     output_a, output_b, middle_grad_ref, attended_grad_ref, weighted_ref, vectors_ref, rows_ref,
     keep_ref, send_ref,
     values_t, biases_ref, attended_t, w_fc1, w_fc2, w_out, slope_scr, whole, third,
 ):
     attention_part(
-        ids_ref, near_ref, far_ref, token_0, token_1, token_2, token_3, condition_ref,
+        ids_ref, near_ref, far_ref, token_0, token_1, token_23, condition_ref,
         w_qkv_ref, hidden_ref, query_ref, keys_ref, values_ref, keys_t, probability_ref,
         biases_ref, attended_t, values_t,
     )
     forward_part(
-        ids_ref, near_ref, far_ref, token_0, upstream_a, upstream_b, condition_ref,
+        ids_ref, near_ref, far_ref, token_0, swapped_ref, cotangent_ref, condition_ref,
         output_a, output_b, middle_grad_ref, attended_grad_ref, weighted_ref, vectors_ref, rows_ref,
         keep_ref, send_ref, biases_ref, attended_t, w_fc1, w_fc2, w_out, slope_scr, whole, third,
     )
 
 
 def backward_kernel(
-    token_0, token_1, token_2, token_3, condition_ref,
+    ids_ref, token_0, token_1, token_23, condition_ref,
     w_qkv_ref, query_ref, keys_ref, values_ref, keys_t, probability_ref,
-    attended_grad_ref, weighted_ref, vectors_in,
-    own_ref, piece_1, piece_2, piece_3, vectors_ref, grad_query_ref, key_grads, value_grads,
-    query_t,
+    attended_grad_ref, weighted_ref, vectors_in, hidden_ref, rows_ref,
+    piece_0, piece_1, piece_2, piece_3, keep_ref, send_ref,
+    query_t, vectors_ref, grad_query_ref, key_grads, value_grads, whole, third, tall,
 ):
     own = token_0.shape[0]
     for pair in range(HEADS // 2):
@@ -392,8 +401,8 @@
     grad_query = query_t[...].T.astype(BF)
     grad_query_ref[...] = grad_query
     shift_sum, scale_sum = None, None
-    pieces = (own_ref, piece_1, piece_2, piece_3)
-    for index, token_ref in enumerate((token_0, token_1, token_2, token_3)):
+    pieces = (piece_0, piece_1, piece_2, piece_3)
+    for index, token_ref in enumerate((token_0, token_1, token_23.at[0], token_23.at[1])):
         rows = slice(index * own, index * own + own)
         grad = dot_nt(key_grads[rows, :], w_qkv_ref[:, D : 2 * D]) + dot_nt(
             value_grads[rows, :], w_qkv_ref[:, 2 * D :]
@@ -404,20 +413,13 @@
         shifts, scales = column_sum(grad), column_sum(grad * normed)
         shift_sum = shifts if shift_sum is None else shift_sum + shifts
         scale_sum = scales if scale_sum is None else scale_sum + scales
-        pieces[index][:own, :] = grad.astype(pieces[index].dtype)
+        pieces[index][:own, :] = grad.astype(BF)
     vectors_ref[...] = vectors_in[...]
     vectors_ref[0:1, :] = shift_sum
     vectors_ref[1:2, :] = scale_sum
-    for piece in pieces[1:]:
-        piece[own:, :] = two_parts(vectors_ref[...])
-
-
-def weight_kernel(
-    ids_ref, hidden_ref, grad_query_ref, key_grads, value_grads, rows_ref,
-    keep_ref, send_ref,
-    whole, third, tall,
-):
-    own = grad_query_ref.shape[0]
+    parts = two_parts(vectors_ref[...])
+    for piece in pieces:
+        piece[own:, :] = parts
     tall[...] = jnp.zeros_like(tall)
     tall[0:8, :] = rows_ref[...]
     tall[0:1, :] = column_sum(grad_query_ref[...].astype(F32))
@@ -442,14 +444,14 @@
 
 
 def final_kernel(
-    tokens_ref, condition_ref, middle_ref, own_ref, a_ref, b_ref, c_ref, vectors_ref, output_ref,
+    tokens_ref, condition_ref, middle_ref, piece_0, piece_1, piece_2, piece_3, output_ref,
     half_ref, send_ref, sums_ref,
 ):
-    own = own_ref.shape[0]
+    own = tokens_ref.shape[0]
     side = own // 2
-    grad = own_ref[...]
-    sums = vectors_ref[...]
-    for piece in (a_ref, b_ref, c_ref):
+    grad = piece_0[:own, :].astype(F32)
+    sums = one_part(piece_0[own:, :])
+    for piece in (piece_1, piece_2, piece_3):
         grad = grad + piece[:own, :].astype(F32)
         sums = sums + one_part(piece[own:, :])
     normed, inverse = normalise(tokens_ref[...].astype(F32))
@@ -463,9 +465,10 @@
     sums_ref[...] = sums
 
 
-def join_kernel(
-    ids_ref, output_ref, grad_ref, other_ref, sums_ref,
+def last_kernel(
+    ids_ref, output_ref, grad_ref, other_ref, sums_ref, pieces_ref,
     output_out, grad_out, modulation_out,
+    qkv_ref, b_query, b_value, b_out, b_fc1, b_fc2, fc1_ref, fc2_ref, out_ref,
 ):
     upper = ids_ref[3]
     side = output_ref.shape[0]
@@ -480,9 +483,6 @@
         cut = slice(part * D, part * D + D)
         modulation_out[0:1, cut] = low[part : part + 1, :]
         modulation_out[1:2, cut] = high[part : part + 1, :]
-
-
-def sum_kernel(pieces_ref, qkv_ref, bias_ref, fc1_ref, fc2_ref, out_ref):
     total = pieces_ref[0].astype(F32)
     for index in range(1, pieces_ref.shape[0]):
         total = total + pieces_ref[index].astype(F32)
@@ -491,7 +491,15 @@
     qkv_ref[:, FIRST : 2 * FIRST] = small[3:6]
     last = jnp.concatenate([small[6:8, :256], small[6:7, 256:]], axis=0)
     qkv_ref[:, 2 * FIRST :] = last[:, :128]
-    bias_ref[...] = last[:, 128:]
+    columns = jnp.concatenate([last[:, 128:], jnp.zeros((5, 128), F32)], axis=0).T
+    for column, ref in enumerate((b_query, b_value, b_out, b_fc2)):
+        ref[...] = columns[column : column + 1, :3]
+    lane = iota((1, 12), 1)
+    wide = jnp.zeros((1, 12), F32)
+    for j in range(3):
+        for part in range(4):
+            wide = jnp.where(lane == 4 * j + part, columns[4 + part : 5 + part, j : j + 1], wide)
+    b_fc1[...] = wide
     swap = interleave()
     one, two = total[0:3], total[3:6]
     last = jnp.concatenate([total[6:8, :TAIL], total[6:7, TAIL : 2 * TAIL]], axis=0)
@@ -528,8 +536,8 @@
     return lax.ppermute(array, X, moves)
 
 
-def ring(array, axis):
-    return [array] + [shift(array, axis, -k, 4) for k in range(1, 4)]
+def trade(array, bits):
+    return lax.ppermute(array, "z", [(i, i ^ bits) for i in range(4)])
 
 
 def sds(*shape, dtype=BF):
@@ -540,17 +548,18 @@
     return pltpu.VMEM(shape, dtype)
 
 
-def hold(array):
-    return pltpu.with_memory_space_constraint(array, pltpu.VMEM)
-
-
-def far(array):
-    return pltpu.with_memory_space_constraint(array, pltpu.HBM)
-
-
-def call(kernel, out_shape, scratch, ids, *operands):
+def hold(*arrays):
+    return [pltpu.with_memory_space_constraint(array, pltpu.VMEM) for array in arrays]
+
+
+def call(kernel, out_shape, scratch, ids, *operands, limit=16):
     specs = [] if ids is None else [pl.BlockSpec(memory_space=pltpu.SMEM)]
-    given = operands if ids is None else (ids, *operands)
+    given = [] if ids is None else [ids]
+    for operand in operands:
+        if isinstance(operand, list):
+            given += operand
+        else:
+            given.append(pltpu.with_memory_space_constraint(operand, pltpu.HBM))
     specs += [pl.BlockSpec(memory_space=pltpu.VMEM)] * (len(given) - len(specs))
     return pl.pallas_call(
         kernel,
@@ -558,7 +567,7 @@
         in_specs=specs,
         out_specs=tuple(pl.BlockSpec(memory_space=pltpu.VMEM) for _ in out_shape),
         scratch_shapes=scratch,
-        compiler_params=pltpu.CompilerParams(vmem_limit_bytes=VMEM_LIMIT),
+        compiler_params=pltpu.CompilerParams(vmem_limit_bytes=limit * 1024 * 1024),
     )(*given)
 
 
@@ -571,24 +580,27 @@
         jnp.pad(b.astype(F32)[None], ((0, 0), (first, 128 - first - b.shape[0])))
         for b, first in ((b_query, 0), (b_value, 3), (b_out, 6), (b_fc2, 9), (b_fc1, 12))
     )
-    payload, own_pair, send_pair, condition = call(
+    upper = lax.axis_index("xh") == 1
+    payload, send_pair, condition = call(
         pack_kernel,
-        (sds(8, FIRST + SECOND), sds(2, side, D), sds(2, side, D), sds(8, D, dtype=F32)),
+        (sds(8, FIRST + SECOND), sds(2, side, D), pltpu.HBM((8, D), F32)),
         [vmem(8, 3 * D + 128 + 2 * FF + D, dtype=F32)],
-        ids, biases, *(far(a) for a in (latents, cotangent, modulation, w_qkv, w_out, w_fc1, w_fc2)),
-    )
-
+        ids, biases, latents, cotangent, modulation, w_qkv, w_out, w_fc1, w_fc2,
+    )
     swapped = shift(send_pair, "xh", 1, 2)
-    column = jnp.stack(ring(payload, "z"))
-    plane = jnp.stack(ring(column, "y"))
-    plane, swapped = lax.optimization_barrier((plane, swapped))
-    tokens = jnp.concatenate([own_pair[0], swapped[0]])
-    all_tokens = ring(tokens, "z")
+    column = jnp.stack([payload, trade(payload, 1)])
+    column = jnp.stack([column, trade(column, 3)]).reshape(4, 8, FIRST + SECOND)
+    column, swapped = lax.optimization_barrier((column, swapped))
+    tokens = jnp.concatenate([jnp.where(upper, latents[1], latents[0]), swapped[0]])
+    near_tokens = trade(tokens, 1)
+    plane = jnp.stack([column] + [shift(column, "y", -k, 4) for k in range(1, 4)])
+    far_tokens = trade(jnp.stack([tokens, near_tokens]), 3)
     before, after = shift_x(plane, 1), shift_x(plane, -1)
+    before, after, far_tokens = lax.optimization_barrier((before, after, far_tokens))
+    all_tokens = (tokens, near_tokens, far_tokens)
     half = plane.shape[0] // 2
     opposite = jnp.concatenate([shift_x(before[:half], 1), shift_x(after[half:], -1)])
     near = jnp.stack([plane, after, opposite, before]).reshape(-1, FIRST + SECOND)
-    near, all_tokens = lax.optimization_barrier((near, all_tokens))
     other = shift(near, "core", 1, 2)
 
     (
@@ -604,9 +616,9 @@
             vmem(length, D),
             vmem(D, length),
             vmem(HEADS, length, own),
-            sds(side, D),
-            sds(side, D),
-            vmem(own, D, dtype=F32),
+            pltpu.HBM((side, D), BF),
+            pltpu.HBM((side, D), BF),
+            pltpu.HBM((own, D), F32),
             vmem(own, D),
             vmem(8, own, dtype=F32),
             vmem(8, D, dtype=F32),
@@ -625,79 +637,79 @@
             vmem(D, 2 * SECOND),
             vmem(D, TAIL),
         ],
-        ids, hold(near), hold(other), *(hold(t) for t in all_tokens), own_pair[1], swapped[1], condition,
+        ids, hold(near, other, *all_tokens, swapped), cotangent, condition,
+        limit=32,
     )
     other_two = shift(send_two, "core", 1, 2)
 
-    hidden_own, piece_1, piece_2, piece_3, vectors, grad_query, key_grads, value_grads = call(
+    piece_0, piece_1, piece_2, piece_3, keep_one, send_one = call(
         backward_kernel,
-        (
-            vmem(own, D, dtype=F32),
-            vmem(own + 16, D),
-            vmem(own + 16, D),
-            vmem(own + 16, D),
+        tuple(vmem(own + 16, D) for _ in range(4)) + (vmem(512, FIRST), vmem(512, FIRST)),
+        [
+            vmem(D, own, dtype=F32),
             vmem(8, D, dtype=F32),
             vmem(own, D),
             vmem(length, D),
             vmem(length, D),
+            vmem(D, 2 * FIRST),
+            vmem(D, 256),
+            vmem(128, D, dtype=F32),
+        ],
+        ids, hold(*all_tokens), condition,
+        hold(
+            w_all, query, keys, values, keys_t, probability, attended_grad, weighted, vectors,
+            hidden, bias_sums,
         ),
-        [vmem(D, own, dtype=F32)],
-        None, *(hold(t) for t in all_tokens), condition,
-        *(
-            hold(a)
-            for a in (w_all, query, keys, values, keys_t, probability, attended_grad, weighted, vectors)
-        ),
-    )
-    arrived = [shift(p, "z", k, 4) for k, p in ((1, piece_1), (2, piece_2), (3, piece_3))]
-    keep_one, send_one = call(
-        weight_kernel,
-        (vmem(512, FIRST), vmem(512, FIRST)),
-        [vmem(D, 2 * FIRST), vmem(D, 256), vmem(128, D, dtype=F32)],
-        ids, *(hold(a) for a in (hidden, grad_query, key_grads, value_grads, bias_sums)),
-    )
+        limit=24,
+    )
+    arrived = (piece_0, trade(piece_1, 1), trade(piece_2, 3), trade(piece_3, 2))
     other_one = shift(send_one, "core", 1, 2)
     mixed = jnp.concatenate([keep_one + other_one, keep_two + other_two], axis=1)
+    mixed, arrived = lax.optimization_barrier((mixed, arrived))
     grad_a, grad_b, sums = call(
         final_kernel,
-        (sds(side, D), vmem(2 * side + 16, D), vmem(8, D, dtype=F32)),
+        (pltpu.HBM((side, D), BF), vmem(2 * side + 16, D), vmem(8, D, dtype=F32)),
         [],
-        None, hold(tokens), condition, hold(middle_grad), hold(hidden_own),
-        *(hold(a) for a in arrived), hold(vectors), output_b,
+        None, hold(tokens), condition, middle_grad, hold(*arrived), output_b,
     )
     mixed, grad_b = lax.optimization_barrier((mixed, grad_b))
     pieces = lax.all_to_all(mixed.reshape(64, 8, FIRST + SECOND), CHIPS, 0, 0, tiled=True)
     grad_back = shift(grad_b, "xh", 1, 2)
-    output, input_grad, modulation_grad = call(
-        join_kernel,
-        (sds(2, side, D), sds(2, side, D), sds(2, 6 * D, dtype=F32)),
-        [],
-        ids, output_a, grad_a, hold(grad_back), hold(sums),
-    )
-    grad_qkv, grad_bias, grad_fc1, grad_fc2, grad_out = call(
-        sum_kernel,
+    (
+        output, input_grad, modulation_grad,
+        grad_qkv, grad_b_query, grad_b_value, grad_b_out, grad_b_fc1, grad_b_fc2, grad_fc1, grad_fc2, grad_out,
+    ) = call(
+        last_kernel,
         (
+            sds(2, side, D),
+            sds(2, side, D),
+            sds(2, 6 * D, dtype=F32),
             sds(3, 3 * D, dtype=F32),
-            sds(3, 128, dtype=F32),
+            sds(1, 3, dtype=F32),
+            sds(1, 3, dtype=F32),
+            sds(1, 3, dtype=F32),
+            sds(1, 12, dtype=F32),
+            sds(1, 3, dtype=F32),
             sds(3, FF, dtype=F32),
             sds(12, D, dtype=F32),
             sds(3, D, dtype=F32),
         ),
         [],
-        None, hold(pieces),
+        ids, output_a, grad_a, hold(grad_back, sums, pieces),
     )
     return (
         output,
         input_grad,
         modulation_grad,
         grad_qkv,
-        grad_bias[:, 0],
-        grad_bias[:, 1],
+        grad_b_query.reshape(3),
+        grad_b_value.reshape(3),
         grad_out,
-        grad_bias[:, 2],
+        grad_b_out.reshape(3),
         grad_fc1,
-        grad_bias[:, 4:8].reshape(12),
+        grad_b_fc1.reshape(12),
         grad_fc2,
-        grad_bias[:, 3],
+        grad_b_fc2.reshape(3),
     )
 
 

time: 143 us -> 130 us (0.909)
  waiting for transfers between devices: 62.6 us -> 52.4 us
  Pallas kernels: 32 us -> 30.2 us
  other arithmetic: 3.19 us -> 4.75 us
  local copies, waits for them, and re-layouts: 1.56 us -> 0.13 us
    ppermute x17 -> x8, waiting for transfers between devices: 53.9 us -> 33 us  [shift(): lax.ppermute(array, axis, [(i, (i + step) % size) for i in range(size)])]
    ppermute x0 -> x7, waiting for transfers between devices: none -> 15.2 us  [trade(): return lax.ppermute(array, 'z', [(i, i ^ bits) for i in range(4)])]
    ppermute x17 -> x8, starting transfers between devices: 26.1 us -> 12 us  [shift(): lax.ppermute(array, axis, [(i, (i + step) % size) for i in range(size)])]
    ppermute x0 -> x7, starting transfers between devices: none -> 12.9 us  [trade(): return lax.ppermute(array, 'z', [(i, i ^ bits) for i in range(4)])]
    ppermute x4, waiting for transfers between devices: 8.65 us -> 4.18 us  [shift_x(): return lax.ppermute(array, X, moves)]
    pallas_call x7 -> x5, Pallas kernels: 32 us -> 30.2 us  [call(): pl.pallas_call(kernel, out_shape=out_shape, in_specs=specs, out_specs=tup...]
  transfers between devices with their start and end apart: 22 -> 20, of which waited for: 14 -> 11; matrix products, arithmetic and copies ran while one was open for 0% -> 2% of each run, Pallas kernels for 6% -> 6%
where the time goes in v3:
time: 130 us; the launch traced here: 129 us
  waiting for transfers between devices  52.4 us (40%)
  starting transfers between devices  41 us (32%)
  Pallas kernels  30.2 us (23%)
  other arithmetic  4.75 us (4%)
    ppermute x8, waiting for transfers between devices, shift(): lax.ppermute(array, axis, [(i, (i + step) % size) for i in range(size)])  33 us
    pallas_call x5, Pallas kernels, call(): pl.pallas_call(kernel, out_shape=out_shape, in_specs=specs, out_specs=tup...  30.2 us
    ppermute x7, waiting for transfers between devices, trade(): return lax.ppermute(array, 'z', [(i, i ^ bits) for i in range(4)])  15.2 us
    ppermute x7, starting transfers between devices, trade(): return lax.ppermute(array, 'z', [(i, i ^ bits) for i in range(4)])  12.9 us
    ppermute x8, starting transfers between devices, shift(): lax.ppermute(array, axis, [(i, (i + step) % size) for i in range(size)])  12 us
    all_to_all x1, starting transfers between devices, body(): lax.all_to_all(mixed.reshape(64, 8, FIRST + SECOND), CHIPS, 0, 0, tiled=T...  9.47 us
    ppermute x4, starting transfers between devices, shift_x(): return lax.ppermute(array, X, moves)  6.61 us
    ppermute x4, waiting for transfers between devices, shift_x(): return lax.ppermute(array, X, moves)  4.18 us
  transfers between devices with their start and end apart: 20, of which 11 were waited for; matrix products, arithmetic and copies ran while one was open for 2% of the time, Pallas kernels for 6%

profile of v3, /device:TPU:8, one launch (start us, length us, event | category | flops | bytes accessed | tf_op | source)
XLA Modules:
  0.0 129.4 jit_solution(15072413114170448533)
XLA Ops:
  2.0 2.0 %shard_map.211 = (bf16[8,1920]{1,0:T(8,128)(2,1)S(1)}, bf16[2,128,384]{2,1,0:T(8,128)(2,1)S(1)}, f32[8,384]{1,0:T(8,128)}) custom-call(s32[5]{0:T(128)S(1)} %stack.80.ids_ref, f32[1,128]{1,0:T(1,128)} %convert_add_fusion.biases_ref, bf16[2,128,384]{2,1,0:T(8,128)(2,1)} %latents_ref.1, bf16[2,128,384]{2,1,0:T(8,128)(2,1)} %cotangent_ref.3, ...), custom_call_target="tpu_custom_call" | custom-call | tf_op jit(solution)/shard_map/pallas_call | solution.py:564
  4.1 1.9 %collective-permute-start = (bf16[8,1920]{1,0:T(8,128)(2,1)S(1)}, bf16[8,1920]{1,0:T(8,128)(2,1)S(1)}, u32[]{:S(2)}, u32[]{:S(2)}) collective-permute-start(bf16[8,1920]{1,0:T(8,128)(2,1)S(1)} %get-tuple-element.64), channel_id=1, source_target_pairs={{0,1},{1,0},{2,3},{3,2},{4,5},{5,4},{6,7},{7,6},{8,9},{9,8},{10,11... | collective-permute-start | bytes 92168 | tf_op jit(solution)/shard_map/ppermute | solution.py:540
  6.0 3.0 %collective-permute-start.2 = (bf16[2,128,384]{2,1,0:T(8,128)(2,1)S(1)}, bf16[2,128,384]{2,1,0:T(8,128)(2,1)S(1)}, u32[]{:S(2)}, u32[]{:S(2)}) collective-permute-start(bf16[2,128,384]{2,1,0:T(8,128)(2,1)S(1)} %get-tuple-element.65), channel_id=1, source_target_pairs={{0,4},{4,0},{1,5},{5,1},{2,6},{6,2},{3,7},{7,3},{8,12},{12,8},{9,1... | collective-permute-start | bytes 589832 | tf_op jit(solution)/shard_map/ppermute | solution.py:527
  9.0 3.1 %collective-permute-start.1 = (bf16[2,8,1920]{2,1,0:T(8,128)(2,1)S(1)}, bf16[2,8,1920]{2,1,0:T(8,128)(2,1)S(1)}, u32[]{:S(2)}, u32[]{:S(2)}) collective-permute-start(bf16[2,8,1920]{2,1,0:T(8,128)(2,1)S(1)} %get-tuple-element.121), channel_id=1, source_target_pairs={{0,3},{1,2},{2,1},{3,0},{4,7},{5,6},{6,5},{7,4},{8,11},{9,10},{10,... | collective-permute-start | bytes 184328 | tf_op jit(solution)/shard_map/ppermute | solution.py:540
  14.6 1.6 %collective-permute-start.5 = (bf16[4,8,1920]{2,1,0:T(8,128)(2,1)S(1)}, bf16[4,8,1920]{2,1,0:T(8,128)(2,1)S(1)}, u32[]{:S(2)}, u32[]{:S(2)}) collective-permute-start(bf16[4,8,1920]{2,1,0:T(8,128)(2,1)S(1)} %bitcast.47), channel_id=1, source_target_pairs={{0,16},{16,32},{32,48},{48,0},{1,17},{17,33},{33,49},{49,1},{2,18}... | collective-permute-start | bytes 368648 | tf_op jit(solution)/shard_map/ppermute | solution.py:527
  17.2 2.4 %collective-permute-start.3 = (bf16[4,8,1920]{2,1,0:T(8,128)(2,1)S(1)}, bf16[4,8,1920]{2,1,0:T(8,128)(2,1)S(1)}, u32[]{:S(2)}, u32[]{:S(2)}) collective-permute-start(bf16[4,8,1920]{2,1,0:T(8,128)(2,1)S(1)} %bitcast.49), channel_id=1, source_target_pairs={{0,48},{16,0},{32,16},{48,32},{1,49},{17,1},{33,17},{49,33},{2,50}... | collective-permute-start | bytes 368648 | tf_op jit(solution)/shard_map/ppermute | solution.py:527
  20.8 1.9 %collective-permute-done.4 = bf16[4,8,1920]{2,1,0:T(8,128)(2,1)S(1)} collective-permute-done((bf16[4,8,1920]{2,1,0:T(8,128)(2,1)S(1)}, bf16[4,8,1920]{2,1,0:T(8,128)(2,1)S(1)}, u32[]{:S(2)}, u32[]{:S(2)}) %collective-permute-start.4) | collective-permute-done | bytes 122912 | tf_op jit(solution)/shard_map/ppermute | solution.py:527
  24.8 2.0 %collective-permute-start.7 = (bf16[4,4,8,1920]{3,2,1,0:T(8,128)(2,1)S(1)}, bf16[4,4,8,1920]{3,2,1,0:T(8,128)(2,1)S(1)}, u32[]{:S(2)}, u32[]{:S(2)}) collective-permute-start(bf16[4,4,8,1920]{3,2,1,0:T(8,128)(2,1)S(1)} %get-tuple-element.117), channel_id=1, source_target_pairs={{0,68},{4,64},{64,0},{68,4},{1,69},{5,65},{65,1},{69,5},{2,70},{6,... | collective-permute-start | bytes 1474568 | tf_op jit(solution)/shard_map/ppermute | solution.py:536
  26.8 3.1 %collective-permute-start.9 = (bf16[2,256,384]{2,1,0:T(8,128)(2,1)S(1)}, bf16[2,256,384]{2,1,0:T(8,128)(2,1)S(1)}, u32[]{:S(2)}, u32[]{:S(2)}) collective-permute-start(bf16[2,256,384]{2,1,0:T(8,128)(2,1)S(1)} %pad_maximum_fusion.3), channel_id=1, source_target_pairs={{0,3},{1,2},{2,1},{3,0},{4,7},{5,6},{6,5},{7,4},{8,11},{9,10},{10,... | collective-permute-start | bytes 1179656 | tf_op jit(solution)/shard_map/ppermute | solution.py:540
  29.9 6.0 %collective-permute-done.9.token_23 = bf16[2,256,384]{2,1,0:T(8,128)(2,1)S(1)} collective-permute-done((bf16[2,256,384]{2,1,0:T(8,128)(2,1)S(1)}, bf16[2,256,384]{2,1,0:T(8,128)(2,1)S(1)}, u32[]{:S(2)}, u32[]{:S(2)}) %collective-permute-start.9) | collective-permute-done | bytes 393248 | tf_op jit(solution)/shard_map/ppermute | solution.py:540
  36.0 3.2 %collective-permute-start.11 = (bf16[2,4,8,1920]{3,2,1,0:T(8,128)(2,1)S(1)}, bf16[2,4,8,1920]{3,2,1,0:T(8,128)(2,1)S(1)}, u32[]{:S(2)}, u32[]{:S(2)}) collective-permute-start(bf16[2,4,8,1920]{3,2,1,0:T(8,128)(2,1)S(1)} %slice.19), channel_id=1, source_target_pairs={{0,68},{4,64},{64,0},{68,4},{1,69},{5,65},{65,1},{69,5},{2,70},{6,... | collective-permute-start | bytes 737288 | tf_op jit(solution)/shard_map/ppermute | solution.py:536
  39.2 4.2 %collective-permute-done.10 = bf16[2,4,8,1920]{3,2,1,0:T(8,128)(2,1)S(1)} collective-permute-done((bf16[2,4,8,1920]{3,2,1,0:T(8,128)(2,1)S(1)}, bf16[2,4,8,1920]{3,2,1,0:T(8,128)(2,1)S(1)}, u32[]{:S(2)}, u32[]{:S(2)}) %collective-permute-start.10) | collective-permute-done | bytes 245792 | tf_op jit(solution)/shard_map/ppermute | solution.py:536
  44.0 4.0 %collective-permute-done.12.far_ref = bf16[512,1920]{1,0:T(8,128)(2,1)S(1)} collective-permute-done((bf16[512,1920]{1,0:T(8,128)(2,1)S(1)}, bf16[512,1920]{1,0:T(8,128)(2,1)S(1)}, u32[]{:S(2)}, u32[]{:S(2)}) %collective-permute-start.12) | collective-permute-done | bytes 1966112 | tf_op jit(solution)/shard_map/ppermute | solution.py:527
  48.0 15.7 %shard_map.212 = (bf16[384,1152]{1,0:T(8,128)(2,1)S(1)}, bf16[1024,384]{1,0:T(8,128)(2,1)S(1)}, bf16[256,384]{1,0:T(8,128)(2,1)S(1)}, bf16[1024,384]{1,0:T(8,128...) custom-call(s32[5]{0:T(128)S(1)} %stack.80.ids_ref, ...), custom_call_target="tpu_custom_call" | custom-call | tf_op jit(solution)/shard_map/pallas_call | solution.py:564
  64.0 7.4 %shard_map.213 = (bf16[272,384]{1,0:T(8,128)(2,1)S(1)}, bf16[272,384]{1,0:T(8,128)(2,1)S(1)}, bf16[272,384]{1,0:T(8,128)(2,1)S(1)}, bf16[272,384]{1,0:T(8,128)(2...) custom-call(s32[5]{0:T(128)S(1)} %stack.80.ids_ref, ...), custom_call_target="tpu_custom_call" | custom-call | tf_op jit(solution)/shard_map/pallas_call | solution.py:564
  71.8 3.1 %collective-permute-start.16 = (bf16[272,384]{1,0:T(8,128)(2,1)S(1)}, bf16[272,384]{1,0:T(8,128)(2,1)S(1)}, u32[]{:S(2)}, u32[]{:S(2)}) collective-permute-start(bf16[272,384]{1,0:T(8,128)(2,1)S(1)} %get-tuple-element.91), channel_id=1, source_target_pairs={{0,3},{1,2},{2,1},{3,0},{4,7},{5,6},{6,5},{7,4},{8,11},{9,10},{10,... | collective-permute-start | bytes 626696 | tf_op jit(solution)/shard_map/ppermute | solution.py:540
  78.2 1.6 %collective-permute-done.15.piece_1 = bf16[272,384]{1,0:T(8,128)(2,1)S(1)} collective-permute-done((bf16[272,384]{1,0:T(8,128)(2,1)S(1)}, bf16[272,384]{1,0:T(8,128)(2,1)S(1)}, u32[]{:S(2)}, u32[]{:S(2)}) %collective-permute-start.15) | collective-permute-done | bytes 208928 | tf_op jit(solution)/shard_map/ppermute | solution.py:540
  79.8 4.2 %collective-permute-done.16.piece_2 = bf16[272,384]{1,0:T(8,128)(2,1)S(1)} collective-permute-done((bf16[272,384]{1,0:T(8,128)(2,1)S(1)}, bf16[272,384]{1,0:T(8,128)(2,1)S(1)}, u32[]{:S(2)}, u32[]{:S(2)}) %collective-permute-start.16) | collective-permute-done | bytes 208928 | tf_op jit(solution)/shard_map/ppermute | solution.py:540
  84.0 1.9 %collective-permute-done.17.piece_3 = bf16[272,384]{1,0:T(8,128)(2,1)S(1)} collective-permute-done((bf16[272,384]{1,0:T(8,128)(2,1)S(1)}, bf16[272,384]{1,0:T(8,128)(2,1)S(1)}, u32[]{:S(2)}, u32[]{:S(2)}) %collective-permute-start.17) | collective-permute-done | bytes 208928 | tf_op jit(solution)/shard_map/ppermute | solution.py:540
  85.9 2.0 %shard_map.214 = (bf16[128,384]{1,0:T(8,128)(2,1)}, bf16[272,384]{1,0:T(8,128)(2,1)S(1)}, f32[8,384]{1,0:T(8,128)S(1)}) custom-call(bf16[256,384]{1,0:T(8,128)(2,1)S(1)} %get-tuple-element.119.token_0.tokens_ref, f32[8,384]{1,0:T(8,128)} %get-tuple-element.71.condition_ref, f32[256,384]{1,0:T(8,128)} %get-tuple-element.73.middle_ref, ...), custom_call_target="tpu_custom_call" | custom-call | tf_op jit(solution)/shard_map/pallas_call | solution.py:564
  87.9 9.5 %all-to-all-start = ((bf16[64,8,1920]{2,1,0:T(8,128)(2,1)}), bf16[64,8,1920]{2,1,0:T(8,128)(2,1)S(1)}, u32[]{:S(2)}, u32[]{:S(2)}) async-start(bf16[64,8,1920]{2,1,0:T(8,128)(2,1)} %bitcast.44), calls=%async_computation | async-start | bytes 3932160 | tf_op jit(solution)/shard_map/all_to_all | solution.py:676
  97.4 3.0 %collective-permute-start.18 = (bf16[272,384]{1,0:T(8,128)(2,1)S(1)}, bf16[272,384]{1,0:T(8,128)(2,1)S(1)}, u32[]{:S(2)}, u32[]{:S(2)}) collective-permute-start(bf16[272,384]{1,0:T(8,128)(2,1)S(1)} %get-tuple-element.101), channel_id=1, source_target_pairs={{0,4},{4,0},{1,5},{5,1},{2,6},{6,2},{3,7},{7,3},{8,12},{12,8},{9,1... | collective-permute-start | bytes 626696 | tf_op jit(solution)/shard_map/ppermute | solution.py:527
  100.4 25.7 %collective-permute-done.18.other_ref = bf16[272,384]{1,0:T(8,128)(2,1)S(1)} collective-permute-done((bf16[272,384]{1,0:T(8,128)(2,1)S(1)}, bf16[272,384]{1,0:T(8,128)(2,1)S(1)}, u32[]{:S(2)}, u32[]{:S(2)}) %collective-permute-start.18) | collective-permute-done | bytes 208928 | tf_op jit(solution)/shard_map/ppermute | solution.py:527
  126.1 3.1 %shard_map.215 = (bf16[2,128,384]{2,1,0:T(8,128)(2,1)}, bf16[2,128,384]{2,1,0:T(8,128)(2,1)}, f32[2,2304]{1,0:T(2,128)}, f32[3,1152]{1,0:T(4,128)}, f32[1,3]{1,0...) custom-call(s32[5]{0:T(128)S(1)} %stack.80.ids_ref, ...), custom_call_target="tpu_custom_call" | custom-call | tf_op jit(solution)/shard_map/pallas_call | solution.py:564
  (37 shorter events, 12.8 us)
Async XLA Ops:
  4.1 4.9 %collective-permute-start = (bf16[8,1920]{1,0:T(8,128)(2,1)S(1)}, bf16[8,1920]{1,0:T(8,128)(2,1)S(1)}, u32[]{:S(2)}, u32[]{:S(2)}) collective-permute-start(bf16[8,1920]{1,0:T(8,128)(2,1)S(1)} %get-tuple-element.64), channel_id=1, source_target_pairs={{0,1},{1,0},{2,3},{3,2},{4,5},{5,4},{6,7},{7,6},{8,9},{9,8},{10,11... | collective-permute-start | bytes 92168 | tf_op jit(solution)/shard_map/ppermute | solution.py:540
  6.0 8.6 %collective-permute-start.2 = (bf16[2,128,384]{2,1,0:T(8,128)(2,1)S(1)}, bf16[2,128,384]{2,1,0:T(8,128)(2,1)S(1)}, u32[]{:S(2)}, u32[]{:S(2)}) collective-permute-start(bf16[2,128,384]{2,1,0:T(8,128)(2,1)S(1)} %get-tuple-element.65), channel_id=1, source_target_pairs={{0,4},{4,0},{1,5},{5,1},{2,6},{6,2},{3,7},{7,3},{8,12},{12,8},{9,1... | collective-permute-start | bytes 589832 | tf_op jit(solution)/shard_map/ppermute | solution.py:527
  9.0 5.5 %collective-permute-start.1 = (bf16[2,8,1920]{2,1,0:T(8,128)(2,1)S(1)}, bf16[2,8,1920]{2,1,0:T(8,128)(2,1)S(1)}, u32[]{:S(2)}, u32[]{:S(2)}) collective-permute-start(bf16[2,8,1920]{2,1,0:T(8,128)(2,1)S(1)} %get-tuple-element.121), channel_id=1, source_target_pairs={{0,3},{1,2},{2,1},{3,0},{4,7},{5,6},{6,5},{7,4},{8,11},{9,10},{10,... | collective-permute-start | bytes 184328 | tf_op jit(solution)/shard_map/ppermute | solution.py:540
  14.6 6.2 %collective-permute-start.5 = (bf16[4,8,1920]{2,1,0:T(8,128)(2,1)S(1)}, bf16[4,8,1920]{2,1,0:T(8,128)(2,1)S(1)}, u32[]{:S(2)}, u32[]{:S(2)}) collective-permute-start(bf16[4,8,1920]{2,1,0:T(8,128)(2,1)S(1)} %bitcast.47), channel_id=1, source_target_pairs={{0,16},{16,32},{32,48},{48,0},{1,17},{17,33},{33,49},{49,1},{2,18}... | collective-permute-start | bytes 368648 | tf_op jit(solution)/shard_map/ppermute | solution.py:527
  16.2 6.5 %collective-permute-start.4 = (bf16[4,8,1920]{2,1,0:T(8,128)(2,1)S(1)}, bf16[4,8,1920]{2,1,0:T(8,128)(2,1)S(1)}, u32[]{:S(2)}, u32[]{:S(2)}) collective-permute-start(bf16[4,8,1920]{2,1,0:T(8,128)(2,1)S(1)} %bitcast.48), channel_id=1, source_target_pairs={{0,32},{16,48},{32,0},{48,16},{1,33},{17,49},{33,1},{49,17},{2,34}... | collective-permute-start | bytes 368648 | tf_op jit(solution)/shard_map/ppermute | solution.py:527
  17.2 6.2 %collective-permute-start.3 = (bf16[4,8,1920]{2,1,0:T(8,128)(2,1)S(1)}, bf16[4,8,1920]{2,1,0:T(8,128)(2,1)S(1)}, u32[]{:S(2)}, u32[]{:S(2)}) collective-permute-start(bf16[4,8,1920]{2,1,0:T(8,128)(2,1)S(1)} %bitcast.49), channel_id=1, source_target_pairs={{0,48},{16,0},{32,16},{48,32},{1,49},{17,1},{33,17},{49,33},{2,50}... | collective-permute-start | bytes 368648 | tf_op jit(solution)/shard_map/ppermute | solution.py:527
  19.6 7.1 %collective-permute-start.8 = (bf16[256,384]{1,0:T(8,128)(2,1)S(1)}, bf16[256,384]{1,0:T(8,128)(2,1)S(1)}, u32[]{:S(2)}, u32[]{:S(2)}) collective-permute-start(bf16[256,384]{1,0:T(8,128)(2,1)S(1)} %get-tuple-element.119.token_0.tokens_ref), channel_id=1, source_target_pairs={{0,1},{1,0},{2,3},{3,2},{4,5},{5,4},{6,7},{7,6},{8,9},{9,8},{10,11... | collective-permute-start | bytes 589832 | tf_op jit(solution)/shard_map/ppermute | solution.py:540
  23.4 12.4 %collective-permute-start.6 = (bf16[4,4,8,1920]{3,2,1,0:T(8,128)(2,1)S(1)}, bf16[4,4,8,1920]{3,2,1,0:T(8,128)(2,1)S(1)}, u32[]{:S(2)}, u32[]{:S(2)}) collective-permute-start(bf16[4,4,8,1920]{3,2,1,0:T(8,128)(2,1)S(1)} %get-tuple-element.117), channel_id=1, source_target_pairs={{0,64},{4,68},{64,4},{68,0},{1,65},{5,69},{65,5},{69,1},{2,66},{6,... | collective-permute-start | bytes 1474568 | tf_op jit(solution)/shard_map/ppermute | solution.py:536
  24.8 11.1 %collective-permute-start.7 = (bf16[4,4,8,1920]{3,2,1,0:T(8,128)(2,1)S(1)}, bf16[4,4,8,1920]{3,2,1,0:T(8,128)(2,1)S(1)}, u32[]{:S(2)}, u32[]{:S(2)}) collective-permute-start(bf16[4,4,8,1920]{3,2,1,0:T(8,128)(2,1)S(1)} %get-tuple-element.117), channel_id=1, source_target_pairs={{0,68},{4,64},{64,0},{68,4},{1,69},{5,65},{65,1},{69,5},{2,70},{6,... | collective-permute-start | bytes 1474568 | tf_op jit(solution)/shard_map/ppermute | solution.py:536
  26.8 9.1 %collective-permute-start.9 = (bf16[2,256,384]{2,1,0:T(8,128)(2,1)S(1)}, bf16[2,256,384]{2,1,0:T(8,128)(2,1)S(1)}, u32[]{:S(2)}, u32[]{:S(2)}) collective-permute-start(bf16[2,256,384]{2,1,0:T(8,128)(2,1)S(1)} %pad_maximum_fusion.3), channel_id=1, source_target_pairs={{0,3},{1,2},{2,1},{3,0},{4,7},{5,6},{6,5},{7,4},{8,11},{9,10},{10,... | collective-permute-start | bytes 1179656 | tf_op jit(solution)/shard_map/ppermute | solution.py:540
  35.9 7.5 %collective-permute-start.10 = (bf16[2,4,8,1920]{3,2,1,0:T(8,128)(2,1)S(1)}, bf16[2,4,8,1920]{3,2,1,0:T(8,128)(2,1)S(1)}, u32[]{:S(2)}, u32[]{:S(2)}) collective-permute-start(bf16[2,4,8,1920]{3,2,1,0:T(8,128)(2,1)S(1)} %slice.18), channel_id=1, source_target_pairs={{0,64},{4,68},{64,4},{68,0},{1,65},{5,69},{65,5},{69,1},{2,66},{6,... | collective-permute-start | bytes 737288 | tf_op jit(solution)/shard_map/ppermute | solution.py:536
  36.0 7.4 %collective-permute-start.11 = (bf16[2,4,8,1920]{3,2,1,0:T(8,128)(2,1)S(1)}, bf16[2,4,8,1920]{3,2,1,0:T(8,128)(2,1)S(1)}, u32[]{:S(2)}, u32[]{:S(2)}) collective-permute-start(bf16[2,4,8,1920]{3,2,1,0:T(8,128)(2,1)S(1)} %slice.19), channel_id=1, source_target_pairs={{0,68},{4,64},{64,0},{68,4},{1,69},{5,65},{65,1},{69,5},{2,70},{6,... | collective-permute-start | bytes 737288 | tf_op jit(solution)/shard_map/ppermute | solution.py:536
  43.8 4.2 %collective-permute-start.12 = (bf16[512,1920]{1,0:T(8,128)(2,1)S(1)}, bf16[512,1920]{1,0:T(8,128)(2,1)S(1)}, u32[]{:S(2)}, u32[]{:S(2)}) collective-permute-start(bf16[512,1920]{1,0:T(8,128)(2,1)S(1)} %bitcast.40), channel_id=1, source_target_pairs={{0,8},{8,0},{1,9},{9,1},{2,10},{10,2},{3,11},{11,3},{4,12},{12,4},... | collective-permute-start | bytes 5898248 | tf_op jit(solution)/shard_map/ppermute | solution.py:527
  63.7 12.7 %collective-permute-start.14 = (bf16[512,1408]{1,0:T(8,128)(2,1)S(1)}, bf16[512,1408]{1,0:T(8,128)(2,1)S(1)}, u32[]{:S(2)}, u32[]{:S(2)}) collective-permute-start(bf16[512,1408]{1,0:T(8,128)(2,1)S(1)} %get-tuple-element.88), channel_id=1, source_target_pairs={{0,8},{8,0},{1,9},{9,1},{2,10},{10,2},{3,11},{11,3},{4,12},{12,4},... | collective-permute-start | bytes 4325384 | tf_op jit(solution)/shard_map/ppermute | solution.py:527
  71.3 4.9 %collective-permute-start.13 = (bf16[512,512]{1,0:T(8,128)(2,1)S(1)}, bf16[512,512]{1,0:T(8,128)(2,1)S(1)}, u32[]{:S(2)}, u32[]{:S(2)}) collective-permute-start(bf16[512,512]{1,0:T(8,128)(2,1)S(1)} %get-tuple-element.86), channel_id=1, source_target_pairs={{0,8},{8,0},{1,9},{9,1},{2,10},{10,2},{3,11},{11,3},{4,12},{12,4},... | collective-permute-start | bytes 1572872 | tf_op jit(solution)/shard_map/ppermute | solution.py:527
  71.8 8.0 %collective-permute-start.15 = (bf16[272,384]{1,0:T(8,128)(2,1)S(1)}, bf16[272,384]{1,0:T(8,128)(2,1)S(1)}, u32[]{:S(2)}, u32[]{:S(2)}) collective-permute-start(bf16[272,384]{1,0:T(8,128)(2,1)S(1)} %get-tuple-element.90), channel_id=1, source_target_pairs={{0,1},{1,0},{2,3},{3,2},{4,5},{5,4},{6,7},{7,6},{8,9},{9,8},{10,11... | collective-permute-start | bytes 626696 | tf_op jit(solution)/shard_map/ppermute | solution.py:540
  71.8 12.2 %collective-permute-start.16 = (bf16[272,384]{1,0:T(8,128)(2,1)S(1)}, bf16[272,384]{1,0:T(8,128)(2,1)S(1)}, u32[]{:S(2)}, u32[]{:S(2)}) collective-permute-start(bf16[272,384]{1,0:T(8,128)(2,1)S(1)} %get-tuple-element.91), channel_id=1, source_target_pairs={{0,3},{1,2},{2,1},{3,0},{4,7},{5,6},{6,5},{7,4},{8,11},{9,10},{10,... | collective-permute-start | bytes 626696 | tf_op jit(solution)/shard_map/ppermute | solution.py:540
  74.9 11.0 %collective-permute-start.17 = (bf16[272,384]{1,0:T(8,128)(2,1)S(1)}, bf16[272,384]{1,0:T(8,128)(2,1)S(1)}, u32[]{:S(2)}, u32[]{:S(2)}) collective-permute-start(bf16[272,384]{1,0:T(8,128)(2,1)S(1)} %get-tuple-element.92), channel_id=1, source_target_pairs={{0,2},{1,3},{2,0},{3,1},{4,6},{5,7},{6,4},{7,5},{8,10},{9,11},{10,... | collective-permute-start | bytes 626696 | tf_op jit(solution)/shard_map/ppermute | solution.py:540
  87.9 38.2 %all-to-all-start = ((bf16[64,8,1920]{2,1,0:T(8,128)(2,1)}), bf16[64,8,1920]{2,1,0:T(8,128)(2,1)S(1)}, u32[]{:S(2)}, u32[]{:S(2)}) async-start(bf16[64,8,1920]{2,1,0:T(8,128)(2,1)} %bitcast.44), calls=%async_computation | async-start | bytes 3932160 | tf_op jit(solution)/shard_map/all_to_all | solution.py:676
  97.4 28.7 %collective-permute-start.18 = (bf16[272,384]{1,0:T(8,128)(2,1)S(1)}, bf16[272,384]{1,0:T(8,128)(2,1)S(1)}, u32[]{:S(2)}, u32[]{:S(2)}) collective-permute-start(bf16[272,384]{1,0:T(8,128)(2,1)S(1)} %get-tuple-element.101), channel_id=1, source_target_pairs={{0,4},{4,0},{1,5},{5,1},{2,6},{6,2},{3,7},{7,3},{8,12},{12,8},{9,1... | collective-permute-start | bytes 626696 | tf_op jit(solution)/shard_map/ppermute | solution.py:527

commit v4 on v3

--- a/solution.py
+++ b/solution.py
@@ -11,9 +11,15 @@
 HEADS = 6
 FF = 1536
 EPSILON = 1e-06
-FIRST = 512
-SECOND = 1408
-TAIL = 640
+FIRST, FIRST_LAST = 768, 512
+SECOND, SECOND_LAST = 1024, 640
+WIDE = FIRST + SECOND
+
+
+def cut_of(more, width):
+    return min(width - more, (more // 256) * 128 + (more // 128 % 2) * 128)
+
+
 FSDP = ("xl", "y", "core")
 SEQ = ("xh", "z")
 CHIPS = ("xl", "y", "xh", "z")
@@ -63,65 +69,71 @@
     return jnp.where((lane >= 64) == (head % 2 == 1), pair, jnp.zeros_like(pair))
 
 
-def unpacker(ids_ref, near_ref, far_ref, offset):
+def places_of(j, base):
+    return (
+        jnp.concatenate([base + j, base + 3 + j], axis=0),
+        jnp.where(j < 2, base + 6 + j, -1),
+        jnp.concatenate([jnp.where(j == 2, base + 6, -1), jnp.where(j == 2, base + 7, -1)], axis=0),
+    )
+
+
+def unpacker(ids, near_ref, far_ref):
     row = iota((96, 1), 0)
     device = (row * 43691) >> 17
     j = row - 3 * device
-    run = (device >> 4) * 4 + (((device >> 3) & 1) ^ ids_ref[2]) * 2 + ((device >> 2) & 1)
-    z = (device & 3) ^ ids_ref[4]
+    z = (device & 3) ^ ids[4]
+    run = (device >> 4) * 4 + (((device >> 3) & 1) ^ ids[2]) * 2 + ((device >> 2) & 1)
     base = run * 32 + (z ^ (z >> 1)) * 8
-    places = [
-        pick(columns, 256)
-        for columns in (
-            jnp.concatenate([base + j, base + 3 + j], axis=0),
-            jnp.concatenate([jnp.where(j < 2, base + 6 + j, -1), jnp.where(j == 2, base + 6, -1)], axis=0),
-        )
-    ]
-    here = 2 * ids_ref[3] + ids_ref[0]
-
-    def band(number, lanes):
+    places = [pick(columns, 256) for columns in places_of(j, base)]
+    here = 2 * ids[3] + ids[0]
+
+    def unpack(number, offset, width, more):
         runs = []
         for low in range(2):
-            y = (2 * (number & 1) + low - ids_ref[1]) & 3
+            y = (2 * (number & 1) + low - ids[1]) & 3
             for ref in (near_ref, far_ref):
                 for upper in range(2):
                     x = (2 * upper + (number >> 1) - here) & 3
                     first = pl.multiple_of((x * 4 + y) * 32, 32)
-                    runs.append(ref[pl.ds(first, 32), lanes])
-        return jnp.concatenate(runs, axis=0)
-
-    def unpack(number, width, more):
-        rows = band(number, slice(offset, offset + width))
+                    runs.append(ref[pl.ds(first, 32), offset : offset + width])
+        rows = jnp.concatenate(runs, axis=0)
         both = dot(places[0], rows).astype(BF)
-        ends = dot(places[1], rows[:, : 2 * more])
-        last = (ends[:96, :more] + ends[96:, more:]).astype(BF)
-        return both[:96], both[96:], last
+        cut = cut_of(more, width)
+        ends = dot(places[2], rows[:, more : more + cut])
+        third = jnp.concatenate([ends[:96], ends[96:, : more - cut]], axis=1)
+        return both[:96], both[96:], (dot(places[1], rows[:, :more]) + third).astype(BF)
 
     return unpack
 
 
-def give(ids_ref, targets, whole, third):
+def give(ids, targets, whole, third):
     width = targets[0].shape[1]
     more = third.shape[1]
+    cut = cut_of(more, width)
     row = iota((256, 1), 0)
     q = row & 7
-    for side, target in enumerate(targets):
-        core = (ids_ref[2] + side) & 1
-        base = ((row >> 6) * 2 + core) * 24 + ((row >> 3) & 7) * 3
-        place = [
-            pick(jnp.where((q >= low) & (q < high), base + q + offset, -1), 192)
-            for low, high, offset in ((0, 3, 0), (3, 6, -3), (6, 8, -6), (6, 7, -4))
-        ]
-        for band in range(2):
-            rows = slice(band * 192, band * 192 + 192)
-            area = slice(band * 256, band * 256 + 256)
-            both = dot(place[0], whole[rows, :width]) + dot(place[1], whole[rows, width:])
-            target[area, :more] = (both[:, :more] + dot(place[2], third[rows, :])).astype(BF)
-            target[area, more : 2 * more] = (
-                both[:, more : 2 * more] + dot(place[3], third[rows, :])
-            ).astype(BF)
-            if 2 * more < width:
-                target[area, 2 * more :] = both[:, 2 * more :].astype(BF)
+    core = (ids[2] + (row >> 7)) & 1
+    base = (((row >> 6) & 1) * 2 + core) * 24 + ((row >> 3) & 7) * 3
+    pair = pick(
+        jnp.where(q < 3, base + q, jnp.where(q < 6, 96 + base + q - 3, -1)), 192
+    )
+    ends = pick(jnp.where(q >= 6, base + q - 6, -1), 96)
+    last = pick(jnp.where(q == 6, base + 2, jnp.where(q == 7, 96 + base + 2, -1)), 192)
+    for band in range(4):
+        rows = slice(band * 96, band * 96 + 96)
+        both = dot(pair, jnp.concatenate([whole[rows, :width], whole[rows, width:]], axis=0))
+        thirds = [third[rows, :cut], third[rows, cut:more]]
+        if more < 2 * cut:
+            thirds[1] = jnp.concatenate([thirds[1], jnp.zeros((96, 2 * cut - more), BF)], axis=1)
+        left = (both[:, :more] + dot(ends, third[rows, :])).astype(BF)
+        right = (both[:, more : more + cut] + dot(last, jnp.concatenate(thirds, axis=0))).astype(BF)
+        for side, target in enumerate(targets):
+            area = slice(band * 128, band * 128 + 128)
+            own = slice(side * 128, side * 128 + 128)
+            target[area, :more] = left[own]
+            target[area, more : more + cut] = right[own]
+            if more + cut < width:
+                target[area, more + cut :] = both[own, more + cut :].astype(BF)
 
 
 def interleave():
@@ -130,8 +142,11 @@
 
 
 def pack_kernel(
-    ids_ref,
-    biases_ref,
+    b_query_ref,
+    b_value_ref,
+    b_out_ref,
+    b_fc2_ref,
+    b_fc1_ref,
     latents_ref,
     cotangent_ref,
     modulation_ref,
@@ -144,7 +159,7 @@
     condition_ref,
     scratch,
 ):
-    upper = ids_ref[3]
+    upper = lax.axis_index("xh")
     send_ref[0] = latents_ref[1 - upper]
     send_ref[1] = cotangent_ref[1 - upper]
     modulation = jnp.where(upper == 1, modulation_ref[1:2, :], modulation_ref[0:1, :])
@@ -155,12 +170,14 @@
     scratch[0:3, : 3 * D] = w_qkv_ref[...].astype(F32)
     row, lane = iota((8, 128), 0), iota((8, 128), 1)
     tile = jnp.zeros((8, 128), F32)
-    for j in range(3):
-        for column in range(8):
-            index = 3 * column + j if column < 4 else 12 + 4 * j + column - 4
-            tile = jnp.where((row == j) & (lane == column), biases_ref[0:1, index : index + 1], tile)
-    scratch[:, 3 * D : 3 * D + 128] = tile
-    start = 3 * D + 128
+    for column, ref in enumerate((b_query_ref, b_value_ref, b_out_ref, b_fc2_ref, b_fc1_ref)):
+        values = ref[...].astype(F32)
+        for index in range(values.shape[1]):
+            j, place = (index, column) if column < 4 else (index // 4, 4 + index % 4)
+            tile = jnp.where((row == j) & (lane == place), values[:, index : index + 1], tile)
+    scratch[:, 5 * D : 5 * D + 128] = tile
+    scratch[0:3, 4 * D : 5 * D] = w_out_ref[...].astype(F32)
+    start = 5 * D + 128
     swap = interleave()
     for block in range(3):
         moved = dot(w_fc1_ref[:, block * 512 : block * 512 + 512], swap)
@@ -172,35 +189,36 @@
     for j in range(3):
         for part in range(4):
             line = 4 * j + part
-            scratch[j : j + 1, start + part * D : start + part * D + D] = rows[line : line + 1, :]
-    start = start + FF
-    scratch[0:3, start : start + D] = w_out_ref[...].astype(F32)
+            lanes = start + part * D if part < 3 else 3 * D
+            scratch[j : j + 1, lanes : lanes + D] = rows[line : line + 1, :]
 
     def place(width, begin, more):
-        result = jnp.zeros((8, width), F32)
+        cut = cut_of(more, width)
         group = scratch[:, begin : begin + width]
-        result = result + jnp.where(iota((8, width), 0) < 3, group, 0.0)
+        row = iota((8, width), 0)
+        result = jnp.where(row < 3, group, 0.0)
         group = scratch[:, begin + width : begin + 2 * width]
-        scratch_rows = [group[j : j + 1, :] for j in range(3)]
         for j in range(3):
-            result = jnp.where(iota((8, width), 0) == 3 + j, scratch_rows[j], result)
+            result = jnp.where(row == 3 + j, group[j : j + 1, :], result)
         group = scratch[:, begin + 2 * width : begin + 2 * width + more]
-        empty = jnp.zeros((1, width - 2 * more), F32)
-        ends = [empty] if width > 2 * more else []
-        six = jnp.concatenate([group[0:1], group[2:3]] + ends, axis=1)
-        seven = jnp.concatenate([group[1:2], jnp.zeros((1, more), F32)] + ends, axis=1)
-        result = jnp.where(iota((8, width), 0) == 6, six, result)
-        result = jnp.where(iota((8, width), 0) == 7, seven, result)
+        for line, first, last in ((6, 0, cut), (7, cut, more)):
+            parts = [group[line - 6 : line - 5], group[2:3, first:last]]
+            rest = width - more - (last - first)
+            if rest:
+                parts.append(jnp.zeros((1, rest), F32))
+            result = jnp.where(row == line, jnp.concatenate(parts, axis=1), result)
         return result.astype(BF)
 
-    payload_ref[:, :FIRST] = place(FIRST, 0, 256)
-    payload_ref[:, FIRST:] = place(SECOND, 3 * D + 128, TAIL)
+    payload_ref[:, :FIRST] = place(FIRST, 0, FIRST_LAST)
+    payload_ref[:, FIRST:] = place(SECOND, 2 * FIRST + FIRST_LAST, SECOND_LAST)
+
+
+def device_ids():
+    return tuple(lax.axis_index(axis) for axis in ("xl", "y", "core", "xh", "z"))
 
 
 def attention_part(
-    ids_ref,
-    near_ref,
-    far_ref,
+    unpack,
     token_0,
     token_1,
     token_23,
@@ -211,20 +229,23 @@
     keys_ref,
     values_ref,
     keys_t,
-    probability_ref,
+    exponent_ref,
     biases_ref,
     attended_t,
     values_t,
+    weights_scr,
+    w_fc2,
+    w_out,
 ):
-    unpack = unpacker(ids_ref, near_ref, far_ref, 0)
     columns = []
     for number in range(4):
         rows = slice(number * 96, number * 96 + 96)
-        one, two, last = unpack(number, FIRST, 256)
+        one, two, last = unpack(number, 0, FIRST, FIRST_LAST)
         w_qkv_ref[rows, :FIRST] = one
-        w_qkv_ref[rows, FIRST : 2 * FIRST] = two
-        w_qkv_ref[rows, 2 * FIRST :] = last[:, :128]
-        columns.append(last[:, 128:].astype(F32))
+        w_qkv_ref[rows, FIRST:] = two[:, :D]
+        w_fc2[3 * D + number * 96 : 3 * D + number * 96 + 96, :] = two[:, D:]
+        w_out[rows, :] = last[:, :D]
+        columns.append(last[:, D:].astype(F32))
     biases = jnp.concatenate(columns, axis=0).T[:8, :]
     biases_ref[...] = biases
     shift_one, scale_one = condition_ref[0:1, :], condition_ref[1:2, :]
@@ -243,20 +264,22 @@
     query = (dot(hidden_ref[:own, :], w_qkv_ref[:, :D]) + biases[0:1, :]).astype(BF)
     query = query * jnp.asarray(0.125, BF)
     query_ref[...] = query
+    weights_scr[...] = jnp.zeros_like(weights_scr)
     for head in range(HEADS):
         tile = slice(head // 2 * 128, head // 2 * 128 + 128)
         cut = slice(head * 64, head * 64 + 64)
         scores = dot_nt(keys_ref[:, tile], one_head(query[:, tile], head))
         exponent = jnp.exp(scores - jnp.max(scores, axis=0, keepdims=True))
-        probability = (exponent * (1.0 / column_sum(exponent))).astype(BF)
-        probability_ref[head] = probability
-        attended_t[cut, :] = dot(values_t[cut, :], probability)
+        weight = 1.0 / column_sum(exponent)
+        weights_scr[head : head + 1, :] = weight
+        exponent = exponent.astype(BF)
+        exponent_ref[head] = exponent
+        attended_t[cut, :] = dot(values_t[cut, :], exponent) * weight
 
 
 def forward_part(
-    ids_ref,
-    near_ref,
-    far_ref,
+    ids,
+    unpack,
     tokens_ref,
     swapped_ref,
     cotangent_ref,
@@ -268,10 +291,12 @@
     weighted_ref,
     vectors_ref,
     rows_ref,
+    more_ref,
     keep_ref,
     send_ref,
     biases_ref,
     attended_t,
+    weights_scr,
     w_fc1,
     w_fc2,
     w_out,
@@ -279,20 +304,15 @@
     whole,
     third,
 ):
-    unpack = unpacker(ids_ref, near_ref, far_ref, FIRST)
     for number in range(4):
         rows = slice(number * 96, number * 96 + 96)
-        one, two, last = unpack(number, SECOND, TAIL)
+        one, two, last = unpack(number, FIRST, SECOND, SECOND_LAST)
         w_fc1[rows, :SECOND] = one
-        w_fc1[rows, SECOND:] = two[:, :128]
-        for part in range(4):
+        w_fc1[rows, SECOND:] = two[:, : FF - SECOND]
+        columns = jnp.concatenate([two[:, FF - SECOND :], last], axis=1)
+        for part in range(3):
             area = slice(part * D + number * 96, part * D + number * 96 + 96)
-            if part < 3:
-                w_fc2[area, :] = two[:, 128 + part * D : 128 + (part + 1) * D]
-            else:
-                w_fc2[area, :128] = two[:, 128 + part * D :]
-                w_fc2[area, 128:] = last[:, :256]
-        w_out[rows, :] = last[:, 256:]
+            w_fc2[area, :] = columns[:, part * D : (part + 1) * D]
     b_out, b_fc2 = biases_ref[2:3, :], biases_ref[3:4, :]
     b_fc1 = jnp.concatenate([biases_ref[4 + i : 5 + i, :] for i in range(4)], axis=1)
     gate_one, shift_two, scale_two, gate_two = (condition_ref[i : i + 1, :] for i in range(2, 6))
@@ -312,21 +332,23 @@
     active = (0.5 * inner * (1.0 + curve)).astype(BF)
     branch_two = dot(active, w_fc2[...]) + b_fc2
     output = (middle + gate_two * branch_two).astype(BF)
-    side = output_a.shape[0]
+    own = tokens_ref.shape[0]
+    side = own // 2
     output_a[...] = output[:side]
     output_b[...] = output[side:]
 
-    upstream = jnp.concatenate([cotangent_ref[ids_ref[3]], swapped_ref[1]], axis=0).astype(F32)
+    upstream = jnp.concatenate([cotangent_ref[ids[3]], swapped_ref[1]], axis=0).astype(F32)
     rows_ref[...] = jnp.zeros_like(rows_ref)
     vectors_ref[...] = jnp.zeros_like(vectors_ref)
     vectors_ref[5:6, :] = column_sum(upstream * branch_two)
     grad_two = (upstream * gate_two).astype(BF)
     rows_ref[3:4, :] = column_sum(grad_two.astype(F32))
     second = dot_tn(active, grad_two).astype(BF)
-    for part in range(3):
-        whole[:, FF + part * D : FF + (part + 1) * D] = second[part * D : (part + 1) * D, :]
-    whole[:, FF + 3 * D :] = second[3 * D :, :128]
-    third[:, :256] = second[3 * D :, 128:]
+    whole[:, FF : FF + D] = second[:D, :]
+    whole[:, FF + D :] = second[D : 2 * D, :128]
+    third[:, :256] = second[D : 2 * D, 128:]
+    third[:, 256:] = second[2 * D : 3 * D, :]
+    more_ref[:, :D] = second[3 * D :, :]
     grad_inner = (dot_nt(grad_two, w_fc2[...]) * slope_scr[...]).astype(BF)
     whole[:, :FF] = dot_tn(hidden_two, grad_inner).astype(BF)
     inner_sum = column_sum(grad_inner.astype(F32))
@@ -341,40 +363,51 @@
     middle_grad_ref[...] = grad_middle
     vectors_ref[2:3, :] = column_sum(grad_middle * branch_one)
     grad_one = (grad_middle * gate_one).astype(BF)
-    third[:, 256:] = dot_tn(attended, grad_one).astype(BF)
+    more_ref[:, D:] = dot_tn(attended, grad_one).astype(BF)
     rows_ref[2:3, :] = column_sum(grad_one.astype(F32))
-    grad_attended = dot_nt(grad_one, w_out[...]).astype(BF)
+    columns = weights_scr[...].T
+    lane = iota((own, 128), 1)
+    weight = jnp.concatenate(
+        [
+            jnp.where(lane < 64, columns[:, 2 * pair : 2 * pair + 1], columns[:, 2 * pair + 1 : 2 * pair + 2])
+            for pair in range(HEADS // 2)
+        ],
+        axis=1,
+    )
+    grad_attended = (dot_nt(grad_one, w_out[...]) * weight).astype(BF)
     attended_grad_ref[...] = grad_attended
     products = grad_attended.astype(F32).T * attended_t[...]
     weighted_ref[...] = jnp.zeros_like(weighted_ref)
     for head in range(HEADS):
         weighted_ref[head : head + 1, :] = column_sum(products[head * 64 : head * 64 + 64, :])
-    give(ids_ref, (keep_ref, send_ref), whole, third)
+    give(ids, (keep_ref, send_ref), whole, third)
 
 
 def front_kernel(
-    ids_ref, near_ref, far_ref, token_0, token_1, token_23, swapped_ref, cotangent_ref, condition_ref,
-    w_qkv_ref, hidden_ref, query_ref, keys_ref, values_ref, keys_t, probability_ref,
+    near_ref, far_ref, token_0, token_1, token_23, swapped_ref, cotangent_ref, condition_ref,
+    w_qkv_ref, hidden_ref, query_ref, keys_ref, values_ref, keys_t, exponent_ref,
     output_a, output_b, middle_grad_ref, attended_grad_ref, weighted_ref, vectors_ref, rows_ref,
-    keep_ref, send_ref,
-    values_t, biases_ref, attended_t, w_fc1, w_fc2, w_out, slope_scr, whole, third,
+    more_ref, keep_ref, send_ref,
+    values_t, weights_scr, biases_ref, attended_t, w_fc1, w_fc2, w_out, slope_scr, whole, third,
 ):
+    ids = device_ids()
+    unpack = unpacker(ids, near_ref, far_ref)
     attention_part(
-        ids_ref, near_ref, far_ref, token_0, token_1, token_23, condition_ref,
-        w_qkv_ref, hidden_ref, query_ref, keys_ref, values_ref, keys_t, probability_ref,
-        biases_ref, attended_t, values_t,
+        unpack, token_0, token_1, token_23, condition_ref,
+        w_qkv_ref, hidden_ref, query_ref, keys_ref, values_ref, keys_t, exponent_ref,
+        biases_ref, attended_t, values_t, weights_scr, w_fc2, w_out,
     )
     forward_part(
-        ids_ref, near_ref, far_ref, token_0, swapped_ref, cotangent_ref, condition_ref,
+        ids, unpack, token_0, swapped_ref, cotangent_ref, condition_ref,
         output_a, output_b, middle_grad_ref, attended_grad_ref, weighted_ref, vectors_ref, rows_ref,
-        keep_ref, send_ref, biases_ref, attended_t, w_fc1, w_fc2, w_out, slope_scr, whole, third,
+        more_ref, keep_ref, send_ref, biases_ref, attended_t, weights_scr, w_fc1, w_fc2, w_out, slope_scr, whole, third,
     )
 
 
 def backward_kernel(
-    ids_ref, token_0, token_1, token_23, condition_ref,
-    w_qkv_ref, query_ref, keys_ref, values_ref, keys_t, probability_ref,
-    attended_grad_ref, weighted_ref, vectors_in, hidden_ref, rows_ref,
+    token_0, token_1, token_23, condition_ref,
+    w_qkv_ref, query_ref, keys_ref, values_ref, keys_t, exponent_ref,
+    attended_grad_ref, weighted_ref, vectors_in, hidden_ref, rows_ref, more_ref,
     piece_0, piece_1, piece_2, piece_3, keep_ref, send_ref,
     query_t, vectors_ref, grad_query_ref, key_grads, value_grads, whole, third, tall,
 ):
@@ -385,13 +418,13 @@
         value_sum = None
         for head in (2 * pair, 2 * pair + 1):
             cut = slice(head * 64, head * 64 + 64)
-            probability = probability_ref[head]
+            exponent = exponent_ref[head]
             grad_head = one_head(attended_grad_ref[:, tile], head)
             grad_probability = dot_nt(values_ref[:, tile], grad_head)
             grad_scores = (
-                probability.astype(F32) * (grad_probability - weighted_ref[head : head + 1, :])
+                exponent.astype(F32) * (grad_probability - weighted_ref[head : head + 1, :])
             ).astype(BF)
-            value_part = dot(probability, grad_head)
+            value_part = dot(exponent, grad_head)
             key_part = dot(grad_scores, one_head(query_ref[:, tile], head))
             value_sum = value_part if value_sum is None else value_sum + value_part
             key_sum = key_part if key_sum is None else key_sum + key_part
@@ -426,11 +459,11 @@
     tall[1:2, :] = column_sum(value_grads[...].astype(F32))
     whole[:, :D] = dot_tn(hidden_ref[:own, :], grad_query_ref[...]).astype(BF)
     whole[:, D : 2 * D] = dot_tn(hidden_ref[...], key_grads[...]).astype(BF)
-    value_weight = dot_tn(hidden_ref[...], value_grads[...]).astype(BF)
-    whole[:, 2 * D :] = value_weight[:, :256]
-    third[:, :128] = value_weight[:, 256:]
-    third[:, 128:] = tall[...].T.astype(BF)
-    give(ids_ref, (keep_ref, send_ref), whole, third)
+    whole[:, 2 * D : 3 * D] = dot_tn(hidden_ref[...], value_grads[...]).astype(BF)
+    whole[:, 3 * D :] = more_ref[:, :D]
+    third[:, :D] = more_ref[:, D:]
+    third[:, D:] = tall[...].T.astype(BF)
+    give(device_ids(), (keep_ref, send_ref), whole, third)
 
 
 def two_parts(vectors):
@@ -465,12 +498,18 @@
     sums_ref[...] = sums
 
 
+def last_rows(block, more):
+    cut = cut_of(more, block.shape[1])
+    third = jnp.concatenate([block[6:7, more : more + cut], block[7:8, more : 2 * more - cut]], axis=1)
+    return jnp.concatenate([block[6:8, :more], third], axis=0)
+
+
 def last_kernel(
-    ids_ref, output_ref, grad_ref, other_ref, sums_ref, pieces_ref,
+    output_ref, grad_ref, other_ref, sums_ref, pieces_ref,
     output_out, grad_out, modulation_out,
     qkv_ref, b_query, b_value, b_out, b_fc1, b_fc2, fc1_ref, fc2_ref, out_ref,
 ):
-    upper = ids_ref[3]
+    upper = lax.axis_index("xh")
     side = output_ref.shape[0]
     output_out[upper] = output_ref[...]
     output_out[1 - upper] = other_ref[side : 2 * side, :]
@@ -488,10 +527,10 @@
         total = total + pieces_ref[index].astype(F32)
     small, total = total[:, :FIRST], total[:, FIRST:]
     qkv_ref[:, :FIRST] = small[0:3]
-    qkv_ref[:, FIRST : 2 * FIRST] = small[3:6]
-    last = jnp.concatenate([small[6:8, :256], small[6:7, 256:]], axis=0)
-    qkv_ref[:, 2 * FIRST :] = last[:, :128]
-    columns = jnp.concatenate([last[:, 128:], jnp.zeros((5, 128), F32)], axis=0).T
+    qkv_ref[:, FIRST:] = small[3:6, :D]
+    last = last_rows(small, FIRST_LAST)
+    out_ref[...] = last[:, :D]
+    columns = jnp.concatenate([last[:, D:], jnp.zeros((5, 128), F32)], axis=0).T
     for column, ref in enumerate((b_query, b_value, b_out, b_fc2)):
         ref[...] = columns[column : column + 1, :3]
     lane = iota((1, 12), 1)
@@ -502,8 +541,7 @@
     b_fc1[...] = wide
     swap = interleave()
     one, two = total[0:3], total[3:6]
-    last = jnp.concatenate([total[6:8, :TAIL], total[6:7, TAIL : 2 * TAIL]], axis=0)
-    fc1 = jnp.concatenate([one, two[:, :128]], axis=1)
+    fc1 = jnp.concatenate([one, two[:, : FF - SECOND]], axis=1)
     for block in range(3):
         rest = jnp.concatenate(
             [fc1[:, i * D + block * 128 : i * D + block * 128 + 128] for i in range(4)], axis=1
@@ -515,12 +553,11 @@
             step = dot_nt(part, swap)
             moved = step if moved is None else moved + step
         fc1_ref[:, block * 512 : block * 512 + 512] = moved
-    fc2 = jnp.concatenate([two[:, 128:], last[:, :256]], axis=1)
+    fc2 = jnp.concatenate([two[:, FF - SECOND :], last_rows(total, SECOND_LAST), small[3:6, D:]], axis=1)
     for j in range(3):
         for part in range(4):
             line = 4 * j + part
             fc2_ref[line : line + 1, :] = fc2[j : j + 1, part * D : part * D + D]
-    out_ref[...] = last[:, 256:]
 
 
 def shift(array, axis, step, size):
@@ -552,19 +589,17 @@
     return [pltpu.with_memory_space_constraint(array, pltpu.VMEM) for array in arrays]
 
 
-def call(kernel, out_shape, scratch, ids, *operands, limit=16):
-    specs = [] if ids is None else [pl.BlockSpec(memory_space=pltpu.SMEM)]
-    given = [] if ids is None else [ids]
+def call(kernel, out_shape, scratch, *operands, limit=16):
+    given = []
     for operand in operands:
         if isinstance(operand, list):
             given += operand
         else:
             given.append(pltpu.with_memory_space_constraint(operand, pltpu.HBM))
-    specs += [pl.BlockSpec(memory_space=pltpu.VMEM)] * (len(given) - len(specs))
     return pl.pallas_call(
         kernel,
         out_shape=out_shape,
-        in_specs=specs,
+        in_specs=[pl.BlockSpec(memory_space=pltpu.VMEM)] * len(given),
         out_specs=tuple(pl.BlockSpec(memory_space=pltpu.VMEM) for _ in out_shape),
         scratch_shapes=scratch,
         compiler_params=pltpu.CompilerParams(vmem_limit_bytes=limit * 1024 * 1024),
@@ -575,21 +610,16 @@
     side = latents.shape[1]
     own = 2 * side
     length = 4 * own
-    ids = jnp.stack([lax.axis_index(a) for a in ("xl", "y", "core", "xh", "z")]).astype(jnp.int32)
-    biases = sum(
-        jnp.pad(b.astype(F32)[None], ((0, 0), (first, 128 - first - b.shape[0])))
-        for b, first in ((b_query, 0), (b_value, 3), (b_out, 6), (b_fc2, 9), (b_fc1, 12))
-    )
     upper = lax.axis_index("xh") == 1
     payload, send_pair, condition = call(
         pack_kernel,
-        (sds(8, FIRST + SECOND), sds(2, side, D), pltpu.HBM((8, D), F32)),
-        [vmem(8, 3 * D + 128 + 2 * FF + D, dtype=F32)],
-        ids, biases, latents, cotangent, modulation, w_qkv, w_out, w_fc1, w_fc2,
+        (sds(8, WIDE), sds(2, side, D), vmem(8, D, dtype=F32)),
+        [vmem(8, 4 * D + 128 + 2 * FF, dtype=F32)],
+        *(b[None] for b in (b_query, b_value, b_out, b_fc2, b_fc1)), latents, cotangent, modulation, w_qkv, w_out, w_fc1, w_fc2,
     )
     swapped = shift(send_pair, "xh", 1, 2)
     column = jnp.stack([payload, trade(payload, 1)])
-    column = jnp.stack([column, trade(column, 3)]).reshape(4, 8, FIRST + SECOND)
+    column = jnp.stack([column, trade(column, 3)]).reshape(4, 8, WIDE)
     column, swapped = lax.optimization_barrier((column, swapped))
     tokens = jnp.concatenate([jnp.where(upper, latents[1], latents[0]), swapped[0]])
     near_tokens = trade(tokens, 1)
@@ -600,12 +630,12 @@
     all_tokens = (tokens, near_tokens, far_tokens)
     half = plane.shape[0] // 2
     opposite = jnp.concatenate([shift_x(before[:half], 1), shift_x(after[half:], -1)])
-    near = jnp.stack([plane, after, opposite, before]).reshape(-1, FIRST + SECOND)
+    near = jnp.stack([plane, after, opposite, before]).reshape(-1, WIDE)
     other = shift(near, "core", 1, 2)
 
     (
-        w_all, hidden, query, keys, values, keys_t, probability,
-        output_a, output_b, middle_grad, attended_grad, weighted, vectors, bias_sums, keep_two, send_two,
+        w_all, hidden, query, keys, values, keys_t, exponents,
+        output_a, output_b, middle_grad, attended_grad, weighted, vectors, bias_sums, more_grads, keep_two, send_two,
     ) = call(
         front_kernel,
         (
@@ -616,18 +646,20 @@
             vmem(length, D),
             vmem(D, length),
             vmem(HEADS, length, own),
-            pltpu.HBM((side, D), BF),
-            pltpu.HBM((side, D), BF),
-            pltpu.HBM((own, D), F32),
+            vmem(side, D),
+            vmem(side, D),
+            vmem(own, D, dtype=F32),
             vmem(own, D),
             vmem(8, own, dtype=F32),
             vmem(8, D, dtype=F32),
             vmem(8, D, dtype=F32),
+            vmem(D, 2 * D),
             vmem(512, SECOND),
             vmem(512, SECOND),
         ),
         [
             vmem(D, length),
+            vmem(128, own, dtype=F32),
             vmem(8, D, dtype=F32),
             vmem(D, own, dtype=F32),
             vmem(D, FF),
@@ -635,9 +667,9 @@
             vmem(D, D),
             vmem(own, FF, dtype=F32),
             vmem(D, 2 * SECOND),
-            vmem(D, TAIL),
+            vmem(D, SECOND_LAST),
         ],
-        ids, hold(near, other, *all_tokens, swapped), cotangent, condition,
+        hold(near, other, *all_tokens, swapped, cotangent, condition),
         limit=32,
     )
     other_two = shift(send_two, "core", 1, 2)
@@ -652,13 +684,12 @@
             vmem(length, D),
             vmem(length, D),
             vmem(D, 2 * FIRST),
-            vmem(D, 256),
+            vmem(D, FIRST_LAST),
             vmem(128, D, dtype=F32),
         ],
-        ids, hold(*all_tokens), condition,
         hold(
-            w_all, query, keys, values, keys_t, probability, attended_grad, weighted, vectors,
-            hidden, bias_sums,
+            *all_tokens, condition, w_all, query, keys, values, keys_t, exponents, attended_grad, weighted, vectors,
+            hidden, bias_sums, more_grads,
         ),
         limit=24,
     )
@@ -668,12 +699,11 @@
     mixed, arrived = lax.optimization_barrier((mixed, arrived))
     grad_a, grad_b, sums = call(
         final_kernel,
-        (pltpu.HBM((side, D), BF), vmem(2 * side + 16, D), vmem(8, D, dtype=F32)),
+        (vmem(side, D), vmem(2 * side + 16, D), vmem(8, D, dtype=F32)),
         [],
-        None, hold(tokens), condition, middle_grad, hold(*arrived), output_b,
-    )
-    mixed, grad_b = lax.optimization_barrier((mixed, grad_b))
-    pieces = lax.all_to_all(mixed.reshape(64, 8, FIRST + SECOND), CHIPS, 0, 0, tiled=True)
+        hold(tokens, condition, middle_grad, *arrived, output_b),
+    )
+    pieces = lax.all_to_all(mixed.reshape(64, 8, WIDE), CHIPS, 0, 0, tiled=True)
     grad_back = shift(grad_b, "xh", 1, 2)
     (
         output, input_grad, modulation_grad,
@@ -695,7 +725,7 @@
             sds(3, D, dtype=F32),
         ),
         [],
-        ids, output_a, grad_a, hold(grad_back, sums, pieces),
+        hold(output_a, grad_a, grad_back, sums, pieces),
     )
     return (
         output,

time: 130 us -> 119 us (0.915)
  Pallas kernels: 30.2 us -> 23.1 us
  waiting for transfers between devices: 52.4 us -> 48.5 us
  other arithmetic: 4.75 us -> 3.38 us
    pallas_call x5, Pallas kernels: 30.2 us -> 23.1 us  [call(): pl.pallas_call(kernel, out_shape=out_shape, in_specs=[pl.BlockSpec(memory...]
    ppermute x7, waiting for transfers between devices: 15.2 us -> 10.7 us  [trade(): return lax.ppermute(array, 'z', [(i, i ^ bits) for i in range(4)])]
    ppermute x4, waiting for transfers between devices: 4.18 us -> 8.46 us  [shift_x(): return lax.ppermute(array, X, moves)]
    ppermute x8, waiting for transfers between devices: 33 us -> 29.4 us  [shift(): lax.ppermute(array, axis, [(i, (i + step) % size) for i in range(size)])]
    add x1 -> x0, other arithmetic: 1.31 us -> none  [body(): sum((jnp.pad(b.astype(F32)[None], ((0, 0), (first, 128 - first - b.shape[...]
  transfers between devices with their start and end apart: 20 -> 20, of which waited for: 11 -> 12; matrix products, arithmetic and copies ran while one was open for 2% -> 3% of each run, Pallas kernels for 6% -> 6%
where the time goes in v4:
time: 119 us; the launch traced here: 118 us
  waiting for transfers between devices  48.5 us (41%)
  starting transfers between devices  41.2 us (35%)
  Pallas kernels  23.1 us (19%)
  other arithmetic  3.38 us (3%)
    ppermute x8, waiting for transfers between devices, shift(): lax.ppermute(array, axis, [(i, (i + step) % size) for i in range(size)])  29.4 us
    pallas_call x5, Pallas kernels, call(): pl.pallas_call(kernel, out_shape=out_shape, in_specs=[pl.BlockSpec(memory...  23.1 us
    ppermute x7, starting transfers between devices, trade(): return lax.ppermute(array, 'z', [(i, i ^ bits) for i in range(4)])  12.9 us
    ppermute x8, starting transfers between devices, shift(): lax.ppermute(array, axis, [(i, (i + step) % size) for i in range(size)])  12.2 us
    ppermute x7, waiting for transfers between devices, trade(): return lax.ppermute(array, 'z', [(i, i ^ bits) for i in range(4)])  10.7 us
    all_to_all x1, starting transfers between devices, body(): pieces = lax.all_to_all(mixed.reshape(64, 8, WIDE), CHIPS, 0, 0, tiled=True)  9.5 us
    ppermute x4, waiting for transfers between devices, shift_x(): return lax.ppermute(array, X, moves)  8.46 us
    ppermute x4, starting transfers between devices, shift_x(): return lax.ppermute(array, X, moves)  6.61 us
  transfers between devices with their start and end apart: 20, of which 12 were waited for; matrix products, arithmetic and copies ran while one was open for 3% of the time, Pallas kernels for 6%

profile of v4, /device:TPU:8, one launch (start us, length us, event | category | flops | bytes accessed | tf_op | source)
XLA Modules:
  0.0 118.1 jit_solution(11354615452861614851)
XLA Ops:
  0.6 1.5 %shard_map.211 = (bf16[8,1792]{1,0:T(8,128)(2,1)S(1)}, bf16[2,128,384]{2,1,0:T(8,128)(2,1)S(1)}, f32[8,384]{1,0:T(8,128)S(1)}) custom-call(bf16[1,3]{1,0:T(2,128)(2,1)} %bitcast.51, bf16[1,3]{1,0:T(2,128)(2,1)} %bitcast.52, bf16[1,3]{1,0:T(2,128)(2,1)} %bitcast.53, bf16[1,3]{1,0:T(2,128)(2,1)} %bitcast.54, bf16[1,12]{1,0:T(2,128)(2,1)} %bitcast.55, ...), custom_call_target="tpu_custom_call" | custom-call | tf_op jit(solution)/shard_map/pallas_call | solution.py:599
  2.2 2.0 %collective-permute-start = (bf16[8,1792]{1,0:T(8,128)(2,1)S(1)}, bf16[8,1792]{1,0:T(8,128)(2,1)S(1)}, u32[]{:S(2)}, u32[]{:S(2)}) collective-permute-start(bf16[8,1792]{1,0:T(8,128)(2,1)S(1)} %get-tuple-element.63), channel_id=1, source_target_pairs={{0,1},{1,0},{2,3},{3,2},{4,5},{5,4},{6,7},{7,6},{8,9},{9,8},{10,11... | collective-permute-start | bytes 86024 | tf_op jit(solution)/shard_map/ppermute | solution.py:577
  4.2 3.0 %collective-permute-start.2 = (bf16[2,128,384]{2,1,0:T(8,128)(2,1)S(1)}, bf16[2,128,384]{2,1,0:T(8,128)(2,1)S(1)}, u32[]{:S(2)}, u32[]{:S(2)}) collective-permute-start(bf16[2,128,384]{2,1,0:T(8,128)(2,1)S(1)} %get-tuple-element.64), channel_id=1, source_target_pairs={{0,4},{4,0},{1,5},{5,1},{2,6},{6,2},{3,7},{7,3},{8,12},{12,8},{9,1... | collective-permute-start | bytes 589832 | tf_op jit(solution)/shard_map/ppermute | solution.py:564
  7.2 3.0 %collective-permute-start.1 = (bf16[2,8,1792]{2,1,0:T(8,128)(2,1)S(1)}, bf16[2,8,1792]{2,1,0:T(8,128)(2,1)S(1)}, u32[]{:S(2)}, u32[]{:S(2)}) collective-permute-start(bf16[2,8,1792]{2,1,0:T(8,128)(2,1)S(1)} %get-tuple-element.119), channel_id=1, source_target_pairs={{0,3},{1,2},{2,1},{3,0},{4,7},{5,6},{6,5},{7,4},{8,11},{9,10},{10,... | collective-permute-start | bytes 172040 | tf_op jit(solution)/shard_map/ppermute | solution.py:577
  12.7 1.6 %collective-permute-start.5 = (bf16[4,8,1792]{2,1,0:T(8,128)(2,1)S(1)}, bf16[4,8,1792]{2,1,0:T(8,128)(2,1)S(1)}, u32[]{:S(2)}, u32[]{:S(2)}) collective-permute-start(bf16[4,8,1792]{2,1,0:T(8,128)(2,1)S(1)} %bitcast.42), channel_id=1, source_target_pairs={{0,16},{16,32},{32,48},{48,0},{1,17},{17,33},{33,49},{49,1},{2,18}... | collective-permute-start | bytes 344072 | tf_op jit(solution)/shard_map/ppermute | solution.py:564
  15.3 2.4 %collective-permute-start.3 = (bf16[4,8,1792]{2,1,0:T(8,128)(2,1)S(1)}, bf16[4,8,1792]{2,1,0:T(8,128)(2,1)S(1)}, u32[]{:S(2)}, u32[]{:S(2)}) collective-permute-start(bf16[4,8,1792]{2,1,0:T(8,128)(2,1)S(1)} %bitcast.44), channel_id=1, source_target_pairs={{0,48},{16,0},{32,16},{48,32},{1,49},{17,1},{33,17},{49,33},{2,50}... | collective-permute-start | bytes 344072 | tf_op jit(solution)/shard_map/ppermute | solution.py:564
  18.8 2.0 %collective-permute-done.4 = bf16[4,8,1792]{2,1,0:T(8,128)(2,1)S(1)} collective-permute-done((bf16[4,8,1792]{2,1,0:T(8,128)(2,1)S(1)}, bf16[4,8,1792]{2,1,0:T(8,128)(2,1)S(1)}, u32[]{:S(2)}, u32[]{:S(2)}) %collective-permute-start.4) | collective-permute-done | bytes 114720 | tf_op jit(solution)/shard_map/ppermute | solution.py:564
  22.7 2.0 %collective-permute-start.7 = (bf16[4,4,8,1792]{3,2,1,0:T(8,128)(2,1)S(1)}, bf16[4,4,8,1792]{3,2,1,0:T(8,128)(2,1)S(1)}, u32[]{:S(2)}, u32[]{:S(2)}) collective-permute-start(bf16[4,4,8,1792]{3,2,1,0:T(8,128)(2,1)S(1)} %get-tuple-element.115), channel_id=1, source_target_pairs={{0,68},{4,64},{64,0},{68,4},{1,69},{5,65},{65,1},{69,5},{2,70},{6,... | collective-permute-start | bytes 1376264 | tf_op jit(solution)/shard_map/ppermute | solution.py:573
  24.8 3.0 %collective-permute-start.9 = (bf16[2,256,384]{2,1,0:T(8,128)(2,1)S(1)}, bf16[2,256,384]{2,1,0:T(8,128)(2,1)S(1)}, u32[]{:S(2)}, u32[]{:S(2)}) collective-permute-start(bf16[2,256,384]{2,1,0:T(8,128)(2,1)S(1)} %pad_maximum_fusion.3), channel_id=1, source_target_pairs={{0,3},{1,2},{2,1},{3,0},{4,7},{5,6},{6,5},{7,4},{8,11},{9,10},{10,... | collective-permute-start | bytes 1179656 | tf_op jit(solution)/shard_map/ppermute | solution.py:577
  27.8 4.5 %collective-permute-done.6 = bf16[4,4,8,1792]{3,2,1,0:T(8,128)(2,1)S(1)} collective-permute-done((bf16[4,4,8,1792]{3,2,1,0:T(8,128)(2,1)S(1)}, bf16[4,4,8,1792]{3,2,1,0:T(8,128)(2,1)S(1)}, u32[]{:S(2)}, u32[]{:S(2)}) %collective-permute-start.6) | collective-permute-done | bytes 458784 | tf_op jit(solution)/shard_map/ppermute | solution.py:573
  32.3 1.6 %collective-permute-done.9.token_23 = bf16[2,256,384]{2,1,0:T(8,128)(2,1)S(1)} collective-permute-done((bf16[2,256,384]{2,1,0:T(8,128)(2,1)S(1)}, bf16[2,256,384]{2,1,0:T(8,128)(2,1)S(1)}, u32[]{:S(2)}, u32[]{:S(2)}) %collective-permute-start.9) | collective-permute-done | bytes 393248 | tf_op jit(solution)/shard_map/ppermute | solution.py:577
  34.0 3.2 %collective-permute-start.11 = (bf16[2,4,8,1792]{3,2,1,0:T(8,128)(2,1)S(1)}, bf16[2,4,8,1792]{3,2,1,0:T(8,128)(2,1)S(1)}, u32[]{:S(2)}, u32[]{:S(2)}) collective-permute-start(bf16[2,4,8,1792]{3,2,1,0:T(8,128)(2,1)S(1)} %slice.19), channel_id=1, source_target_pairs={{0,68},{4,64},{64,0},{68,4},{1,69},{5,65},{65,1},{69,5},{2,70},{6,... | collective-permute-start | bytes 688136 | tf_op jit(solution)/shard_map/ppermute | solution.py:573
  37.2 4.0 %collective-permute-done.10 = bf16[2,4,8,1792]{3,2,1,0:T(8,128)(2,1)S(1)} collective-permute-done((bf16[2,4,8,1792]{3,2,1,0:T(8,128)(2,1)S(1)}, bf16[2,4,8,1792]{3,2,1,0:T(8,128)(2,1)S(1)}, u32[]{:S(2)}, u32[]{:S(2)}) %collective-permute-start.10) | collective-permute-done | bytes 229408 | tf_op jit(solution)/shard_map/ppermute | solution.py:573
  41.8 3.8 %collective-permute-done.12.far_ref = bf16[512,1792]{1,0:T(8,128)(2,1)S(1)} collective-permute-done((bf16[512,1792]{1,0:T(8,128)(2,1)S(1)}, bf16[512,1792]{1,0:T(8,128)(2,1)S(1)}, u32[]{:S(2)}, u32[]{:S(2)}) %collective-permute-start.12) | collective-permute-done | bytes 1835040 | tf_op jit(solution)/shard_map/ppermute | solution.py:564
  45.5 12.4 %shard_map.212 = (bf16[384,1152]{1,0:T(8,128)(2,1)S(1)}, bf16[1024,384]{1,0:T(8,128)(2,1)S(1)}, bf16[256,384]{1,0:T(8,128)(2,1)S(1)}, bf16[1024,384]{1,0:T(8,128...) custom-call(bf16[512,1792]{1,0:T(8,128)(2,1)S(1)} %bitcast.36, ...), custom_call_target="tpu_custom_call" | custom-call | tf_op jit(solution)/shard_map/pallas_call | solution.py:599
  58.4 6.6 %shard_map.213 = (bf16[272,384]{1,0:T(8,128)(2,1)S(1)}, bf16[272,384]{1,0:T(8,128)(2,1)S(1)}, bf16[272,384]{1,0:T(8,128)(2,1)S(1)}, bf16[272,384]{1,0:T(8,128)(2...) custom-call(bf16[256,384]{1,0:T(8,128)(2,1)S(1)} %get-tuple-element.117.token_0.tokens_ref, ...), custom_call_target="tpu_custom_call" | custom-call | tf_op jit(solution)/shard_map/pallas_call | solution.py:599
  65.5 3.0 %collective-permute-start.16 = (bf16[272,384]{1,0:T(8,128)(2,1)S(1)}, bf16[272,384]{1,0:T(8,128)(2,1)S(1)}, u32[]{:S(2)}, u32[]{:S(2)}) collective-permute-start(bf16[272,384]{1,0:T(8,128)(2,1)S(1)} %get-tuple-element.91), channel_id=1, source_target_pairs={{0,3},{1,2},{2,1},{3,0},{4,7},{5,6},{6,5},{7,4},{8,11},{9,10},{10,... | collective-permute-start | bytes 626696 | tf_op jit(solution)/shard_map/ppermute | solution.py:577
  71.9 1.6 %collective-permute-done.15.piece_1 = bf16[272,384]{1,0:T(8,128)(2,1)S(1)} collective-permute-done((bf16[272,384]{1,0:T(8,128)(2,1)S(1)}, bf16[272,384]{1,0:T(8,128)(2,1)S(1)}, u32[]{:S(2)}, u32[]{:S(2)}) %collective-permute-start.15) | collective-permute-done | bytes 208928 | tf_op jit(solution)/shard_map/ppermute | solution.py:577
  73.5 4.2 %collective-permute-done.16.piece_2 = bf16[272,384]{1,0:T(8,128)(2,1)S(1)} collective-permute-done((bf16[272,384]{1,0:T(8,128)(2,1)S(1)}, bf16[272,384]{1,0:T(8,128)(2,1)S(1)}, u32[]{:S(2)}, u32[]{:S(2)}) %collective-permute-start.16) | collective-permute-done | bytes 208928 | tf_op jit(solution)/shard_map/ppermute | solution.py:577
  77.7 1.9 %collective-permute-done.17.piece_3 = bf16[272,384]{1,0:T(8,128)(2,1)S(1)} collective-permute-done((bf16[272,384]{1,0:T(8,128)(2,1)S(1)}, bf16[272,384]{1,0:T(8,128)(2,1)S(1)}, u32[]{:S(2)}, u32[]{:S(2)}) %collective-permute-start.17) | collective-permute-done | bytes 208928 | tf_op jit(solution)/shard_map/ppermute | solution.py:577
  79.6 9.5 %all-to-all-start = ((bf16[64,8,1792]{2,1,0:T(8,128)(2,1)}), bf16[64,8,1792]{2,1,0:T(8,128)(2,1)S(1)}, u32[]{:S(2)}, u32[]{:S(2)}) async-start(bf16[64,8,1792]{2,1,0:T(8,128)(2,1)} %bitcast.39), calls=%async_computation | async-start | bytes 3670016 | tf_op jit(solution)/shard_map/all_to_all | solution.py:706
  90.3 3.0 %collective-permute-start.18 = (bf16[272,384]{1,0:T(8,128)(2,1)S(1)}, bf16[272,384]{1,0:T(8,128)(2,1)S(1)}, u32[]{:S(2)}, u32[]{:S(2)}) collective-permute-start(bf16[272,384]{1,0:T(8,128)(2,1)S(1)} %get-tuple-element.99), channel_id=1, source_target_pairs={{0,4},{4,0},{1,5},{5,1},{2,6},{6,2},{3,7},{7,3},{8,12},{12,8},{9,1... | collective-permute-start | bytes 626696 | tf_op jit(solution)/shard_map/ppermute | solution.py:564
  93.4 22.4 %collective-permute-done.18.other_ref = bf16[272,384]{1,0:T(8,128)(2,1)S(1)} collective-permute-done((bf16[272,384]{1,0:T(8,128)(2,1)S(1)}, bf16[272,384]{1,0:T(8,128)(2,1)S(1)}, u32[]{:S(2)}, u32[]{:S(2)}) %collective-permute-start.18) | collective-permute-done | bytes 208928 | tf_op jit(solution)/shard_map/ppermute | solution.py:564
  115.8 2.1 %shard_map.215 = (bf16[2,128,384]{2,1,0:T(8,128)(2,1)}, bf16[2,128,384]{2,1,0:T(8,128)(2,1)}, f32[2,2304]{1,0:T(2,128)}, f32[3,1152]{1,0:T(4,128)}, f32[1,3]{1,0...) custom-call(bf16[128,384]{1,0:T(8,128)(2,1)S(1)} %get-tuple-element., ...), custom_call_target="tpu_custom_call" | custom-call | tf_op jit(solution)/shard_map/pallas_call | solution.py:599
  (41 shorter events, 12.6 us)
Async XLA Ops:
  2.2 5.0 %collective-permute-start = (bf16[8,1792]{1,0:T(8,128)(2,1)S(1)}, bf16[8,1792]{1,0:T(8,128)(2,1)S(1)}, u32[]{:S(2)}, u32[]{:S(2)}) collective-permute-start(bf16[8,1792]{1,0:T(8,128)(2,1)S(1)} %get-tuple-element.63), channel_id=1, source_target_pairs={{0,1},{1,0},{2,3},{3,2},{4,5},{5,4},{6,7},{7,6},{8,9},{9,8},{10,11... | collective-permute-start | bytes 86024 | tf_op jit(solution)/shard_map/ppermute | solution.py:577
  4.2 8.5 %collective-permute-start.2 = (bf16[2,128,384]{2,1,0:T(8,128)(2,1)S(1)}, bf16[2,128,384]{2,1,0:T(8,128)(2,1)S(1)}, u32[]{:S(2)}, u32[]{:S(2)}) collective-permute-start(bf16[2,128,384]{2,1,0:T(8,128)(2,1)S(1)} %get-tuple-element.64), channel_id=1, source_target_pairs={{0,4},{4,0},{1,5},{5,1},{2,6},{6,2},{3,7},{7,3},{8,12},{12,8},{9,1... | collective-permute-start | bytes 589832 | tf_op jit(solution)/shard_map/ppermute | solution.py:564
  7.2 5.5 %collective-permute-start.1 = (bf16[2,8,1792]{2,1,0:T(8,128)(2,1)S(1)}, bf16[2,8,1792]{2,1,0:T(8,128)(2,1)S(1)}, u32[]{:S(2)}, u32[]{:S(2)}) collective-permute-start(bf16[2,8,1792]{2,1,0:T(8,128)(2,1)S(1)} %get-tuple-element.119), channel_id=1, source_target_pairs={{0,3},{1,2},{2,1},{3,0},{4,7},{5,6},{6,5},{7,4},{8,11},{9,10},{10,... | collective-permute-start | bytes 172040 | tf_op jit(solution)/shard_map/ppermute | solution.py:577
  12.7 6.0 %collective-permute-start.5 = (bf16[4,8,1792]{2,1,0:T(8,128)(2,1)S(1)}, bf16[4,8,1792]{2,1,0:T(8,128)(2,1)S(1)}, u32[]{:S(2)}, u32[]{:S(2)}) collective-permute-start(bf16[4,8,1792]{2,1,0:T(8,128)(2,1)S(1)} %bitcast.42), channel_id=1, source_target_pairs={{0,16},{16,32},{32,48},{48,0},{1,17},{17,33},{33,49},{49,1},{2,18}... | collective-permute-start | bytes 344072 | tf_op jit(solution)/shard_map/ppermute | solution.py:564
  14.4 6.4 %collective-permute-start.4 = (bf16[4,8,1792]{2,1,0:T(8,128)(2,1)S(1)}, bf16[4,8,1792]{2,1,0:T(8,128)(2,1)S(1)}, u32[]{:S(2)}, u32[]{:S(2)}) collective-permute-start(bf16[4,8,1792]{2,1,0:T(8,128)(2,1)S(1)} %bitcast.43), channel_id=1, source_target_pairs={{0,32},{16,48},{32,0},{48,16},{1,33},{17,49},{33,1},{49,17},{2,34}... | collective-permute-start | bytes 344072 | tf_op jit(solution)/shard_map/ppermute | solution.py:564
  15.3 6.0 %collective-permute-start.3 = (bf16[4,8,1792]{2,1,0:T(8,128)(2,1)S(1)}, bf16[4,8,1792]{2,1,0:T(8,128)(2,1)S(1)}, u32[]{:S(2)}, u32[]{:S(2)}) collective-permute-start(bf16[4,8,1792]{2,1,0:T(8,128)(2,1)S(1)} %bitcast.44), channel_id=1, source_target_pairs={{0,48},{16,0},{32,16},{48,32},{1,49},{17,1},{33,17},{49,33},{2,50}... | collective-permute-start | bytes 344072 | tf_op jit(solution)/shard_map/ppermute | solution.py:564
  17.8 6.9 %collective-permute-start.8 = (bf16[256,384]{1,0:T(8,128)(2,1)S(1)}, bf16[256,384]{1,0:T(8,128)(2,1)S(1)}, u32[]{:S(2)}, u32[]{:S(2)}) collective-permute-start(bf16[256,384]{1,0:T(8,128)(2,1)S(1)} %get-tuple-element.117.token_0.tokens_ref), channel_id=1, source_target_pairs={{0,1},{1,0},{2,3},{3,2},{4,5},{5,4},{6,7},{7,6},{8,9},{9,8},{10,11... | collective-permute-start | bytes 589832 | tf_op jit(solution)/shard_map/ppermute | solution.py:577
  21.4 10.9 %collective-permute-start.6 = (bf16[4,4,8,1792]{3,2,1,0:T(8,128)(2,1)S(1)}, bf16[4,4,8,1792]{3,2,1,0:T(8,128)(2,1)S(1)}, u32[]{:S(2)}, u32[]{:S(2)}) collective-permute-start(bf16[4,4,8,1792]{3,2,1,0:T(8,128)(2,1)S(1)} %get-tuple-element.115), channel_id=1, source_target_pairs={{0,64},{4,68},{64,4},{68,0},{1,65},{5,69},{65,5},{69,1},{2,66},{6,... | collective-permute-start | bytes 1376264 | tf_op jit(solution)/shard_map/ppermute | solution.py:573
  22.7 9.6 %collective-permute-start.7 = (bf16[4,4,8,1792]{3,2,1,0:T(8,128)(2,1)S(1)}, bf16[4,4,8,1792]{3,2,1,0:T(8,128)(2,1)S(1)}, u32[]{:S(2)}, u32[]{:S(2)}) collective-permute-start(bf16[4,4,8,1792]{3,2,1,0:T(8,128)(2,1)S(1)} %get-tuple-element.115), channel_id=1, source_target_pairs={{0,68},{4,64},{64,0},{68,4},{1,69},{5,65},{65,1},{69,5},{2,70},{6,... | collective-permute-start | bytes 1376264 | tf_op jit(solution)/shard_map/ppermute | solution.py:573
  24.8 9.1 %collective-permute-start.9 = (bf16[2,256,384]{2,1,0:T(8,128)(2,1)S(1)}, bf16[2,256,384]{2,1,0:T(8,128)(2,1)S(1)}, u32[]{:S(2)}, u32[]{:S(2)}) collective-permute-start(bf16[2,256,384]{2,1,0:T(8,128)(2,1)S(1)} %pad_maximum_fusion.3), channel_id=1, source_target_pairs={{0,3},{1,2},{2,1},{3,0},{4,7},{5,6},{6,5},{7,4},{8,11},{9,10},{10,... | collective-permute-start | bytes 1179656 | tf_op jit(solution)/shard_map/ppermute | solution.py:577
  33.9 7.3 %collective-permute-start.10 = (bf16[2,4,8,1792]{3,2,1,0:T(8,128)(2,1)S(1)}, bf16[2,4,8,1792]{3,2,1,0:T(8,128)(2,1)S(1)}, u32[]{:S(2)}, u32[]{:S(2)}) collective-permute-start(bf16[2,4,8,1792]{3,2,1,0:T(8,128)(2,1)S(1)} %slice.18), channel_id=1, source_target_pairs={{0,64},{4,68},{64,4},{68,0},{1,65},{5,69},{65,5},{69,1},{2,66},{6,... | collective-permute-start | bytes 688136 | tf_op jit(solution)/shard_map/ppermute | solution.py:573
  34.0 7.2 %collective-permute-start.11 = (bf16[2,4,8,1792]{3,2,1,0:T(8,128)(2,1)S(1)}, bf16[2,4,8,1792]{3,2,1,0:T(8,128)(2,1)S(1)}, u32[]{:S(2)}, u32[]{:S(2)}) collective-permute-start(bf16[2,4,8,1792]{3,2,1,0:T(8,128)(2,1)S(1)} %slice.19), channel_id=1, source_target_pairs={{0,68},{4,64},{64,0},{68,4},{1,69},{5,65},{65,1},{69,5},{2,70},{6,... | collective-permute-start | bytes 688136 | tf_op jit(solution)/shard_map/ppermute | solution.py:573
  41.2 4.3 %copy-start = (bf16[2,128,384]{2,1,0:T(8,128)(2,1)S(1)}, bf16[2,128,384]{2,1,0:T(8,128)(2,1)}, u32[]{:S(2)}) copy-start(bf16[2,128,384]{2,1,0:T(8,128)(2,1)} %cotangent_ref.3) | copy-start | bytes 589828
  41.5 4.0 %collective-permute-start.12 = (bf16[512,1792]{1,0:T(8,128)(2,1)S(1)}, bf16[512,1792]{1,0:T(8,128)(2,1)S(1)}, u32[]{:S(2)}, u32[]{:S(2)}) collective-permute-start(bf16[512,1792]{1,0:T(8,128)(2,1)S(1)} %bitcast.35), channel_id=1, source_target_pairs={{0,8},{8,0},{1,9},{9,1},{2,10},{10,2},{3,11},{11,3},{4,12},{12,4},... | collective-permute-start | bytes 5505032 | tf_op jit(solution)/shard_map/ppermute | solution.py:564
  57.9 7.1 %copy-start.1 = (bf16[128,384]{1,0:T(8,128)(2,1)}, bf16[128,384]{1,0:T(8,128)(2,1)S(1)}, u32[]{:S(2)}) copy-start(bf16[128,384]{1,0:T(8,128)(2,1)S(1)} %get-tuple-element.97.output_ref) | copy-start | bytes 294916
  57.9 12.2 %collective-permute-start.14 = (bf16[512,1024]{1,0:T(8,128)(2,1)S(1)}, bf16[512,1024]{1,0:T(8,128)(2,1)S(1)}, u32[]{:S(2)}, u32[]{:S(2)}) collective-permute-start(bf16[512,1024]{1,0:T(8,128)(2,1)S(1)} %get-tuple-element.88), channel_id=1, source_target_pairs={{0,8},{8,0},{1,9},{9,1},{2,10},{10,2},{3,11},{11,3},{4,12},{12,4},... | collective-permute-start | bytes 3145736 | tf_op jit(solution)/shard_map/ppermute | solution.py:564
  65.0 4.9 %collective-permute-start.13 = (bf16[512,768]{1,0:T(8,128)(2,1)S(1)}, bf16[512,768]{1,0:T(8,128)(2,1)S(1)}, u32[]{:S(2)}, u32[]{:S(2)}) collective-permute-start(bf16[512,768]{1,0:T(8,128)(2,1)S(1)} %get-tuple-element.86), channel_id=1, source_target_pairs={{0,8},{8,0},{1,9},{9,1},{2,10},{10,2},{3,11},{11,3},{4,12},{12,4},... | collective-permute-start | bytes 2359304 | tf_op jit(solution)/shard_map/ppermute | solution.py:564
  65.5 8.0 %collective-permute-start.15 = (bf16[272,384]{1,0:T(8,128)(2,1)S(1)}, bf16[272,384]{1,0:T(8,128)(2,1)S(1)}, u32[]{:S(2)}, u32[]{:S(2)}) collective-permute-start(bf16[272,384]{1,0:T(8,128)(2,1)S(1)} %get-tuple-element.90), channel_id=1, source_target_pairs={{0,1},{1,0},{2,3},{3,2},{4,5},{5,4},{6,7},{7,6},{8,9},{9,8},{10,11... | collective-permute-start | bytes 626696 | tf_op jit(solution)/shard_map/ppermute | solution.py:577
  65.5 12.2 %collective-permute-start.16 = (bf16[272,384]{1,0:T(8,128)(2,1)S(1)}, bf16[272,384]{1,0:T(8,128)(2,1)S(1)}, u32[]{:S(2)}, u32[]{:S(2)}) collective-permute-start(bf16[272,384]{1,0:T(8,128)(2,1)S(1)} %get-tuple-element.91), channel_id=1, source_target_pairs={{0,3},{1,2},{2,1},{3,0},{4,7},{5,6},{6,5},{7,4},{8,11},{9,10},{10,... | collective-permute-start | bytes 626696 | tf_op jit(solution)/shard_map/ppermute | solution.py:577
  68.5 11.1 %collective-permute-start.17 = (bf16[272,384]{1,0:T(8,128)(2,1)S(1)}, bf16[272,384]{1,0:T(8,128)(2,1)S(1)}, u32[]{:S(2)}, u32[]{:S(2)}) collective-permute-start(bf16[272,384]{1,0:T(8,128)(2,1)S(1)} %get-tuple-element.92), channel_id=1, source_target_pairs={{0,2},{1,3},{2,0},{3,1},{4,6},{5,7},{6,4},{7,5},{8,10},{9,11},{10,... | collective-permute-start | bytes 626696 | tf_op jit(solution)/shard_map/ppermute | solution.py:577
  79.6 36.2 %all-to-all-start = ((bf16[64,8,1792]{2,1,0:T(8,128)(2,1)}), bf16[64,8,1792]{2,1,0:T(8,128)(2,1)S(1)}, u32[]{:S(2)}, u32[]{:S(2)}) async-start(bf16[64,8,1792]{2,1,0:T(8,128)(2,1)} %bitcast.39), calls=%async_computation | async-start | bytes 3670016 | tf_op jit(solution)/shard_map/all_to_all | solution.py:706
  89.1 0.9 copy-start.2
  90.3 25.5 %collective-permute-start.18 = (bf16[272,384]{1,0:T(8,128)(2,1)S(1)}, bf16[272,384]{1,0:T(8,128)(2,1)S(1)}, u32[]{:S(2)}, u32[]{:S(2)}) collective-permute-start(bf16[272,384]{1,0:T(8,128)(2,1)S(1)} %get-tuple-element.99), channel_id=1, source_target_pairs={{0,4},{4,0},{1,5},{5,1},{2,6},{6,2},{3,7},{7,3},{8,12},{12,8},{9,1... | collective-permute-start | bytes 626696 | tf_op jit(solution)/shard_map/ppermute | solution.py:564

commit v5 on v4

--- a/solution.py
+++ b/solution.py
@@ -112,6 +112,7 @@
     cut = cut_of(more, width)
     row = iota((256, 1), 0)
     q = row & 7
+    here = 2 * ids[3] + ids[0]
     core = (ids[2] + (row >> 7)) & 1
     base = (((row >> 6) & 1) * 2 + core) * 24 + ((row >> 3) & 7) * 3
     pair = pick(
@@ -128,12 +129,17 @@
         left = (both[:, :more] + dot(ends, third[rows, :])).astype(BF)
         right = (both[:, more : more + cut] + dot(last, jnp.concatenate(thirds, axis=0))).astype(BF)
         for side, target in enumerate(targets):
-            area = slice(band * 128, band * 128 + 128)
-            own = slice(side * 128, side * 128 + 128)
-            target[area, :more] = left[own]
-            target[area, more : more + cut] = right[own]
-            if more + cut < width:
-                target[area, more + cut :] = both[own, more + cut :].astype(BF)
+            for low in range(2):
+                for upper in range(2):
+                    x = (2 * upper + (band >> 1) - here) & 3
+                    first = x * 128 + (2 * (band & 1) + low) * 32
+                    area = pl.ds(pl.multiple_of(first, 32), 32)
+                    run = side * 128 + low * 64 + upper * 32
+                    own = slice(run, run + 32)
+                    target[area, :more] = left[own]
+                    target[area, more : more + cut] = right[own]
+                    if more + cut < width:
+                        target[area, more + cut :] = both[own, more + cut :].astype(BF)
 
 
 def interleave():
@@ -498,6 +504,37 @@
     sums_ref[...] = sums
 
 
+def mix_kernel(
+    keep_one, back_one, keep_two, back_two,
+    own_ref, right_ref, left_ref, up_ref, down_ref,
+):
+    def put(ref, first, count):
+        rows = slice(first, first + count)
+        ref[:, :FIRST] = (keep_one[rows, :].astype(F32) + back_one[rows, :].astype(F32)).astype(BF)
+        ref[:, FIRST:] = (keep_two[rows, :].astype(F32) + back_two[rows, :].astype(F32)).astype(BF)
+
+    put(own_ref, 0, 128)
+    put(right_ref, 128, 128)
+    put(up_ref, 256, 64)
+    put(down_ref, 320, 64)
+    put(left_ref, 384, 128)
+
+
+def fold_kernel(right_ref, left_ref, up_ref, down_ref, right_out, left_out):
+    half = up_ref.shape[0]
+    right_out[:half, :] = (right_ref[:half, :].astype(F32) + up_ref[...].astype(F32)).astype(BF)
+    right_out[half:, :] = right_ref[half:, :]
+    left_out[:half, :] = left_ref[:half, :]
+    left_out[half:, :] = (left_ref[half:, :].astype(F32) + down_ref[...].astype(F32)).astype(BF)
+
+
+def add_kernel(own_ref, left_ref, right_ref, out_ref):
+    for index in range(out_ref.shape[0]):
+        rows = slice(index * 8, index * 8 + 8)
+        total = own_ref[rows, :].astype(F32) + left_ref[rows, :].astype(F32)
+        out_ref[index] = (total + right_ref[rows, :].astype(F32)).astype(BF)
+
+
 def last_rows(block, more):
     cut = cut_of(more, block.shape[1])
     third = jnp.concatenate([block[6:7, more : more + cut], block[7:8, more : 2 * more - cut]], axis=1)
@@ -695,15 +732,26 @@
     )
     arrived = (piece_0, trade(piece_1, 1), trade(piece_2, 3), trade(piece_3, 2))
     other_one = shift(send_one, "core", 1, 2)
-    mixed = jnp.concatenate([keep_one + other_one, keep_two + other_two], axis=1)
-    mixed, arrived = lax.optimization_barrier((mixed, arrived))
+    own_sum, right, left, up, down = call(
+        mix_kernel,
+        (vmem(128, WIDE), vmem(128, WIDE), vmem(128, WIDE), vmem(64, WIDE), vmem(64, WIDE)),
+        [],
+        hold(keep_one, other_one, keep_two, other_two),
+    )
+    up, down = shift_x(up, 1), shift_x(down, -1)
+    right, left = call(
+        fold_kernel, (vmem(128, WIDE), vmem(128, WIDE)), [], hold(right, left, up, down)
+    )
+    from_left, from_right = shift_x(right, 1), shift_x(left, -1)
+    from_left, from_right, arrived = lax.optimization_barrier((from_left, from_right, arrived))
+    (shares,) = call(add_kernel, (sds(16, 8, WIDE),), [], hold(own_sum, from_left, from_right))
+    pieces = lax.all_to_all(shares, ("y", "z"), 0, 0, tiled=True)
     grad_a, grad_b, sums = call(
         final_kernel,
         (vmem(side, D), vmem(2 * side + 16, D), vmem(8, D, dtype=F32)),
         [],
         hold(tokens, condition, middle_grad, *arrived, output_b),
     )
-    pieces = lax.all_to_all(mixed.reshape(64, 8, WIDE), CHIPS, 0, 0, tiled=True)
     grad_back = shift(grad_b, "xh", 1, 2)
     (
         output, input_grad, modulation_grad,

time: 119 us -> 113 us (0.950)
  waiting for transfers between devices: 48.5 us -> 41.1 us
  other arithmetic: 3.38 us -> 1.41 us
  starting transfers between devices: 41.2 us -> 43 us
  Pallas kernels: 23.1 us -> 24.5 us
    ppermute x8, waiting for transfers between devices: 29.4 us -> 14.8 us  [shift(): lax.ppermute(array, axis, [(i, (i + step) % size) for i in range(size)])]
    ppermute x4 -> x8, starting transfers between devices: 6.61 us -> 13.3 us  [shift_x(): return lax.ppermute(array, X, moves)]
    ppermute x4 -> x8, waiting for transfers between devices: 8.46 us -> 14.5 us  [shift_x(): return lax.ppermute(array, X, moves)]
    all_to_all x1, starting transfers between devices: 9.5 us -> 6.23 us  [body(): pieces = lax.all_to_all(shares, ('y', 'z'), 0, 0, tiled=True)]
    ppermute x8, starting transfers between devices: 12.2 us -> 10.6 us  [shift(): lax.ppermute(array, axis, [(i, (i + step) % size) for i in range(size)])]
    pallas_call x5 -> x8, Pallas kernels: 23.1 us -> 24.5 us  [call(): pl.pallas_call(kernel, out_shape=out_shape, in_specs=[pl.BlockSpec(memory...]
    concatenate x1 -> x0, other arithmetic: 1.38 us -> none  [body(): jnp.concatenate([keep_one + other_one, keep_two + other_two], axis=1)]
  transfers between devices with their start and end apart: 20 -> 24, of which waited for: 12 -> 14; matrix products, arithmetic and copies ran while one was open for 3% -> 1% of each run, Pallas kernels for 6% -> 6%
where the time goes in v5:
time: 113 us; the launch traced here: 111 us
  starting transfers between devices  43 us (38%)
  waiting for transfers between devices  41.1 us (36%)
  Pallas kernels  24.5 us (22%)
  other arithmetic  1.41 us (1%)
    pallas_call x8, Pallas kernels, call(): pl.pallas_call(kernel, out_shape=out_shape, in_specs=[pl.BlockSpec(memory...  24.5 us
    ppermute x8, waiting for transfers between devices, shift(): lax.ppermute(array, axis, [(i, (i + step) % size) for i in range(size)])  14.8 us
    ppermute x8, waiting for transfers between devices, shift_x(): return lax.ppermute(array, X, moves)  14.5 us
    ppermute x8, starting transfers between devices, shift_x(): return lax.ppermute(array, X, moves)  13.3 us
    ppermute x7, starting transfers between devices, trade(): return lax.ppermute(array, 'z', [(i, i ^ bits) for i in range(4)])  12.9 us
    ppermute x7, waiting for transfers between devices, trade(): return lax.ppermute(array, 'z', [(i, i ^ bits) for i in range(4)])  11.8 us
    ppermute x8, starting transfers between devices, shift(): lax.ppermute(array, axis, [(i, (i + step) % size) for i in range(size)])  10.6 us
    all_to_all x1, starting transfers between devices, body(): pieces = lax.all_to_all(shares, ('y', 'z'), 0, 0, tiled=True)  6.23 us
  transfers between devices with their start and end apart: 24, of which 14 were waited for; matrix products, arithmetic and copies ran while one was open for 1% of the time, Pallas kernels for 6%

profile of v5, /device:TPU:8, one launch (start us, length us, event | category | flops | bytes accessed | tf_op | source)
XLA Modules:
  0.0 111.1 jit_solution(8597573508461415310)
XLA Ops:
  2.2 2.0 %collective-permute-start = (bf16[8,1792]{1,0:T(8,128)(2,1)S(1)}, bf16[8,1792]{1,0:T(8,128)(2,1)S(1)}, u32[]{:S(2)}, u32[]{:S(2)}) collective-permute-start(bf16[8,1792]{1,0:T(8,128)(2,1)S(1)} %get-tuple-element.71), channel_id=1, source_target_pairs={{0,1},{1,0},{2,3},{3,2},{4,5},{5,4},{6,7},{7,6},{8,9},{9,8},{10,11... | collective-permute-start | bytes 86024 | tf_op jit(solution)/shard_map/ppermute | solution.py:614
  4.2 3.0 %collective-permute-start.2 = (bf16[2,128,384]{2,1,0:T(8,128)(2,1)S(1)}, bf16[2,128,384]{2,1,0:T(8,128)(2,1)S(1)}, u32[]{:S(2)}, u32[]{:S(2)}) collective-permute-start(bf16[2,128,384]{2,1,0:T(8,128)(2,1)S(1)} %get-tuple-element.72), channel_id=1, source_target_pairs={{0,4},{4,0},{1,5},{5,1},{2,6},{6,2},{3,7},{7,3},{8,12},{12,8},{9,1... | collective-permute-start | bytes 589832 | tf_op jit(solution)/shard_map/ppermute | solution.py:601
  7.2 3.0 %collective-permute-start.1 = (bf16[2,8,1792]{2,1,0:T(8,128)(2,1)S(1)}, bf16[2,8,1792]{2,1,0:T(8,128)(2,1)S(1)}, u32[]{:S(2)}, u32[]{:S(2)}) collective-permute-start(bf16[2,8,1792]{2,1,0:T(8,128)(2,1)S(1)} %get-tuple-element.135), channel_id=1, source_target_pairs={{0,3},{1,2},{2,1},{3,0},{4,7},{5,6},{6,5},{7,4},{8,11},{9,10},{10,... | collective-permute-start | bytes 172040 | tf_op jit(solution)/shard_map/ppermute | solution.py:614
  15.3 2.4 %collective-permute-start.3 = (bf16[4,8,1792]{2,1,0:T(8,128)(2,1)S(1)}, bf16[4,8,1792]{2,1,0:T(8,128)(2,1)S(1)}, u32[]{:S(2)}, u32[]{:S(2)}) collective-permute-start(bf16[4,8,1792]{2,1,0:T(8,128)(2,1)S(1)} %bitcast.42), channel_id=1, source_target_pairs={{0,48},{16,0},{32,16},{48,32},{1,49},{17,1},{33,17},{49,33},{2,50}... | collective-permute-start | bytes 344072 | tf_op jit(solution)/shard_map/ppermute | solution.py:601
  18.8 2.0 %collective-permute-done.4 = bf16[4,8,1792]{2,1,0:T(8,128)(2,1)S(1)} collective-permute-done((bf16[4,8,1792]{2,1,0:T(8,128)(2,1)S(1)}, bf16[4,8,1792]{2,1,0:T(8,128)(2,1)S(1)}, u32[]{:S(2)}, u32[]{:S(2)}) %collective-permute-start.4) | collective-permute-done | bytes 114720 | tf_op jit(solution)/shard_map/ppermute | solution.py:601
  22.7 2.0 %collective-permute-start.7 = (bf16[4,4,8,1792]{3,2,1,0:T(8,128)(2,1)S(1)}, bf16[4,4,8,1792]{3,2,1,0:T(8,128)(2,1)S(1)}, u32[]{:S(2)}, u32[]{:S(2)}) collective-permute-start(bf16[4,4,8,1792]{3,2,1,0:T(8,128)(2,1)S(1)} %get-tuple-element.131), channel_id=1, source_target_pairs={{0,68},{4,64},{64,0},{68,4},{1,69},{5,65},{65,1},{69,5},{2,70},{6,... | collective-permute-start | bytes 1376264 | tf_op jit(solution)/shard_map/ppermute | solution.py:610
  24.8 3.0 %collective-permute-start.9 = (bf16[2,256,384]{2,1,0:T(8,128)(2,1)S(1)}, bf16[2,256,384]{2,1,0:T(8,128)(2,1)S(1)}, u32[]{:S(2)}, u32[]{:S(2)}) collective-permute-start(bf16[2,256,384]{2,1,0:T(8,128)(2,1)S(1)} %pad_maximum_fusion.2), channel_id=1, source_target_pairs={{0,3},{1,2},{2,1},{3,0},{4,7},{5,6},{6,5},{7,4},{8,11},{9,10},{10,... | collective-permute-start | bytes 1179656 | tf_op jit(solution)/shard_map/ppermute | solution.py:614
  27.8 4.5 %collective-permute-done.6 = bf16[4,4,8,1792]{3,2,1,0:T(8,128)(2,1)S(1)} collective-permute-done((bf16[4,4,8,1792]{3,2,1,0:T(8,128)(2,1)S(1)}, bf16[4,4,8,1792]{3,2,1,0:T(8,128)(2,1)S(1)}, u32[]{:S(2)}, u32[]{:S(2)}) %collective-permute-start.6) | collective-permute-done | bytes 458784 | tf_op jit(solution)/shard_map/ppermute | solution.py:610
  34.0 3.2 %collective-permute-start.11 = (bf16[2,4,8,1792]{3,2,1,0:T(8,128)(2,1)S(1)}, bf16[2,4,8,1792]{3,2,1,0:T(8,128)(2,1)S(1)}, u32[]{:S(2)}, u32[]{:S(2)}) collective-permute-start(bf16[2,4,8,1792]{3,2,1,0:T(8,128)(2,1)S(1)} %slice.19), channel_id=1, source_target_pairs={{0,68},{4,64},{64,0},{68,4},{1,69},{5,65},{65,1},{69,5},{2,70},{6,... | collective-permute-start | bytes 688136 | tf_op jit(solution)/shard_map/ppermute | solution.py:610
  37.2 4.0 %collective-permute-done.10 = bf16[2,4,8,1792]{3,2,1,0:T(8,128)(2,1)S(1)} collective-permute-done((bf16[2,4,8,1792]{3,2,1,0:T(8,128)(2,1)S(1)}, bf16[2,4,8,1792]{3,2,1,0:T(8,128)(2,1)S(1)}, u32[]{:S(2)}, u32[]{:S(2)}) %collective-permute-start.10) | collective-permute-done | bytes 229408 | tf_op jit(solution)/shard_map/ppermute | solution.py:610
  41.8 3.8 %collective-permute-done.12.far_ref = bf16[512,1792]{1,0:T(8,128)(2,1)S(1)} collective-permute-done((bf16[512,1792]{1,0:T(8,128)(2,1)S(1)}, bf16[512,1792]{1,0:T(8,128)(2,1)S(1)}, u32[]{:S(2)}, u32[]{:S(2)}) %collective-permute-start.12) | collective-permute-done | bytes 1835040 | tf_op jit(solution)/shard_map/ppermute | solution.py:601
  45.5 12.4 %shard_map.212 = (bf16[384,1152]{1,0:T(8,128)(2,1)S(1)}, bf16[1024,384]{1,0:T(8,128)(2,1)S(1)}, bf16[256,384]{1,0:T(8,128)(2,1)S(1)}, bf16[1024,384]{1,0:T(8,128...) custom-call(bf16[512,1792]{1,0:T(8,128)(2,1)S(1)} %bitcast.35, ...), custom_call_target="tpu_custom_call" | custom-call | tf_op jit(solution)/shard_map/pallas_call | solution.py:636
  58.4 6.6 %shard_map.213 = (bf16[272,384]{1,0:T(8,128)(2,1)S(1)}, bf16[272,384]{1,0:T(8,128)(2,1)S(1)}, bf16[272,384]{1,0:T(8,128)(2,1)S(1)}, bf16[272,384]{1,0:T(8,128)(2...) custom-call(bf16[256,384]{1,0:T(8,128)(2,1)S(1)} %get-tuple-element.133.token_0.tokens_ref, ...), custom_call_target="tpu_custom_call" | custom-call | tf_op jit(solution)/shard_map/pallas_call | solution.py:636
  65.5 1.9 %collective-permute-done.13.back_one = bf16[512,768]{1,0:T(8,128)(2,1)S(1)} collective-permute-done((bf16[512,768]{1,0:T(8,128)(2,1)S(1)}, bf16[512,768]{1,0:T(8,128)(2,1)S(1)}, u32[]{:S(2)}, u32[]{:S(2)}) %collective-permute-start.13) | collective-permute-done | bytes 786464 | tf_op jit(solution)/shard_map/ppermute | solution.py:601
  68.2 3.0 %collective-permute-start.16 = (bf16[64,1792]{1,0:T(8,128)(2,1)S(1)}, bf16[64,1792]{1,0:T(8,128)(2,1)S(1)}, u32[]{:S(2)}, u32[]{:S(2)}) collective-permute-start(bf16[64,1792]{1,0:T(8,128)(2,1)S(1)} %get-tuple-element.100), channel_id=1, source_target_pairs={{0,68},{4,64},{64,0},{68,4},{1,69},{5,65},{65,1},{69,5},{2,70},{6,... | collective-permute-start | bytes 688136 | tf_op jit(solution)/shard_map/ppermute | solution.py:610
  71.2 6.0 %collective-permute-done.15.up_ref = bf16[64,1792]{1,0:T(8,128)(2,1)S(1)} collective-permute-done((bf16[64,1792]{1,0:T(8,128)(2,1)S(1)}, bf16[64,1792]{1,0:T(8,128)(2,1)S(1)}, u32[]{:S(2)}, u32[]{:S(2)}) %collective-permute-start.15) | collective-permute-done | bytes 229408 | tf_op jit(solution)/shard_map/ppermute | solution.py:610
  78.6 2.1 %collective-permute-start.18 = (bf16[128,1792]{1,0:T(8,128)(2,1)S(1)}, bf16[128,1792]{1,0:T(8,128)(2,1)S(1)}, u32[]{:S(2)}, u32[]{:S(2)}) collective-permute-start(bf16[128,1792]{1,0:T(8,128)(2,1)S(1)} %get-tuple-element.102), channel_id=1, source_target_pairs={{0,68},{4,64},{64,0},{68,4},{1,69},{5,65},{65,1},{69,5},{2,70},{6,... | collective-permute-start | bytes 1376264 | tf_op jit(solution)/shard_map/ppermute | solution.py:610
  80.7 3.0 %collective-permute-start.20 = (bf16[272,384]{1,0:T(8,128)(2,1)S(1)}, bf16[272,384]{1,0:T(8,128)(2,1)S(1)}, u32[]{:S(2)}, u32[]{:S(2)}) collective-permute-start(bf16[272,384]{1,0:T(8,128)(2,1)S(1)} %get-tuple-element.105), channel_id=1, source_target_pairs={{0,3},{1,2},{2,1},{3,0},{4,7},{5,6},{6,5},{7,4},{8,11},{9,10},{10,... | collective-permute-start | bytes 626696 | tf_op jit(solution)/shard_map/ppermute | solution.py:614
  85.2 3.7 %collective-permute-done.19.piece_1 = bf16[272,384]{1,0:T(8,128)(2,1)S(1)} collective-permute-done((bf16[272,384]{1,0:T(8,128)(2,1)S(1)}, bf16[272,384]{1,0:T(8,128)(2,1)S(1)}, u32[]{:S(2)}, u32[]{:S(2)}) %collective-permute-start.19) | collective-permute-done | bytes 208928 | tf_op jit(solution)/shard_map/ppermute | solution.py:614
  88.8 3.2 %collective-permute-done.20.piece_2 = bf16[272,384]{1,0:T(8,128)(2,1)S(1)} collective-permute-done((bf16[272,384]{1,0:T(8,128)(2,1)S(1)}, bf16[272,384]{1,0:T(8,128)(2,1)S(1)}, u32[]{:S(2)}, u32[]{:S(2)}) %collective-permute-start.20) | collective-permute-done | bytes 208928 | tf_op jit(solution)/shard_map/ppermute | solution.py:614
  92.0 1.9 %collective-permute-done.21.piece_3 = bf16[272,384]{1,0:T(8,128)(2,1)S(1)} collective-permute-done((bf16[272,384]{1,0:T(8,128)(2,1)S(1)}, bf16[272,384]{1,0:T(8,128)(2,1)S(1)}, u32[]{:S(2)}, u32[]{:S(2)}) %collective-permute-start.21) | collective-permute-done | bytes 208928 | tf_op jit(solution)/shard_map/ppermute | solution.py:614
  94.9 6.2 %all-to-all-start = ((bf16[16,8,1792]{2,1,0:T(8,128)(2,1)}), bf16[16,8,1792]{2,1,0:T(8,128)(2,1)S(1)}, u32[]{:S(2)}, u32[]{:S(2)}) async-start(bf16[16,8,1792]{2,1,0:T(8,128)(2,1)} %shard_map.217), calls=%async_computation | async-start | bytes 917504 | tf_op jit(solution)/shard_map/all_to_all | solution.py:748
  102.8 6.0 %collective-permute-done.22.other_ref = bf16[272,384]{1,0:T(8,128)(2,1)S(1)} collective-permute-done((bf16[272,384]{1,0:T(8,128)(2,1)S(1)}, bf16[272,384]{1,0:T(8,128)(2,1)S(1)}, u32[]{:S(2)}, u32[]{:S(2)}) %collective-permute-start.22) | collective-permute-done | bytes 208928 | tf_op jit(solution)/shard_map/ppermute | solution.py:601
  108.8 2.1 %shard_map.218 = (bf16[2,128,384]{2,1,0:T(8,128)(2,1)}, bf16[2,128,384]{2,1,0:T(8,128)(2,1)}, f32[2,2304]{1,0:T(2,128)}, f32[3,1152]{1,0:T(4,128)}, f32[1,3]{1,0...) custom-call(bf16[128,384]{1,0:T(8,128)(2,1)S(1)} %get-tuple-element., ...), custom_call_target="tpu_custom_call" | custom-call | tf_op jit(solution)/shard_map/pallas_call | solution.py:636
  (45 shorter events, 19.0 us)
Async XLA Ops:
  2.2 5.0 %collective-permute-start = (bf16[8,1792]{1,0:T(8,128)(2,1)S(1)}, bf16[8,1792]{1,0:T(8,128)(2,1)S(1)}, u32[]{:S(2)}, u32[]{:S(2)}) collective-permute-start(bf16[8,1792]{1,0:T(8,128)(2,1)S(1)} %get-tuple-element.71), channel_id=1, source_target_pairs={{0,1},{1,0},{2,3},{3,2},{4,5},{5,4},{6,7},{7,6},{8,9},{9,8},{10,11... | collective-permute-start | bytes 86024 | tf_op jit(solution)/shard_map/ppermute | solution.py:614
  4.2 8.5 %collective-permute-start.2 = (bf16[2,128,384]{2,1,0:T(8,128)(2,1)S(1)}, bf16[2,128,384]{2,1,0:T(8,128)(2,1)S(1)}, u32[]{:S(2)}, u32[]{:S(2)}) collective-permute-start(bf16[2,128,384]{2,1,0:T(8,128)(2,1)S(1)} %get-tuple-element.72), channel_id=1, source_target_pairs={{0,4},{4,0},{1,5},{5,1},{2,6},{6,2},{3,7},{7,3},{8,12},{12,8},{9,1... | collective-permute-start | bytes 589832 | tf_op jit(solution)/shard_map/ppermute | solution.py:601
  7.2 5.5 %collective-permute-start.1 = (bf16[2,8,1792]{2,1,0:T(8,128)(2,1)S(1)}, bf16[2,8,1792]{2,1,0:T(8,128)(2,1)S(1)}, u32[]{:S(2)}, u32[]{:S(2)}) collective-permute-start(bf16[2,8,1792]{2,1,0:T(8,128)(2,1)S(1)} %get-tuple-element.135), channel_id=1, source_target_pairs={{0,3},{1,2},{2,1},{3,0},{4,7},{5,6},{6,5},{7,4},{8,11},{9,10},{10,... | collective-permute-start | bytes 172040 | tf_op jit(solution)/shard_map/ppermute | solution.py:614
  12.7 6.0 %collective-permute-start.5 = (bf16[4,8,1792]{2,1,0:T(8,128)(2,1)S(1)}, bf16[4,8,1792]{2,1,0:T(8,128)(2,1)S(1)}, u32[]{:S(2)}, u32[]{:S(2)}) collective-permute-start(bf16[4,8,1792]{2,1,0:T(8,128)(2,1)S(1)} %bitcast.40), channel_id=1, source_target_pairs={{0,16},{16,32},{32,48},{48,0},{1,17},{17,33},{33,49},{49,1},{2,18}... | collective-permute-start | bytes 344072 | tf_op jit(solution)/shard_map/ppermute | solution.py:601
  14.4 6.4 %collective-permute-start.4 = (bf16[4,8,1792]{2,1,0:T(8,128)(2,1)S(1)}, bf16[4,8,1792]{2,1,0:T(8,128)(2,1)S(1)}, u32[]{:S(2)}, u32[]{:S(2)}) collective-permute-start(bf16[4,8,1792]{2,1,0:T(8,128)(2,1)S(1)} %bitcast.41), channel_id=1, source_target_pairs={{0,32},{16,48},{32,0},{48,16},{1,33},{17,49},{33,1},{49,17},{2,34}... | collective-permute-start | bytes 344072 | tf_op jit(solution)/shard_map/ppermute | solution.py:601
  15.3 6.0 %collective-permute-start.3 = (bf16[4,8,1792]{2,1,0:T(8,128)(2,1)S(1)}, bf16[4,8,1792]{2,1,0:T(8,128)(2,1)S(1)}, u32[]{:S(2)}, u32[]{:S(2)}) collective-permute-start(bf16[4,8,1792]{2,1,0:T(8,128)(2,1)S(1)} %bitcast.42), channel_id=1, source_target_pairs={{0,48},{16,0},{32,16},{48,32},{1,49},{17,1},{33,17},{49,33},{2,50}... | collective-permute-start | bytes 344072 | tf_op jit(solution)/shard_map/ppermute | solution.py:601
  17.8 6.9 %collective-permute-start.8 = (bf16[256,384]{1,0:T(8,128)(2,1)S(1)}, bf16[256,384]{1,0:T(8,128)(2,1)S(1)}, u32[]{:S(2)}, u32[]{:S(2)}) collective-permute-start(bf16[256,384]{1,0:T(8,128)(2,1)S(1)} %get-tuple-element.133.token_0.tokens_ref), channel_id=1, source_target_pairs={{0,1},{1,0},{2,3},{3,2},{4,5},{5,4},{6,7},{7,6},{8,9},{9,8},{10,11... | collective-permute-start | bytes 589832 | tf_op jit(solution)/shard_map/ppermute | solution.py:614
  21.4 10.9 %collective-permute-start.6 = (bf16[4,4,8,1792]{3,2,1,0:T(8,128)(2,1)S(1)}, bf16[4,4,8,1792]{3,2,1,0:T(8,128)(2,1)S(1)}, u32[]{:S(2)}, u32[]{:S(2)}) collective-permute-start(bf16[4,4,8,1792]{3,2,1,0:T(8,128)(2,1)S(1)} %get-tuple-element.131), channel_id=1, source_target_pairs={{0,64},{4,68},{64,4},{68,0},{1,65},{5,69},{65,5},{69,1},{2,66},{6,... | collective-permute-start | bytes 1376264 | tf_op jit(solution)/shard_map/ppermute | solution.py:610
  22.7 9.6 %collective-permute-start.7 = (bf16[4,4,8,1792]{3,2,1,0:T(8,128)(2,1)S(1)}, bf16[4,4,8,1792]{3,2,1,0:T(8,128)(2,1)S(1)}, u32[]{:S(2)}, u32[]{:S(2)}) collective-permute-start(bf16[4,4,8,1792]{3,2,1,0:T(8,128)(2,1)S(1)} %get-tuple-element.131), channel_id=1, source_target_pairs={{0,68},{4,64},{64,0},{68,4},{1,69},{5,65},{65,1},{69,5},{2,70},{6,... | collective-permute-start | bytes 1376264 | tf_op jit(solution)/shard_map/ppermute | solution.py:610
  24.8 9.1 %collective-permute-start.9 = (bf16[2,256,384]{2,1,0:T(8,128)(2,1)S(1)}, bf16[2,256,384]{2,1,0:T(8,128)(2,1)S(1)}, u32[]{:S(2)}, u32[]{:S(2)}) collective-permute-start(bf16[2,256,384]{2,1,0:T(8,128)(2,1)S(1)} %pad_maximum_fusion.2), channel_id=1, source_target_pairs={{0,3},{1,2},{2,1},{3,0},{4,7},{5,6},{6,5},{7,4},{8,11},{9,10},{10,... | collective-permute-start | bytes 1179656 | tf_op jit(solution)/shard_map/ppermute | solution.py:614
  33.9 7.3 %collective-permute-start.10 = (bf16[2,4,8,1792]{3,2,1,0:T(8,128)(2,1)S(1)}, bf16[2,4,8,1792]{3,2,1,0:T(8,128)(2,1)S(1)}, u32[]{:S(2)}, u32[]{:S(2)}) collective-permute-start(bf16[2,4,8,1792]{3,2,1,0:T(8,128)(2,1)S(1)} %slice.18), channel_id=1, source_target_pairs={{0,64},{4,68},{64,4},{68,0},{1,65},{5,69},{65,5},{69,1},{2,66},{6,... | collective-permute-start | bytes 688136 | tf_op jit(solution)/shard_map/ppermute | solution.py:610
  34.0 7.2 %collective-permute-start.11 = (bf16[2,4,8,1792]{3,2,1,0:T(8,128)(2,1)S(1)}, bf16[2,4,8,1792]{3,2,1,0:T(8,128)(2,1)S(1)}, u32[]{:S(2)}, u32[]{:S(2)}) collective-permute-start(bf16[2,4,8,1792]{3,2,1,0:T(8,128)(2,1)S(1)} %slice.19), channel_id=1, source_target_pairs={{0,68},{4,64},{64,0},{68,4},{1,69},{5,65},{65,1},{69,5},{2,70},{6,... | collective-permute-start | bytes 688136 | tf_op jit(solution)/shard_map/ppermute | solution.py:610
  41.5 4.0 %collective-permute-start.12 = (bf16[512,1792]{1,0:T(8,128)(2,1)S(1)}, bf16[512,1792]{1,0:T(8,128)(2,1)S(1)}, u32[]{:S(2)}, u32[]{:S(2)}) collective-permute-start(bf16[512,1792]{1,0:T(8,128)(2,1)S(1)} %bitcast.34), channel_id=1, source_target_pairs={{0,8},{8,0},{1,9},{9,1},{2,10},{10,2},{3,11},{11,3},{4,12},{12,4},... | collective-permute-start | bytes 5505032 | tf_op jit(solution)/shard_map/ppermute | solution.py:601
  57.9 9.5 %collective-permute-start.14 = (bf16[512,1024]{1,0:T(8,128)(2,1)S(1)}, bf16[512,1024]{1,0:T(8,128)(2,1)S(1)}, u32[]{:S(2)}, u32[]{:S(2)}) collective-permute-start(bf16[512,1024]{1,0:T(8,128)(2,1)S(1)} %get-tuple-element.96), channel_id=1, source_target_pairs={{0,8},{8,0},{1,9},{9,1},{2,10},{10,2},{3,11},{11,3},{4,12},{12,4},... | collective-permute-start | bytes 3145736 | tf_op jit(solution)/shard_map/ppermute | solution.py:601
  65.0 2.4 %collective-permute-start.13 = (bf16[512,768]{1,0:T(8,128)(2,1)S(1)}, bf16[512,768]{1,0:T(8,128)(2,1)S(1)}, u32[]{:S(2)}, u32[]{:S(2)}) collective-permute-start(bf16[512,768]{1,0:T(8,128)(2,1)S(1)} %get-tuple-element.94), channel_id=1, source_target_pairs={{0,8},{8,0},{1,9},{9,1},{2,10},{10,2},{3,11},{11,3},{4,12},{12,4},... | collective-permute-start | bytes 2359304 | tf_op jit(solution)/shard_map/ppermute | solution.py:601
  67.8 9.4 %collective-permute-start.15 = (bf16[64,1792]{1,0:T(8,128)(2,1)S(1)}, bf16[64,1792]{1,0:T(8,128)(2,1)S(1)}, u32[]{:S(2)}, u32[]{:S(2)}) collective-permute-start(bf16[64,1792]{1,0:T(8,128)(2,1)S(1)} %get-tuple-element.99), channel_id=1, source_target_pairs={{0,64},{4,68},{64,4},{68,0},{1,65},{5,69},{65,5},{69,1},{2,66},{6,... | collective-permute-start | bytes 688136 | tf_op jit(solution)/shard_map/ppermute | solution.py:610
  68.2 9.1 %collective-permute-start.16 = (bf16[64,1792]{1,0:T(8,128)(2,1)S(1)}, bf16[64,1792]{1,0:T(8,128)(2,1)S(1)}, u32[]{:S(2)}, u32[]{:S(2)}) collective-permute-start(bf16[64,1792]{1,0:T(8,128)(2,1)S(1)} %get-tuple-element.100), channel_id=1, source_target_pairs={{0,68},{4,64},{64,0},{68,4},{1,69},{5,65},{65,1},{69,5},{2,70},{6,... | collective-permute-start | bytes 688136 | tf_op jit(solution)/shard_map/ppermute | solution.py:610
  77.4 16.5 %collective-permute-start.17 = (bf16[128,1792]{1,0:T(8,128)(2,1)S(1)}, bf16[128,1792]{1,0:T(8,128)(2,1)S(1)}, u32[]{:S(2)}, u32[]{:S(2)}) collective-permute-start(bf16[128,1792]{1,0:T(8,128)(2,1)S(1)} %get-tuple-element.101), channel_id=1, source_target_pairs={{0,64},{4,68},{64,4},{68,0},{1,65},{5,69},{65,5},{69,1},{2,66},{6,... | collective-permute-start | bytes 1376264 | tf_op jit(solution)/shard_map/ppermute | solution.py:610
  78.6 15.3 %collective-permute-start.18 = (bf16[128,1792]{1,0:T(8,128)(2,1)S(1)}, bf16[128,1792]{1,0:T(8,128)(2,1)S(1)}, u32[]{:S(2)}, u32[]{:S(2)}) collective-permute-start(bf16[128,1792]{1,0:T(8,128)(2,1)S(1)} %get-tuple-element.102), channel_id=1, source_target_pairs={{0,68},{4,64},{64,0},{68,4},{1,69},{5,65},{65,1},{69,5},{2,70},{6,... | collective-permute-start | bytes 1376264 | tf_op jit(solution)/shard_map/ppermute | solution.py:610
  80.7 8.1 %collective-permute-start.19 = (bf16[272,384]{1,0:T(8,128)(2,1)S(1)}, bf16[272,384]{1,0:T(8,128)(2,1)S(1)}, u32[]{:S(2)}, u32[]{:S(2)}) collective-permute-start(bf16[272,384]{1,0:T(8,128)(2,1)S(1)} %get-tuple-element.104), channel_id=1, source_target_pairs={{0,1},{1,0},{2,3},{3,2},{4,5},{5,4},{6,7},{7,6},{8,9},{9,8},{10,11... | collective-permute-start | bytes 626696 | tf_op jit(solution)/shard_map/ppermute | solution.py:614
  80.7 11.3 %collective-permute-start.20 = (bf16[272,384]{1,0:T(8,128)(2,1)S(1)}, bf16[272,384]{1,0:T(8,128)(2,1)S(1)}, u32[]{:S(2)}, u32[]{:S(2)}) collective-permute-start(bf16[272,384]{1,0:T(8,128)(2,1)S(1)} %get-tuple-element.105), channel_id=1, source_target_pairs={{0,3},{1,2},{2,1},{3,0},{4,7},{5,6},{6,5},{7,4},{8,11},{9,10},{10,... | collective-permute-start | bytes 626696 | tf_op jit(solution)/shard_map/ppermute | solution.py:614
  83.7 10.2 %collective-permute-start.21 = (bf16[272,384]{1,0:T(8,128)(2,1)S(1)}, bf16[272,384]{1,0:T(8,128)(2,1)S(1)}, u32[]{:S(2)}, u32[]{:S(2)}) collective-permute-start(bf16[272,384]{1,0:T(8,128)(2,1)S(1)} %get-tuple-element.106), channel_id=1, source_target_pairs={{0,2},{1,3},{2,0},{3,1},{4,6},{5,7},{6,4},{7,5},{8,10},{9,11},{10,... | collective-permute-start | bytes 626696 | tf_op jit(solution)/shard_map/ppermute | solution.py:614
  94.9 14.0 %all-to-all-start = ((bf16[16,8,1792]{2,1,0:T(8,128)(2,1)}), bf16[16,8,1792]{2,1,0:T(8,128)(2,1)S(1)}, u32[]{:S(2)}, u32[]{:S(2)}) async-start(bf16[16,8,1792]{2,1,0:T(8,128)(2,1)} %shard_map.217), calls=%async_computation | async-start | bytes 917504 | tf_op jit(solution)/shard_map/all_to_all | solution.py:748
  101.4 7.4 %collective-permute-start.22 = (bf16[272,384]{1,0:T(8,128)(2,1)S(1)}, bf16[272,384]{1,0:T(8,128)(2,1)S(1)}, u32[]{:S(2)}, u32[]{:S(2)}) collective-permute-start(bf16[272,384]{1,0:T(8,128)(2,1)S(1)} %get-tuple-element.113), channel_id=1, source_target_pairs={{0,4},{4,0},{1,5},{5,1},{2,6},{6,2},{3,7},{7,3},{8,12},{12,8},{9,1... | collective-permute-start | bytes 626696 | tf_op jit(solution)/shard_map/ppermute | solution.py:601
  (1 other events, 4.3 us)

commit v6 on v5

--- a/solution.py
+++ b/solution.py
@@ -185,11 +185,16 @@
     scratch[0:3, 4 * D : 5 * D] = w_out_ref[...].astype(F32)
     start = 5 * D + 128
     swap = interleave()
+    fc1 = jnp.concatenate([w_fc1_ref[...].astype(F32), jnp.zeros((5, FF), F32)], axis=0)
+    blocks = [fc1[:, block * 512 : block * 512 + 512] for block in range(3)]
+    blocks = jnp.concatenate(blocks + [jnp.zeros((8, 512), F32)], axis=0)
+    moved = dot(blocks.astype(BF), swap)
     for block in range(3):
-        moved = dot(w_fc1_ref[:, block * 512 : block * 512 + 512], swap)
         for part in range(4):
             lanes = start + part * D + block * 128
-            scratch[0:3, lanes : lanes + 128] = moved[:, part * 128 : part * 128 + 128]
+            scratch[0:3, lanes : lanes + 128] = moved[
+                block * 8 : block * 8 + 3, part * 128 : part * 128 + 128
+            ]
     start = start + FF
     rows = w_fc2_ref[...].astype(F32)
     for j in range(3):
@@ -223,14 +228,22 @@
     return tuple(lax.axis_index(axis) for axis in ("xl", "y", "core", "xh", "z"))
 
 
+def token_kernel(token_0, token_1, token_23, condition_ref, hidden_ref, hidden_t, normed_ref):
+    shift_one, scale_one = condition_ref[0:1, :], condition_ref[1:2, :]
+    own = token_0.shape[0]
+    for index, token_ref in enumerate((token_0, token_1, token_23.at[0], token_23.at[1])):
+        rows = slice(index * own, index * own + own)
+        normed, _ = normalise(token_ref[...].astype(F32))
+        normed_ref[rows, :] = normed
+        hidden = (normed * (1.0 + scale_one) + shift_one).astype(BF)
+        hidden_ref[rows, :] = hidden
+        hidden_t[:, rows] = hidden.T
+
+
 def attention_part(
     unpack,
-    token_0,
-    token_1,
-    token_23,
-    condition_ref,
+    hidden_ref,
     w_qkv_ref,
-    hidden_ref,
     query_ref,
     keys_ref,
     values_ref,
@@ -254,13 +267,11 @@
         columns.append(last[:, D:].astype(F32))
     biases = jnp.concatenate(columns, axis=0).T[:8, :]
     biases_ref[...] = biases
-    shift_one, scale_one = condition_ref[0:1, :], condition_ref[1:2, :]
-    own = token_0.shape[0]
-    for index, token_ref in enumerate((token_0, token_1, token_23.at[0], token_23.at[1])):
-        normed, _ = normalise(token_ref[...].astype(F32))
-        hidden = (normed * (1.0 + scale_one) + shift_one).astype(BF)
+    length = hidden_ref.shape[0]
+    own = length // 4
+    for index in range(4):
         rows = slice(index * own, index * own + own)
-        hidden_ref[rows, :] = hidden
+        hidden = hidden_ref[rows, :]
         keys = dot(hidden, w_qkv_ref[:, D : 2 * D])
         values = dot(hidden, w_qkv_ref[:, 2 * D :]) + biases[1:2, :]
         keys_ref[rows, :] = keys.astype(BF)
@@ -390,8 +401,8 @@
 
 
 def front_kernel(
-    near_ref, far_ref, token_0, token_1, token_23, swapped_ref, cotangent_ref, condition_ref,
-    w_qkv_ref, hidden_ref, query_ref, keys_ref, values_ref, keys_t, exponent_ref,
+    near_ref, far_ref, token_0, hidden_ref, swapped_ref, cotangent_ref, condition_ref,
+    w_qkv_ref, query_ref, keys_ref, values_ref, keys_t, exponent_ref,
     output_a, output_b, middle_grad_ref, attended_grad_ref, weighted_ref, vectors_ref, rows_ref,
     more_ref, keep_ref, send_ref,
     values_t, weights_scr, biases_ref, attended_t, w_fc1, w_fc2, w_out, slope_scr, whole, third,
@@ -399,8 +410,8 @@
     ids = device_ids()
     unpack = unpacker(ids, near_ref, far_ref)
     attention_part(
-        unpack, token_0, token_1, token_23, condition_ref,
-        w_qkv_ref, hidden_ref, query_ref, keys_ref, values_ref, keys_t, exponent_ref,
+        unpack, hidden_ref,
+        w_qkv_ref, query_ref, keys_ref, values_ref, keys_t, exponent_ref,
         biases_ref, attended_t, values_t, weights_scr, w_fc2, w_out,
     )
     forward_part(
@@ -411,13 +422,13 @@
 
 
 def backward_kernel(
-    token_0, token_1, token_23, condition_ref,
+    normed_ref,
     w_qkv_ref, query_ref, keys_ref, values_ref, keys_t, exponent_ref,
-    attended_grad_ref, weighted_ref, vectors_in, hidden_ref, rows_ref, more_ref,
+    attended_grad_ref, weighted_ref, vectors_in, hidden_t, rows_ref, more_ref,
     piece_0, piece_1, piece_2, piece_3, keep_ref, send_ref,
     query_t, vectors_ref, grad_query_ref, key_grads, value_grads, whole, third, tall,
 ):
-    own = token_0.shape[0]
+    own = query_ref.shape[0]
     for pair in range(HEADS // 2):
         tile = slice(pair * 128, pair * 128 + 128)
         key_sum = None
@@ -441,14 +452,14 @@
     grad_query_ref[...] = grad_query
     shift_sum, scale_sum = None, None
     pieces = (piece_0, piece_1, piece_2, piece_3)
-    for index, token_ref in enumerate((token_0, token_1, token_23.at[0], token_23.at[1])):
+    for index in range(4):
         rows = slice(index * own, index * own + own)
         grad = dot_nt(key_grads[rows, :], w_qkv_ref[:, D : 2 * D]) + dot_nt(
             value_grads[rows, :], w_qkv_ref[:, 2 * D :]
         )
         if index == 0:
             grad = grad + dot_nt(grad_query, w_qkv_ref[:, :D])
-        normed, _ = normalise(token_ref[...].astype(F32))
+        normed = normed_ref[rows, :]
         shifts, scales = column_sum(grad), column_sum(grad * normed)
         shift_sum = shifts if shift_sum is None else shift_sum + shifts
         scale_sum = scales if scale_sum is None else scale_sum + scales
@@ -463,9 +474,9 @@
     tall[0:8, :] = rows_ref[...]
     tall[0:1, :] = column_sum(grad_query_ref[...].astype(F32))
     tall[1:2, :] = column_sum(value_grads[...].astype(F32))
-    whole[:, :D] = dot_tn(hidden_ref[:own, :], grad_query_ref[...]).astype(BF)
-    whole[:, D : 2 * D] = dot_tn(hidden_ref[...], key_grads[...]).astype(BF)
-    whole[:, 2 * D : 3 * D] = dot_tn(hidden_ref[...], value_grads[...]).astype(BF)
+    whole[:, :D] = dot(hidden_t[:, :own], grad_query_ref[...]).astype(BF)
+    whole[:, D : 2 * D] = dot(hidden_t[...], key_grads[...]).astype(BF)
+    whole[:, 2 * D : 3 * D] = dot(hidden_t[...], value_grads[...]).astype(BF)
     whole[:, 3 * D :] = more_ref[:, :D]
     third[:, :D] = more_ref[:, D:]
     third[:, D:] = tall[...].T.astype(BF)
@@ -529,10 +540,12 @@
 
 
 def add_kernel(own_ref, left_ref, right_ref, out_ref):
-    for index in range(out_ref.shape[0]):
-        rows = slice(index * 8, index * 8 + 8)
+    for index in range(0, out_ref.shape[0], 2):
+        rows = slice(index * 8, index * 8 + 16)
         total = own_ref[rows, :].astype(F32) + left_ref[rows, :].astype(F32)
-        out_ref[index] = (total + right_ref[rows, :].astype(F32)).astype(BF)
+        total = total + right_ref[rows, :].astype(F32)
+        out_ref[index] = total[:8].astype(BF)
+        out_ref[index + 1] = total[8:].astype(BF)
 
 
 def last_rows(block, more):
@@ -541,10 +554,9 @@
     return jnp.concatenate([block[6:8, :more], third], axis=0)
 
 
-def last_kernel(
-    output_ref, grad_ref, other_ref, sums_ref, pieces_ref,
+def join_kernel(
+    output_ref, grad_ref, other_ref, sums_ref,
     output_out, grad_out, modulation_out,
-    qkv_ref, b_query, b_value, b_out, b_fc1, b_fc2, fc1_ref, fc2_ref, out_ref,
 ):
     upper = lax.axis_index("xh")
     side = output_ref.shape[0]
@@ -559,6 +571,12 @@
         cut = slice(part * D, part * D + D)
         modulation_out[0:1, cut] = low[part : part + 1, :]
         modulation_out[1:2, cut] = high[part : part + 1, :]
+
+
+def last_kernel(
+    pieces_ref,
+    qkv_ref, b_query, b_value, b_out, b_fc1, b_fc2, fc1_ref, fc2_ref, out_ref,
+):
     total = pieces_ref[0].astype(F32)
     for index in range(1, pieces_ref.shape[0]):
         total = total + pieces_ref[index].astype(F32)
@@ -579,17 +597,22 @@
     swap = interleave()
     one, two = total[0:3], total[3:6]
     fc1 = jnp.concatenate([one, two[:, : FF - SECOND]], axis=1)
-    for block in range(3):
-        rest = jnp.concatenate(
+    fc1 = jnp.concatenate([fc1, jnp.zeros((5, FF), F32)], axis=0)
+    blocks = [
+        jnp.concatenate(
             [fc1[:, i * D + block * 128 : i * D + block * 128 + 128] for i in range(4)], axis=1
         )
-        moved = None
-        for _ in range(3):
-            part = rest.astype(BF)
-            rest = rest - part.astype(F32)
-            step = dot_nt(part, swap)
-            moved = step if moved is None else moved + step
-        fc1_ref[:, block * 512 : block * 512 + 512] = moved
+        for block in range(3)
+    ]
+    rest = jnp.concatenate(blocks + [jnp.zeros((8, 512), F32)], axis=0)
+    parts = []
+    for _ in range(3):
+        parts.append(rest.astype(BF))
+        rest = rest - parts[-1].astype(F32)
+    moved = dot_nt(jnp.concatenate(parts, axis=0), swap)
+    moved = moved[:32] + moved[32:64] + moved[64:]
+    for block in range(3):
+        fc1_ref[:, block * 512 : block * 512 + 512] = moved[block * 8 : block * 8 + 3]
     fc2 = jnp.concatenate([two[:, FF - SECOND :], last_rows(total, SECOND_LAST), small[3:6, D:]], axis=1)
     for j in range(3):
         for part in range(4):
@@ -664,20 +687,24 @@
     far_tokens = trade(jnp.stack([tokens, near_tokens]), 3)
     before, after = shift_x(plane, 1), shift_x(plane, -1)
     before, after, far_tokens = lax.optimization_barrier((before, after, far_tokens))
-    all_tokens = (tokens, near_tokens, far_tokens)
+    hidden, hidden_t, normed = call(
+        token_kernel,
+        (vmem(length, D), vmem(D, length), vmem(length, D, dtype=F32)),
+        [],
+        hold(tokens, near_tokens, far_tokens, condition),
+    )
     half = plane.shape[0] // 2
     opposite = jnp.concatenate([shift_x(before[:half], 1), shift_x(after[half:], -1)])
     near = jnp.stack([plane, after, opposite, before]).reshape(-1, WIDE)
     other = shift(near, "core", 1, 2)
 
     (
-        w_all, hidden, query, keys, values, keys_t, exponents,
+        w_all, query, keys, values, keys_t, exponents,
         output_a, output_b, middle_grad, attended_grad, weighted, vectors, bias_sums, more_grads, keep_two, send_two,
     ) = call(
         front_kernel,
         (
             vmem(D, 3 * D),
-            vmem(length, D),
             vmem(own, D),
             vmem(length, D),
             vmem(length, D),
@@ -706,7 +733,7 @@
             vmem(D, 2 * SECOND),
             vmem(D, SECOND_LAST),
         ],
-        hold(near, other, *all_tokens, swapped, cotangent, condition),
+        hold(near, other, tokens, hidden, swapped, cotangent, condition),
         limit=32,
     )
     other_two = shift(send_two, "core", 1, 2)
@@ -725,8 +752,8 @@
             vmem(128, D, dtype=F32),
         ],
         hold(
-            *all_tokens, condition, w_all, query, keys, values, keys_t, exponents, attended_grad, weighted, vectors,
-            hidden, bias_sums, more_grads,
+            normed, w_all, query, keys, values, keys_t, exponents, attended_grad, weighted, vectors,
+            hidden_t, bias_sums, more_grads,
         ),
         limit=24,
     )
@@ -753,15 +780,17 @@
         hold(tokens, condition, middle_grad, *arrived, output_b),
     )
     grad_back = shift(grad_b, "xh", 1, 2)
+    output, input_grad, modulation_grad = call(
+        join_kernel,
+        (sds(2, side, D), sds(2, side, D), sds(2, 6 * D, dtype=F32)),
+        [],
+        hold(output_a, grad_a, grad_back, sums),
+    )
     (
-        output, input_grad, modulation_grad,
         grad_qkv, grad_b_query, grad_b_value, grad_b_out, grad_b_fc1, grad_b_fc2, grad_fc1, grad_fc2, grad_out,
     ) = call(
         last_kernel,
         (
-            sds(2, side, D),
-            sds(2, side, D),
-            sds(2, 6 * D, dtype=F32),
             sds(3, 3 * D, dtype=F32),
             sds(1, 3, dtype=F32),
             sds(1, 3, dtype=F32),
@@ -773,7 +802,7 @@
             sds(3, D, dtype=F32),
         ),
         [],
-        hold(output_a, grad_a, grad_back, sums, pieces),
+        hold(pieces),
     )
     return (
         output,

time: 113 us -> 111 us (0.982)
    pallas_call x8 -> x10, Pallas kernels: 24.5 us -> 24.5 us  [call(): pl.pallas_call(kernel, out_shape=out_shape, in_specs=[pl.BlockSpec(memory...]
  transfers between devices with their start and end apart: 24 -> 24, of which waited for: 14 -> 14; matrix products, arithmetic and copies ran while one was open for 1% -> 1% of each run, Pallas kernels for 6% -> 8%
where the time goes in v6:
time: 111 us; the launch traced here: 110 us
  starting transfers between devices  43 us (39%)
  waiting for transfers between devices  40.3 us (36%)
  Pallas kernels  24.5 us (22%)
  other arithmetic  1.41 us (1%)
    pallas_call x10, Pallas kernels, call(): pl.pallas_call(kernel, out_shape=out_shape, in_specs=[pl.BlockSpec(memory...  24.5 us
    ppermute x8, waiting for transfers between devices, shift_x(): return lax.ppermute(array, X, moves)  14.5 us
    ppermute x8, waiting for transfers between devices, shift(): lax.ppermute(array, axis, [(i, (i + step) % size) for i in range(size)])  14 us
    ppermute x8, starting transfers between devices, shift_x(): return lax.ppermute(array, X, moves)  13.3 us
    ppermute x7, starting transfers between devices, trade(): return lax.ppermute(array, 'z', [(i, i ^ bits) for i in range(4)])  12.9 us
    ppermute x7, waiting for transfers between devices, trade(): return lax.ppermute(array, 'z', [(i, i ^ bits) for i in range(4)])  11.8 us
    ppermute x8, starting transfers between devices, shift(): lax.ppermute(array, axis, [(i, (i + step) % size) for i in range(size)])  10.6 us
    all_to_all x1, starting transfers between devices, body(): pieces = lax.all_to_all(shares, ('y', 'z'), 0, 0, tiled=True)  6.26 us
  transfers between devices with their start and end apart: 24, of which 14 were waited for; matrix products, arithmetic and copies ran while one was open for 1% of the time, Pallas kernels for 8%

profile of v6, /device:TPU:8, one launch (start us, length us, event | category | flops | bytes accessed | tf_op | source)
XLA Modules:
  0.0 110.1 jit_solution(870217611850840725)
XLA Ops:
  2.0 2.0 %collective-permute-start = (bf16[8,1792]{1,0:T(8,128)(2,1)S(1)}, bf16[8,1792]{1,0:T(8,128)(2,1)S(1)}, u32[]{:S(2)}, u32[]{:S(2)}) collective-permute-start(bf16[8,1792]{1,0:T(8,128)(2,1)S(1)} %get-tuple-element.73), channel_id=1, source_target_pairs={{0,1},{1,0},{2,3},{3,2},{4,5},{5,4},{6,7},{7,6},{8,9},{9,8},{10,11... | collective-permute-start | bytes 86024 | tf_op jit(solution)/shard_map/ppermute | solution.py:637
  4.0 3.0 %collective-permute-start.2 = (bf16[2,128,384]{2,1,0:T(8,128)(2,1)S(1)}, bf16[2,128,384]{2,1,0:T(8,128)(2,1)S(1)}, u32[]{:S(2)}, u32[]{:S(2)}) collective-permute-start(bf16[2,128,384]{2,1,0:T(8,128)(2,1)S(1)} %get-tuple-element.74), channel_id=1, source_target_pairs={{0,4},{4,0},{1,5},{5,1},{2,6},{6,2},{3,7},{7,3},{8,12},{12,8},{9,1... | collective-permute-start | bytes 589832 | tf_op jit(solution)/shard_map/ppermute | solution.py:624
  7.1 3.0 %collective-permute-start.1 = (bf16[2,8,1792]{2,1,0:T(8,128)(2,1)S(1)}, bf16[2,8,1792]{2,1,0:T(8,128)(2,1)S(1)}, u32[]{:S(2)}, u32[]{:S(2)}) collective-permute-start(bf16[2,8,1792]{2,1,0:T(8,128)(2,1)S(1)} %get-tuple-element.139), channel_id=1, source_target_pairs={{0,3},{1,2},{2,1},{3,0},{4,7},{5,6},{6,5},{7,4},{8,11},{9,10},{10,... | collective-permute-start | bytes 172040 | tf_op jit(solution)/shard_map/ppermute | solution.py:637
  12.6 1.6 %collective-permute-start.5 = (bf16[4,8,1792]{2,1,0:T(8,128)(2,1)S(1)}, bf16[4,8,1792]{2,1,0:T(8,128)(2,1)S(1)}, u32[]{:S(2)}, u32[]{:S(2)}) collective-permute-start(bf16[4,8,1792]{2,1,0:T(8,128)(2,1)S(1)} %bitcast.40), channel_id=1, source_target_pairs={{0,16},{16,32},{32,48},{48,0},{1,17},{17,33},{33,49},{49,1},{2,18}... | collective-permute-start | bytes 344072 | tf_op jit(solution)/shard_map/ppermute | solution.py:624
  15.1 2.4 %collective-permute-start.3 = (bf16[4,8,1792]{2,1,0:T(8,128)(2,1)S(1)}, bf16[4,8,1792]{2,1,0:T(8,128)(2,1)S(1)}, u32[]{:S(2)}, u32[]{:S(2)}) collective-permute-start(bf16[4,8,1792]{2,1,0:T(8,128)(2,1)S(1)} %bitcast.42), channel_id=1, source_target_pairs={{0,48},{16,0},{32,16},{48,32},{1,49},{17,1},{33,17},{49,33},{2,50}... | collective-permute-start | bytes 344072 | tf_op jit(solution)/shard_map/ppermute | solution.py:624
  18.6 2.0 %collective-permute-done.4 = bf16[4,8,1792]{2,1,0:T(8,128)(2,1)S(1)} collective-permute-done((bf16[4,8,1792]{2,1,0:T(8,128)(2,1)S(1)}, bf16[4,8,1792]{2,1,0:T(8,128)(2,1)S(1)}, u32[]{:S(2)}, u32[]{:S(2)}) %collective-permute-start.4) | collective-permute-done | bytes 114720 | tf_op jit(solution)/shard_map/ppermute | solution.py:624
  22.5 2.0 %collective-permute-start.7 = (bf16[4,4,8,1792]{3,2,1,0:T(8,128)(2,1)S(1)}, bf16[4,4,8,1792]{3,2,1,0:T(8,128)(2,1)S(1)}, u32[]{:S(2)}, u32[]{:S(2)}) collective-permute-start(bf16[4,4,8,1792]{3,2,1,0:T(8,128)(2,1)S(1)} %get-tuple-element.135), channel_id=1, source_target_pairs={{0,68},{4,64},{64,0},{68,4},{1,69},{5,65},{65,1},{69,5},{2,70},{6,... | collective-permute-start | bytes 1376264 | tf_op jit(solution)/shard_map/ppermute | solution.py:633
  24.6 3.0 %collective-permute-start.9 = (bf16[2,256,384]{2,1,0:T(8,128)(2,1)S(1)}, bf16[2,256,384]{2,1,0:T(8,128)(2,1)S(1)}, u32[]{:S(2)}, u32[]{:S(2)}) collective-permute-start(bf16[2,256,384]{2,1,0:T(8,128)(2,1)S(1)} %pad_maximum_fusion.2), channel_id=1, source_target_pairs={{0,3},{1,2},{2,1},{3,0},{4,7},{5,6},{6,5},{7,4},{8,11},{9,10},{10,... | collective-permute-start | bytes 1179656 | tf_op jit(solution)/shard_map/ppermute | solution.py:637
  27.7 4.5 %collective-permute-done.6 = bf16[4,4,8,1792]{3,2,1,0:T(8,128)(2,1)S(1)} collective-permute-done((bf16[4,4,8,1792]{3,2,1,0:T(8,128)(2,1)S(1)}, bf16[4,4,8,1792]{3,2,1,0:T(8,128)(2,1)S(1)}, u32[]{:S(2)}, u32[]{:S(2)}) %collective-permute-start.6) | collective-permute-done | bytes 458784 | tf_op jit(solution)/shard_map/ppermute | solution.py:633
  33.8 3.2 %collective-permute-start.11 = (bf16[2,4,8,1792]{3,2,1,0:T(8,128)(2,1)S(1)}, bf16[2,4,8,1792]{3,2,1,0:T(8,128)(2,1)S(1)}, u32[]{:S(2)}, u32[]{:S(2)}) collective-permute-start(bf16[2,4,8,1792]{3,2,1,0:T(8,128)(2,1)S(1)} %slice.19), channel_id=1, source_target_pairs={{0,68},{4,64},{64,0},{68,4},{1,69},{5,65},{65,1},{69,5},{2,70},{6,... | collective-permute-start | bytes 688136 | tf_op jit(solution)/shard_map/ppermute | solution.py:633
  37.0 4.0 %collective-permute-done.10 = bf16[2,4,8,1792]{3,2,1,0:T(8,128)(2,1)S(1)} collective-permute-done((bf16[2,4,8,1792]{3,2,1,0:T(8,128)(2,1)S(1)}, bf16[2,4,8,1792]{3,2,1,0:T(8,128)(2,1)S(1)}, u32[]{:S(2)}, u32[]{:S(2)}) %collective-permute-start.10) | collective-permute-done | bytes 229408 | tf_op jit(solution)/shard_map/ppermute | solution.py:633
  42.5 2.9 %collective-permute-done.12.far_ref = bf16[512,1792]{1,0:T(8,128)(2,1)S(1)} collective-permute-done((bf16[512,1792]{1,0:T(8,128)(2,1)S(1)}, bf16[512,1792]{1,0:T(8,128)(2,1)S(1)}, u32[]{:S(2)}, u32[]{:S(2)}) %collective-permute-start.12) | collective-permute-done | bytes 1835040 | tf_op jit(solution)/shard_map/ppermute | solution.py:624
  45.4 12.2 %shard_map.213 = (bf16[384,1152]{1,0:T(8,128)(2,1)S(1)}, bf16[256,384]{1,0:T(8,128)(2,1)S(1)}, bf16[1024,384]{1,0:T(8,128)(2,1)S(1)}, bf16[1024,384]{1,0:T(8,128...) custom-call(bf16[512,1792]{1,0:T(8,128)(2,1)S(1)} %bitcast.35, ...), custom_call_target="tpu_custom_call" | custom-call | tf_op jit(solution)/shard_map/pallas_call | solution.py:659
  58.1 6.5 %shard_map.214 = (bf16[272,384]{1,0:T(8,128)(2,1)S(1)}, bf16[272,384]{1,0:T(8,128)(2,1)S(1)}, bf16[272,384]{1,0:T(8,128)(2,1)S(1)}, bf16[272,384]{1,0:T(8,128)(2...) custom-call(f32[1024,384]{1,0:T(8,128)S(1)} %get-tuple-element.84.normed_ref, ...), custom_call_target="tpu_custom_call" | custom-call | tf_op jit(solution)/shard_map/pallas_call | solution.py:659
  65.0 1.9 %collective-permute-done.13.back_one = bf16[512,768]{1,0:T(8,128)(2,1)S(1)} collective-permute-done((bf16[512,768]{1,0:T(8,128)(2,1)S(1)}, bf16[512,768]{1,0:T(8,128)(2,1)S(1)}, u32[]{:S(2)}, u32[]{:S(2)}) %collective-permute-start.13) | collective-permute-done | bytes 786464 | tf_op jit(solution)/shard_map/ppermute | solution.py:624
  67.7 3.0 %collective-permute-start.16 = (bf16[64,1792]{1,0:T(8,128)(2,1)S(1)}, bf16[64,1792]{1,0:T(8,128)(2,1)S(1)}, u32[]{:S(2)}, u32[]{:S(2)}) collective-permute-start(bf16[64,1792]{1,0:T(8,128)(2,1)S(1)} %get-tuple-element.104), channel_id=1, source_target_pairs={{0,68},{4,64},{64,0},{68,4},{1,69},{5,65},{65,1},{69,5},{2,70},{6,... | collective-permute-start | bytes 688136 | tf_op jit(solution)/shard_map/ppermute | solution.py:633
  70.8 6.0 %collective-permute-done.15.up_ref = bf16[64,1792]{1,0:T(8,128)(2,1)S(1)} collective-permute-done((bf16[64,1792]{1,0:T(8,128)(2,1)S(1)}, bf16[64,1792]{1,0:T(8,128)(2,1)S(1)}, u32[]{:S(2)}, u32[]{:S(2)}) %collective-permute-start.15) | collective-permute-done | bytes 229408 | tf_op jit(solution)/shard_map/ppermute | solution.py:633
  78.1 2.1 %collective-permute-start.18 = (bf16[128,1792]{1,0:T(8,128)(2,1)S(1)}, bf16[128,1792]{1,0:T(8,128)(2,1)S(1)}, u32[]{:S(2)}, u32[]{:S(2)}) collective-permute-start(bf16[128,1792]{1,0:T(8,128)(2,1)S(1)} %get-tuple-element.106), channel_id=1, source_target_pairs={{0,68},{4,64},{64,0},{68,4},{1,69},{5,65},{65,1},{69,5},{2,70},{6,... | collective-permute-start | bytes 1376264 | tf_op jit(solution)/shard_map/ppermute | solution.py:633
  80.2 3.0 %collective-permute-start.20 = (bf16[272,384]{1,0:T(8,128)(2,1)S(1)}, bf16[272,384]{1,0:T(8,128)(2,1)S(1)}, u32[]{:S(2)}, u32[]{:S(2)}) collective-permute-start(bf16[272,384]{1,0:T(8,128)(2,1)S(1)} %get-tuple-element.109), channel_id=1, source_target_pairs={{0,3},{1,2},{2,1},{3,0},{4,7},{5,6},{6,5},{7,4},{8,11},{9,10},{10,... | collective-permute-start | bytes 626696 | tf_op jit(solution)/shard_map/ppermute | solution.py:637
  84.7 3.7 %collective-permute-done.19.piece_1 = bf16[272,384]{1,0:T(8,128)(2,1)S(1)} collective-permute-done((bf16[272,384]{1,0:T(8,128)(2,1)S(1)}, bf16[272,384]{1,0:T(8,128)(2,1)S(1)}, u32[]{:S(2)}, u32[]{:S(2)}) %collective-permute-start.19) | collective-permute-done | bytes 208928 | tf_op jit(solution)/shard_map/ppermute | solution.py:637
  88.3 3.1 %collective-permute-done.20.piece_2 = bf16[272,384]{1,0:T(8,128)(2,1)S(1)} collective-permute-done((bf16[272,384]{1,0:T(8,128)(2,1)S(1)}, bf16[272,384]{1,0:T(8,128)(2,1)S(1)}, u32[]{:S(2)}, u32[]{:S(2)}) %collective-permute-start.20) | collective-permute-done | bytes 208928 | tf_op jit(solution)/shard_map/ppermute | solution.py:637
  91.5 1.9 %collective-permute-done.21.piece_3 = bf16[272,384]{1,0:T(8,128)(2,1)S(1)} collective-permute-done((bf16[272,384]{1,0:T(8,128)(2,1)S(1)}, bf16[272,384]{1,0:T(8,128)(2,1)S(1)}, u32[]{:S(2)}, u32[]{:S(2)}) %collective-permute-start.21) | collective-permute-done | bytes 208928 | tf_op jit(solution)/shard_map/ppermute | solution.py:637
  94.3 6.3 %all-to-all-start = ((bf16[16,8,1792]{2,1,0:T(8,128)(2,1)}), bf16[16,8,1792]{2,1,0:T(8,128)(2,1)S(1)}, u32[]{:S(2)}, u32[]{:S(2)}) async-start(bf16[16,8,1792]{2,1,0:T(8,128)(2,1)} %shard_map.219), calls=%async_computation | async-start | bytes 917504 | tf_op jit(solution)/shard_map/all_to_all | solution.py:775
  102.3 6.0 %collective-permute-done.22.other_ref = bf16[272,384]{1,0:T(8,128)(2,1)S(1)} collective-permute-done((bf16[272,384]{1,0:T(8,128)(2,1)S(1)}, bf16[272,384]{1,0:T(8,128)(2,1)S(1)}, u32[]{:S(2)}, u32[]{:S(2)}) %collective-permute-start.22) | collective-permute-done | bytes 208928 | tf_op jit(solution)/shard_map/ppermute | solution.py:624
  (47 shorter events, 19.8 us)
Async XLA Ops:
  2.0 5.0 %collective-permute-start = (bf16[8,1792]{1,0:T(8,128)(2,1)S(1)}, bf16[8,1792]{1,0:T(8,128)(2,1)S(1)}, u32[]{:S(2)}, u32[]{:S(2)}) collective-permute-start(bf16[8,1792]{1,0:T(8,128)(2,1)S(1)} %get-tuple-element.73), channel_id=1, source_target_pairs={{0,1},{1,0},{2,3},{3,2},{4,5},{5,4},{6,7},{7,6},{8,9},{9,8},{10,11... | collective-permute-start | bytes 86024 | tf_op jit(solution)/shard_map/ppermute | solution.py:637
  4.0 8.5 %collective-permute-start.2 = (bf16[2,128,384]{2,1,0:T(8,128)(2,1)S(1)}, bf16[2,128,384]{2,1,0:T(8,128)(2,1)S(1)}, u32[]{:S(2)}, u32[]{:S(2)}) collective-permute-start(bf16[2,128,384]{2,1,0:T(8,128)(2,1)S(1)} %get-tuple-element.74), channel_id=1, source_target_pairs={{0,4},{4,0},{1,5},{5,1},{2,6},{6,2},{3,7},{7,3},{8,12},{12,8},{9,1... | collective-permute-start | bytes 589832 | tf_op jit(solution)/shard_map/ppermute | solution.py:624
  7.1 5.5 %collective-permute-start.1 = (bf16[2,8,1792]{2,1,0:T(8,128)(2,1)S(1)}, bf16[2,8,1792]{2,1,0:T(8,128)(2,1)S(1)}, u32[]{:S(2)}, u32[]{:S(2)}) collective-permute-start(bf16[2,8,1792]{2,1,0:T(8,128)(2,1)S(1)} %get-tuple-element.139), channel_id=1, source_target_pairs={{0,3},{1,2},{2,1},{3,0},{4,7},{5,6},{6,5},{7,4},{8,11},{9,10},{10,... | collective-permute-start | bytes 172040 | tf_op jit(solution)/shard_map/ppermute | solution.py:637
  12.6 6.0 %collective-permute-start.5 = (bf16[4,8,1792]{2,1,0:T(8,128)(2,1)S(1)}, bf16[4,8,1792]{2,1,0:T(8,128)(2,1)S(1)}, u32[]{:S(2)}, u32[]{:S(2)}) collective-permute-start(bf16[4,8,1792]{2,1,0:T(8,128)(2,1)S(1)} %bitcast.40), channel_id=1, source_target_pairs={{0,16},{16,32},{32,48},{48,0},{1,17},{17,33},{33,49},{49,1},{2,18}... | collective-permute-start | bytes 344072 | tf_op jit(solution)/shard_map/ppermute | solution.py:624
  14.2 6.4 %collective-permute-start.4 = (bf16[4,8,1792]{2,1,0:T(8,128)(2,1)S(1)}, bf16[4,8,1792]{2,1,0:T(8,128)(2,1)S(1)}, u32[]{:S(2)}, u32[]{:S(2)}) collective-permute-start(bf16[4,8,1792]{2,1,0:T(8,128)(2,1)S(1)} %bitcast.41), channel_id=1, source_target_pairs={{0,32},{16,48},{32,0},{48,16},{1,33},{17,49},{33,1},{49,17},{2,34}... | collective-permute-start | bytes 344072 | tf_op jit(solution)/shard_map/ppermute | solution.py:624
  15.1 6.0 %collective-permute-start.3 = (bf16[4,8,1792]{2,1,0:T(8,128)(2,1)S(1)}, bf16[4,8,1792]{2,1,0:T(8,128)(2,1)S(1)}, u32[]{:S(2)}, u32[]{:S(2)}) collective-permute-start(bf16[4,8,1792]{2,1,0:T(8,128)(2,1)S(1)} %bitcast.42), channel_id=1, source_target_pairs={{0,48},{16,0},{32,16},{48,32},{1,49},{17,1},{33,17},{49,33},{2,50}... | collective-permute-start | bytes 344072 | tf_op jit(solution)/shard_map/ppermute | solution.py:624
  17.6 6.9 %collective-permute-start.8 = (bf16[256,384]{1,0:T(8,128)(2,1)S(1)}, bf16[256,384]{1,0:T(8,128)(2,1)S(1)}, u32[]{:S(2)}, u32[]{:S(2)}) collective-permute-start(bf16[256,384]{1,0:T(8,128)(2,1)S(1)} %get-tuple-element.137.token_0.tokens_ref), channel_id=1, source_target_pairs={{0,1},{1,0},{2,3},{3,2},{4,5},{5,4},{6,7},{7,6},{8,9},{9,8},{10,11... | collective-permute-start | bytes 589832 | tf_op jit(solution)/shard_map/ppermute | solution.py:637
  21.2 10.9 %collective-permute-start.6 = (bf16[4,4,8,1792]{3,2,1,0:T(8,128)(2,1)S(1)}, bf16[4,4,8,1792]{3,2,1,0:T(8,128)(2,1)S(1)}, u32[]{:S(2)}, u32[]{:S(2)}) collective-permute-start(bf16[4,4,8,1792]{3,2,1,0:T(8,128)(2,1)S(1)} %get-tuple-element.135), channel_id=1, source_target_pairs={{0,64},{4,68},{64,4},{68,0},{1,65},{5,69},{65,5},{69,1},{2,66},{6,... | collective-permute-start | bytes 1376264 | tf_op jit(solution)/shard_map/ppermute | solution.py:633
  22.5 9.6 %collective-permute-start.7 = (bf16[4,4,8,1792]{3,2,1,0:T(8,128)(2,1)S(1)}, bf16[4,4,8,1792]{3,2,1,0:T(8,128)(2,1)S(1)}, u32[]{:S(2)}, u32[]{:S(2)}) collective-permute-start(bf16[4,4,8,1792]{3,2,1,0:T(8,128)(2,1)S(1)} %get-tuple-element.135), channel_id=1, source_target_pairs={{0,68},{4,64},{64,0},{68,4},{1,69},{5,65},{65,1},{69,5},{2,70},{6,... | collective-permute-start | bytes 1376264 | tf_op jit(solution)/shard_map/ppermute | solution.py:633
  24.6 9.1 %collective-permute-start.9 = (bf16[2,256,384]{2,1,0:T(8,128)(2,1)S(1)}, bf16[2,256,384]{2,1,0:T(8,128)(2,1)S(1)}, u32[]{:S(2)}, u32[]{:S(2)}) collective-permute-start(bf16[2,256,384]{2,1,0:T(8,128)(2,1)S(1)} %pad_maximum_fusion.2), channel_id=1, source_target_pairs={{0,3},{1,2},{2,1},{3,0},{4,7},{5,6},{6,5},{7,4},{8,11},{9,10},{10,... | collective-permute-start | bytes 1179656 | tf_op jit(solution)/shard_map/ppermute | solution.py:637
  33.7 7.3 %collective-permute-start.10 = (bf16[2,4,8,1792]{3,2,1,0:T(8,128)(2,1)S(1)}, bf16[2,4,8,1792]{3,2,1,0:T(8,128)(2,1)S(1)}, u32[]{:S(2)}, u32[]{:S(2)}) collective-permute-start(bf16[2,4,8,1792]{3,2,1,0:T(8,128)(2,1)S(1)} %slice.18), channel_id=1, source_target_pairs={{0,64},{4,68},{64,4},{68,0},{1,65},{5,69},{65,5},{69,1},{2,66},{6,... | collective-permute-start | bytes 688136 | tf_op jit(solution)/shard_map/ppermute | solution.py:633
  33.8 7.2 %collective-permute-start.11 = (bf16[2,4,8,1792]{3,2,1,0:T(8,128)(2,1)S(1)}, bf16[2,4,8,1792]{3,2,1,0:T(8,128)(2,1)S(1)}, u32[]{:S(2)}, u32[]{:S(2)}) collective-permute-start(bf16[2,4,8,1792]{3,2,1,0:T(8,128)(2,1)S(1)} %slice.19), channel_id=1, source_target_pairs={{0,68},{4,64},{64,0},{68,4},{1,69},{5,65},{65,1},{69,5},{2,70},{6,... | collective-permute-start | bytes 688136 | tf_op jit(solution)/shard_map/ppermute | solution.py:633
  41.3 4.0 %collective-permute-start.12 = (bf16[512,1792]{1,0:T(8,128)(2,1)S(1)}, bf16[512,1792]{1,0:T(8,128)(2,1)S(1)}, u32[]{:S(2)}, u32[]{:S(2)}) collective-permute-start(bf16[512,1792]{1,0:T(8,128)(2,1)S(1)} %bitcast.34), channel_id=1, source_target_pairs={{0,8},{8,0},{1,9},{9,1},{2,10},{10,2},{3,11},{11,3},{4,12},{12,4},... | collective-permute-start | bytes 5505032 | tf_op jit(solution)/shard_map/ppermute | solution.py:624
  57.6 9.3 %collective-permute-start.14 = (bf16[512,1024]{1,0:T(8,128)(2,1)S(1)}, bf16[512,1024]{1,0:T(8,128)(2,1)S(1)}, u32[]{:S(2)}, u32[]{:S(2)}) collective-permute-start(bf16[512,1024]{1,0:T(8,128)(2,1)S(1)} %get-tuple-element.100), channel_id=1, source_target_pairs={{0,8},{8,0},{1,9},{9,1},{2,10},{10,2},{3,11},{11,3},{4,12},{12,4},... | collective-permute-start | bytes 3145736 | tf_op jit(solution)/shard_map/ppermute | solution.py:624
  64.6 2.4 %collective-permute-start.13 = (bf16[512,768]{1,0:T(8,128)(2,1)S(1)}, bf16[512,768]{1,0:T(8,128)(2,1)S(1)}, u32[]{:S(2)}, u32[]{:S(2)}) collective-permute-start(bf16[512,768]{1,0:T(8,128)(2,1)S(1)} %get-tuple-element.98), channel_id=1, source_target_pairs={{0,8},{8,0},{1,9},{9,1},{2,10},{10,2},{3,11},{11,3},{4,12},{12,4},... | collective-permute-start | bytes 2359304 | tf_op jit(solution)/shard_map/ppermute | solution.py:624
  67.4 9.4 %collective-permute-start.15 = (bf16[64,1792]{1,0:T(8,128)(2,1)S(1)}, bf16[64,1792]{1,0:T(8,128)(2,1)S(1)}, u32[]{:S(2)}, u32[]{:S(2)}) collective-permute-start(bf16[64,1792]{1,0:T(8,128)(2,1)S(1)} %get-tuple-element.103), channel_id=1, source_target_pairs={{0,64},{4,68},{64,4},{68,0},{1,65},{5,69},{65,5},{69,1},{2,66},{6,... | collective-permute-start | bytes 688136 | tf_op jit(solution)/shard_map/ppermute | solution.py:633
  67.7 9.1 %collective-permute-start.16 = (bf16[64,1792]{1,0:T(8,128)(2,1)S(1)}, bf16[64,1792]{1,0:T(8,128)(2,1)S(1)}, u32[]{:S(2)}, u32[]{:S(2)}) collective-permute-start(bf16[64,1792]{1,0:T(8,128)(2,1)S(1)} %get-tuple-element.104), channel_id=1, source_target_pairs={{0,68},{4,64},{64,0},{68,4},{1,69},{5,65},{65,1},{69,5},{2,70},{6,... | collective-permute-start | bytes 688136 | tf_op jit(solution)/shard_map/ppermute | solution.py:633
  76.9 16.5 %collective-permute-start.17 = (bf16[128,1792]{1,0:T(8,128)(2,1)S(1)}, bf16[128,1792]{1,0:T(8,128)(2,1)S(1)}, u32[]{:S(2)}, u32[]{:S(2)}) collective-permute-start(bf16[128,1792]{1,0:T(8,128)(2,1)S(1)} %get-tuple-element.105), channel_id=1, source_target_pairs={{0,64},{4,68},{64,4},{68,0},{1,65},{5,69},{65,5},{69,1},{2,66},{6,... | collective-permute-start | bytes 1376264 | tf_op jit(solution)/shard_map/ppermute | solution.py:633
  78.1 15.3 %collective-permute-start.18 = (bf16[128,1792]{1,0:T(8,128)(2,1)S(1)}, bf16[128,1792]{1,0:T(8,128)(2,1)S(1)}, u32[]{:S(2)}, u32[]{:S(2)}) collective-permute-start(bf16[128,1792]{1,0:T(8,128)(2,1)S(1)} %get-tuple-element.106), channel_id=1, source_target_pairs={{0,68},{4,64},{64,0},{68,4},{1,69},{5,65},{65,1},{69,5},{2,70},{6,... | collective-permute-start | bytes 1376264 | tf_op jit(solution)/shard_map/ppermute | solution.py:633
  80.2 8.1 %collective-permute-start.19 = (bf16[272,384]{1,0:T(8,128)(2,1)S(1)}, bf16[272,384]{1,0:T(8,128)(2,1)S(1)}, u32[]{:S(2)}, u32[]{:S(2)}) collective-permute-start(bf16[272,384]{1,0:T(8,128)(2,1)S(1)} %get-tuple-element.108), channel_id=1, source_target_pairs={{0,1},{1,0},{2,3},{3,2},{4,5},{5,4},{6,7},{7,6},{8,9},{9,8},{10,11... | collective-permute-start | bytes 626696 | tf_op jit(solution)/shard_map/ppermute | solution.py:637
  80.2 11.2 %collective-permute-start.20 = (bf16[272,384]{1,0:T(8,128)(2,1)S(1)}, bf16[272,384]{1,0:T(8,128)(2,1)S(1)}, u32[]{:S(2)}, u32[]{:S(2)}) collective-permute-start(bf16[272,384]{1,0:T(8,128)(2,1)S(1)} %get-tuple-element.109), channel_id=1, source_target_pairs={{0,3},{1,2},{2,1},{3,0},{4,7},{5,6},{6,5},{7,4},{8,11},{9,10},{10,... | collective-permute-start | bytes 626696 | tf_op jit(solution)/shard_map/ppermute | solution.py:637
  83.2 10.2 %collective-permute-start.21 = (bf16[272,384]{1,0:T(8,128)(2,1)S(1)}, bf16[272,384]{1,0:T(8,128)(2,1)S(1)}, u32[]{:S(2)}, u32[]{:S(2)}) collective-permute-start(bf16[272,384]{1,0:T(8,128)(2,1)S(1)} %get-tuple-element.110), channel_id=1, source_target_pairs={{0,2},{1,3},{2,0},{3,1},{4,6},{5,7},{6,4},{7,5},{8,10},{9,11},{10,... | collective-permute-start | bytes 626696 | tf_op jit(solution)/shard_map/ppermute | solution.py:637
  94.3 14.8 %all-to-all-start = ((bf16[16,8,1792]{2,1,0:T(8,128)(2,1)}), bf16[16,8,1792]{2,1,0:T(8,128)(2,1)S(1)}, u32[]{:S(2)}, u32[]{:S(2)}) async-start(bf16[16,8,1792]{2,1,0:T(8,128)(2,1)} %shard_map.219), calls=%async_computation | async-start | bytes 917504 | tf_op jit(solution)/shard_map/all_to_all | solution.py:775
  100.9 7.4 %collective-permute-start.22 = (bf16[272,384]{1,0:T(8,128)(2,1)S(1)}, bf16[272,384]{1,0:T(8,128)(2,1)S(1)}, u32[]{:S(2)}, u32[]{:S(2)}) collective-permute-start(bf16[272,384]{1,0:T(8,128)(2,1)S(1)} %get-tuple-element.117), channel_id=1, source_target_pairs={{0,4},{4,0},{1,5},{5,1},{2,6},{6,2},{3,7},{7,3},{8,12},{12,8},{9,1... | collective-permute-start | bytes 626696 | tf_op jit(solution)/shard_map/ppermute | solution.py:624
  (1 other events, 4.3 us)

commit v7 on v6

--- a/solution.py
+++ b/solution.py
@@ -282,16 +282,18 @@
     query = query * jnp.asarray(0.125, BF)
     query_ref[...] = query
     weights_scr[...] = jnp.zeros_like(weights_scr)
+    ones = jnp.ones((16, length), BF)
     for head in range(HEADS):
         tile = slice(head // 2 * 128, head // 2 * 128 + 128)
         cut = slice(head * 64, head * 64 + 64)
         scores = dot_nt(keys_ref[:, tile], one_head(query[:, tile], head))
         exponent = jnp.exp(scores - jnp.max(scores, axis=0, keepdims=True))
-        weight = 1.0 / column_sum(exponent)
-        weights_scr[head : head + 1, :] = weight
         exponent = exponent.astype(BF)
         exponent_ref[head] = exponent
-        attended_t[cut, :] = dot(values_t[cut, :], exponent) * weight
+        product = dot(jnp.concatenate([values_t[cut, :], ones], axis=0), exponent)
+        weight = 1.0 / product[64:65]
+        weights_scr[head : head + 1, :] = weight
+        attended_t[cut, :] = product[:64] * weight
 
 
 def forward_part(

time: 111 us -> 111 us (level)
  no operation moved by 1% of the time
where the time goes in v7:
time: 111 us; the launch traced here: 110 us
  starting transfers between devices  43 us (39%)
  waiting for transfers between devices  40.3 us (36%)
  Pallas kernels  24.7 us (22%)
  other arithmetic  1.41 us (1%)
    pallas_call x10, Pallas kernels, call(): pl.pallas_call(kernel, out_shape=out_shape, in_specs=[pl.BlockSpec(memory...  24.7 us
    ppermute x8, waiting for transfers between devices, shift_x(): return lax.ppermute(array, X, moves)  14.5 us
    ppermute x8, waiting for transfers between devices, shift(): lax.ppermute(array, axis, [(i, (i + step) % size) for i in range(size)])  14 us
    ppermute x8, starting transfers between devices, shift_x(): return lax.ppermute(array, X, moves)  13.3 us
    ppermute x7, starting transfers between devices, trade(): return lax.ppermute(array, 'z', [(i, i ^ bits) for i in range(4)])  12.9 us
    ppermute x7, waiting for transfers between devices, trade(): return lax.ppermute(array, 'z', [(i, i ^ bits) for i in range(4)])  11.8 us
    ppermute x8, starting transfers between devices, shift(): lax.ppermute(array, axis, [(i, (i + step) % size) for i in range(size)])  10.6 us
    all_to_all x1, starting transfers between devices, body(): pieces = lax.all_to_all(shares, ('y', 'z'), 0, 0, tiled=True)  6.26 us
  transfers between devices with their start and end apart: 24, of which 14 were waited for; matrix products, arithmetic and copies ran while one was open for 1% of the time, Pallas kernels for 8%

profile of v7, /device:TPU:8, one launch (start us, length us, event | category | flops | bytes accessed | tf_op | source)
XLA Modules:
  0.0 110.2 jit_solution(1541340399030007937)
XLA Ops:
  2.0 2.0 %collective-permute-start = (bf16[8,1792]{1,0:T(8,128)(2,1)S(1)}, bf16[8,1792]{1,0:T(8,128)(2,1)S(1)}, u32[]{:S(2)}, u32[]{:S(2)}) collective-permute-start(bf16[8,1792]{1,0:T(8,128)(2,1)S(1)} %get-tuple-element.73), channel_id=1, source_target_pairs={{0,1},{1,0},{2,3},{3,2},{4,5},{5,4},{6,7},{7,6},{8,9},{9,8},{10,11... | collective-permute-start | bytes 86024 | tf_op jit(solution)/shard_map/ppermute | solution.py:639
  4.0 3.0 %collective-permute-start.2 = (bf16[2,128,384]{2,1,0:T(8,128)(2,1)S(1)}, bf16[2,128,384]{2,1,0:T(8,128)(2,1)S(1)}, u32[]{:S(2)}, u32[]{:S(2)}) collective-permute-start(bf16[2,128,384]{2,1,0:T(8,128)(2,1)S(1)} %get-tuple-element.74), channel_id=1, source_target_pairs={{0,4},{4,0},{1,5},{5,1},{2,6},{6,2},{3,7},{7,3},{8,12},{12,8},{9,1... | collective-permute-start | bytes 589832 | tf_op jit(solution)/shard_map/ppermute | solution.py:626
  7.1 3.0 %collective-permute-start.1 = (bf16[2,8,1792]{2,1,0:T(8,128)(2,1)S(1)}, bf16[2,8,1792]{2,1,0:T(8,128)(2,1)S(1)}, u32[]{:S(2)}, u32[]{:S(2)}) collective-permute-start(bf16[2,8,1792]{2,1,0:T(8,128)(2,1)S(1)} %get-tuple-element.139), channel_id=1, source_target_pairs={{0,3},{1,2},{2,1},{3,0},{4,7},{5,6},{6,5},{7,4},{8,11},{9,10},{10,... | collective-permute-start | bytes 172040 | tf_op jit(solution)/shard_map/ppermute | solution.py:639
  12.6 1.6 %collective-permute-start.5 = (bf16[4,8,1792]{2,1,0:T(8,128)(2,1)S(1)}, bf16[4,8,1792]{2,1,0:T(8,128)(2,1)S(1)}, u32[]{:S(2)}, u32[]{:S(2)}) collective-permute-start(bf16[4,8,1792]{2,1,0:T(8,128)(2,1)S(1)} %bitcast.40), channel_id=1, source_target_pairs={{0,16},{16,32},{32,48},{48,0},{1,17},{17,33},{33,49},{49,1},{2,18}... | collective-permute-start | bytes 344072 | tf_op jit(solution)/shard_map/ppermute | solution.py:626
  15.1 2.4 %collective-permute-start.3 = (bf16[4,8,1792]{2,1,0:T(8,128)(2,1)S(1)}, bf16[4,8,1792]{2,1,0:T(8,128)(2,1)S(1)}, u32[]{:S(2)}, u32[]{:S(2)}) collective-permute-start(bf16[4,8,1792]{2,1,0:T(8,128)(2,1)S(1)} %bitcast.42), channel_id=1, source_target_pairs={{0,48},{16,0},{32,16},{48,32},{1,49},{17,1},{33,17},{49,33},{2,50}... | collective-permute-start | bytes 344072 | tf_op jit(solution)/shard_map/ppermute | solution.py:626
  18.6 2.0 %collective-permute-done.4 = bf16[4,8,1792]{2,1,0:T(8,128)(2,1)S(1)} collective-permute-done((bf16[4,8,1792]{2,1,0:T(8,128)(2,1)S(1)}, bf16[4,8,1792]{2,1,0:T(8,128)(2,1)S(1)}, u32[]{:S(2)}, u32[]{:S(2)}) %collective-permute-start.4) | collective-permute-done | bytes 114720 | tf_op jit(solution)/shard_map/ppermute | solution.py:626
  22.5 2.0 %collective-permute-start.7 = (bf16[4,4,8,1792]{3,2,1,0:T(8,128)(2,1)S(1)}, bf16[4,4,8,1792]{3,2,1,0:T(8,128)(2,1)S(1)}, u32[]{:S(2)}, u32[]{:S(2)}) collective-permute-start(bf16[4,4,8,1792]{3,2,1,0:T(8,128)(2,1)S(1)} %get-tuple-element.135), channel_id=1, source_target_pairs={{0,68},{4,64},{64,0},{68,4},{1,69},{5,65},{65,1},{69,5},{2,70},{6,... | collective-permute-start | bytes 1376264 | tf_op jit(solution)/shard_map/ppermute | solution.py:635
  24.6 3.0 %collective-permute-start.9 = (bf16[2,256,384]{2,1,0:T(8,128)(2,1)S(1)}, bf16[2,256,384]{2,1,0:T(8,128)(2,1)S(1)}, u32[]{:S(2)}, u32[]{:S(2)}) collective-permute-start(bf16[2,256,384]{2,1,0:T(8,128)(2,1)S(1)} %pad_maximum_fusion.2), channel_id=1, source_target_pairs={{0,3},{1,2},{2,1},{3,0},{4,7},{5,6},{6,5},{7,4},{8,11},{9,10},{10,... | collective-permute-start | bytes 1179656 | tf_op jit(solution)/shard_map/ppermute | solution.py:639
  27.7 4.5 %collective-permute-done.6 = bf16[4,4,8,1792]{3,2,1,0:T(8,128)(2,1)S(1)} collective-permute-done((bf16[4,4,8,1792]{3,2,1,0:T(8,128)(2,1)S(1)}, bf16[4,4,8,1792]{3,2,1,0:T(8,128)(2,1)S(1)}, u32[]{:S(2)}, u32[]{:S(2)}) %collective-permute-start.6) | collective-permute-done | bytes 458784 | tf_op jit(solution)/shard_map/ppermute | solution.py:635
  33.8 3.2 %collective-permute-start.11 = (bf16[2,4,8,1792]{3,2,1,0:T(8,128)(2,1)S(1)}, bf16[2,4,8,1792]{3,2,1,0:T(8,128)(2,1)S(1)}, u32[]{:S(2)}, u32[]{:S(2)}) collective-permute-start(bf16[2,4,8,1792]{3,2,1,0:T(8,128)(2,1)S(1)} %slice.19), channel_id=1, source_target_pairs={{0,68},{4,64},{64,0},{68,4},{1,69},{5,65},{65,1},{69,5},{2,70},{6,... | collective-permute-start | bytes 688136 | tf_op jit(solution)/shard_map/ppermute | solution.py:635
  37.0 4.0 %collective-permute-done.10 = bf16[2,4,8,1792]{3,2,1,0:T(8,128)(2,1)S(1)} collective-permute-done((bf16[2,4,8,1792]{3,2,1,0:T(8,128)(2,1)S(1)}, bf16[2,4,8,1792]{3,2,1,0:T(8,128)(2,1)S(1)}, u32[]{:S(2)}, u32[]{:S(2)}) %collective-permute-start.10) | collective-permute-done | bytes 229408 | tf_op jit(solution)/shard_map/ppermute | solution.py:635
  42.5 2.9 %collective-permute-done.12.far_ref = bf16[512,1792]{1,0:T(8,128)(2,1)S(1)} collective-permute-done((bf16[512,1792]{1,0:T(8,128)(2,1)S(1)}, bf16[512,1792]{1,0:T(8,128)(2,1)S(1)}, u32[]{:S(2)}, u32[]{:S(2)}) %collective-permute-start.12) | collective-permute-done | bytes 1835040 | tf_op jit(solution)/shard_map/ppermute | solution.py:626
  45.4 12.4 %shard_map.213 = (bf16[384,1152]{1,0:T(8,128)(2,1)S(1)}, bf16[256,384]{1,0:T(8,128)(2,1)S(1)}, bf16[1024,384]{1,0:T(8,128)(2,1)S(1)}, bf16[1024,384]{1,0:T(8,128...) custom-call(bf16[512,1792]{1,0:T(8,128)(2,1)S(1)} %bitcast.35, ...), custom_call_target="tpu_custom_call" | custom-call | tf_op jit(solution)/shard_map/pallas_call | solution.py:661
  58.2 6.5 %shard_map.214 = (bf16[272,384]{1,0:T(8,128)(2,1)S(1)}, bf16[272,384]{1,0:T(8,128)(2,1)S(1)}, bf16[272,384]{1,0:T(8,128)(2,1)S(1)}, bf16[272,384]{1,0:T(8,128)(2...) custom-call(f32[1024,384]{1,0:T(8,128)S(1)} %get-tuple-element.84.normed_ref, ...), custom_call_target="tpu_custom_call" | custom-call | tf_op jit(solution)/shard_map/pallas_call | solution.py:661
  65.2 1.9 %collective-permute-done.13.back_one = bf16[512,768]{1,0:T(8,128)(2,1)S(1)} collective-permute-done((bf16[512,768]{1,0:T(8,128)(2,1)S(1)}, bf16[512,768]{1,0:T(8,128)(2,1)S(1)}, u32[]{:S(2)}, u32[]{:S(2)}) %collective-permute-start.13) | collective-permute-done | bytes 786464 | tf_op jit(solution)/shard_map/ppermute | solution.py:626
  67.9 3.0 %collective-permute-start.16 = (bf16[64,1792]{1,0:T(8,128)(2,1)S(1)}, bf16[64,1792]{1,0:T(8,128)(2,1)S(1)}, u32[]{:S(2)}, u32[]{:S(2)}) collective-permute-start(bf16[64,1792]{1,0:T(8,128)(2,1)S(1)} %get-tuple-element.104), channel_id=1, source_target_pairs={{0,68},{4,64},{64,0},{68,4},{1,69},{5,65},{65,1},{69,5},{2,70},{6,... | collective-permute-start | bytes 688136 | tf_op jit(solution)/shard_map/ppermute | solution.py:635
  70.9 6.0 %collective-permute-done.15.up_ref = bf16[64,1792]{1,0:T(8,128)(2,1)S(1)} collective-permute-done((bf16[64,1792]{1,0:T(8,128)(2,1)S(1)}, bf16[64,1792]{1,0:T(8,128)(2,1)S(1)}, u32[]{:S(2)}, u32[]{:S(2)}) %collective-permute-start.15) | collective-permute-done | bytes 229408 | tf_op jit(solution)/shard_map/ppermute | solution.py:635
  78.3 2.1 %collective-permute-start.18 = (bf16[128,1792]{1,0:T(8,128)(2,1)S(1)}, bf16[128,1792]{1,0:T(8,128)(2,1)S(1)}, u32[]{:S(2)}, u32[]{:S(2)}) collective-permute-start(bf16[128,1792]{1,0:T(8,128)(2,1)S(1)} %get-tuple-element.106), channel_id=1, source_target_pairs={{0,68},{4,64},{64,0},{68,4},{1,69},{5,65},{65,1},{69,5},{2,70},{6,... | collective-permute-start | bytes 1376264 | tf_op jit(solution)/shard_map/ppermute | solution.py:635
  80.4 3.0 %collective-permute-start.20 = (bf16[272,384]{1,0:T(8,128)(2,1)S(1)}, bf16[272,384]{1,0:T(8,128)(2,1)S(1)}, u32[]{:S(2)}, u32[]{:S(2)}) collective-permute-start(bf16[272,384]{1,0:T(8,128)(2,1)S(1)} %get-tuple-element.109), channel_id=1, source_target_pairs={{0,3},{1,2},{2,1},{3,0},{4,7},{5,6},{6,5},{7,4},{8,11},{9,10},{10,... | collective-permute-start | bytes 626696 | tf_op jit(solution)/shard_map/ppermute | solution.py:639
  84.8 3.7 %collective-permute-done.19.piece_1 = bf16[272,384]{1,0:T(8,128)(2,1)S(1)} collective-permute-done((bf16[272,384]{1,0:T(8,128)(2,1)S(1)}, bf16[272,384]{1,0:T(8,128)(2,1)S(1)}, u32[]{:S(2)}, u32[]{:S(2)}) %collective-permute-start.19) | collective-permute-done | bytes 208928 | tf_op jit(solution)/shard_map/ppermute | solution.py:639
  88.5 3.1 %collective-permute-done.20.piece_2 = bf16[272,384]{1,0:T(8,128)(2,1)S(1)} collective-permute-done((bf16[272,384]{1,0:T(8,128)(2,1)S(1)}, bf16[272,384]{1,0:T(8,128)(2,1)S(1)}, u32[]{:S(2)}, u32[]{:S(2)}) %collective-permute-start.20) | collective-permute-done | bytes 208928 | tf_op jit(solution)/shard_map/ppermute | solution.py:639
  91.6 1.9 %collective-permute-done.21.piece_3 = bf16[272,384]{1,0:T(8,128)(2,1)S(1)} collective-permute-done((bf16[272,384]{1,0:T(8,128)(2,1)S(1)}, bf16[272,384]{1,0:T(8,128)(2,1)S(1)}, u32[]{:S(2)}, u32[]{:S(2)}) %collective-permute-start.21) | collective-permute-done | bytes 208928 | tf_op jit(solution)/shard_map/ppermute | solution.py:639
  94.5 6.3 %all-to-all-start = ((bf16[16,8,1792]{2,1,0:T(8,128)(2,1)}), bf16[16,8,1792]{2,1,0:T(8,128)(2,1)S(1)}, u32[]{:S(2)}, u32[]{:S(2)}) async-start(bf16[16,8,1792]{2,1,0:T(8,128)(2,1)} %shard_map.219), calls=%async_computation | async-start | bytes 917504 | tf_op jit(solution)/shard_map/all_to_all | solution.py:777
  102.5 6.0 %collective-permute-done.22.other_ref = bf16[272,384]{1,0:T(8,128)(2,1)S(1)} collective-permute-done((bf16[272,384]{1,0:T(8,128)(2,1)S(1)}, bf16[272,384]{1,0:T(8,128)(2,1)S(1)}, u32[]{:S(2)}, u32[]{:S(2)}) %collective-permute-start.22) | collective-permute-done | bytes 208928 | tf_op jit(solution)/shard_map/ppermute | solution.py:626
  (47 shorter events, 19.8 us)
Async XLA Ops:
  2.0 5.0 %collective-permute-start = (bf16[8,1792]{1,0:T(8,128)(2,1)S(1)}, bf16[8,1792]{1,0:T(8,128)(2,1)S(1)}, u32[]{:S(2)}, u32[]{:S(2)}) collective-permute-start(bf16[8,1792]{1,0:T(8,128)(2,1)S(1)} %get-tuple-element.73), channel_id=1, source_target_pairs={{0,1},{1,0},{2,3},{3,2},{4,5},{5,4},{6,7},{7,6},{8,9},{9,8},{10,11... | collective-permute-start | bytes 86024 | tf_op jit(solution)/shard_map/ppermute | solution.py:639
  4.0 8.5 %collective-permute-start.2 = (bf16[2,128,384]{2,1,0:T(8,128)(2,1)S(1)}, bf16[2,128,384]{2,1,0:T(8,128)(2,1)S(1)}, u32[]{:S(2)}, u32[]{:S(2)}) collective-permute-start(bf16[2,128,384]{2,1,0:T(8,128)(2,1)S(1)} %get-tuple-element.74), channel_id=1, source_target_pairs={{0,4},{4,0},{1,5},{5,1},{2,6},{6,2},{3,7},{7,3},{8,12},{12,8},{9,1... | collective-permute-start | bytes 589832 | tf_op jit(solution)/shard_map/ppermute | solution.py:626
  7.1 5.5 %collective-permute-start.1 = (bf16[2,8,1792]{2,1,0:T(8,128)(2,1)S(1)}, bf16[2,8,1792]{2,1,0:T(8,128)(2,1)S(1)}, u32[]{:S(2)}, u32[]{:S(2)}) collective-permute-start(bf16[2,8,1792]{2,1,0:T(8,128)(2,1)S(1)} %get-tuple-element.139), channel_id=1, source_target_pairs={{0,3},{1,2},{2,1},{3,0},{4,7},{5,6},{6,5},{7,4},{8,11},{9,10},{10,... | collective-permute-start | bytes 172040 | tf_op jit(solution)/shard_map/ppermute | solution.py:639
  12.6 6.0 %collective-permute-start.5 = (bf16[4,8,1792]{2,1,0:T(8,128)(2,1)S(1)}, bf16[4,8,1792]{2,1,0:T(8,128)(2,1)S(1)}, u32[]{:S(2)}, u32[]{:S(2)}) collective-permute-start(bf16[4,8,1792]{2,1,0:T(8,128)(2,1)S(1)} %bitcast.40), channel_id=1, source_target_pairs={{0,16},{16,32},{32,48},{48,0},{1,17},{17,33},{33,49},{49,1},{2,18}... | collective-permute-start | bytes 344072 | tf_op jit(solution)/shard_map/ppermute | solution.py:626
  14.2 6.4 %collective-permute-start.4 = (bf16[4,8,1792]{2,1,0:T(8,128)(2,1)S(1)}, bf16[4,8,1792]{2,1,0:T(8,128)(2,1)S(1)}, u32[]{:S(2)}, u32[]{:S(2)}) collective-permute-start(bf16[4,8,1792]{2,1,0:T(8,128)(2,1)S(1)} %bitcast.41), channel_id=1, source_target_pairs={{0,32},{16,48},{32,0},{48,16},{1,33},{17,49},{33,1},{49,17},{2,34}... | collective-permute-start | bytes 344072 | tf_op jit(solution)/shard_map/ppermute | solution.py:626
  15.1 6.0 %collective-permute-start.3 = (bf16[4,8,1792]{2,1,0:T(8,128)(2,1)S(1)}, bf16[4,8,1792]{2,1,0:T(8,128)(2,1)S(1)}, u32[]{:S(2)}, u32[]{:S(2)}) collective-permute-start(bf16[4,8,1792]{2,1,0:T(8,128)(2,1)S(1)} %bitcast.42), channel_id=1, source_target_pairs={{0,48},{16,0},{32,16},{48,32},{1,49},{17,1},{33,17},{49,33},{2,50}... | collective-permute-start | bytes 344072 | tf_op jit(solution)/shard_map/ppermute | solution.py:626
  17.6 6.9 %collective-permute-start.8 = (bf16[256,384]{1,0:T(8,128)(2,1)S(1)}, bf16[256,384]{1,0:T(8,128)(2,1)S(1)}, u32[]{:S(2)}, u32[]{:S(2)}) collective-permute-start(bf16[256,384]{1,0:T(8,128)(2,1)S(1)} %get-tuple-element.137.token_0.tokens_ref), channel_id=1, source_target_pairs={{0,1},{1,0},{2,3},{3,2},{4,5},{5,4},{6,7},{7,6},{8,9},{9,8},{10,11... | collective-permute-start | bytes 589832 | tf_op jit(solution)/shard_map/ppermute | solution.py:639
  21.2 10.9 %collective-permute-start.6 = (bf16[4,4,8,1792]{3,2,1,0:T(8,128)(2,1)S(1)}, bf16[4,4,8,1792]{3,2,1,0:T(8,128)(2,1)S(1)}, u32[]{:S(2)}, u32[]{:S(2)}) collective-permute-start(bf16[4,4,8,1792]{3,2,1,0:T(8,128)(2,1)S(1)} %get-tuple-element.135), channel_id=1, source_target_pairs={{0,64},{4,68},{64,4},{68,0},{1,65},{5,69},{65,5},{69,1},{2,66},{6,... | collective-permute-start | bytes 1376264 | tf_op jit(solution)/shard_map/ppermute | solution.py:635
  22.5 9.6 %collective-permute-start.7 = (bf16[4,4,8,1792]{3,2,1,0:T(8,128)(2,1)S(1)}, bf16[4,4,8,1792]{3,2,1,0:T(8,128)(2,1)S(1)}, u32[]{:S(2)}, u32[]{:S(2)}) collective-permute-start(bf16[4,4,8,1792]{3,2,1,0:T(8,128)(2,1)S(1)} %get-tuple-element.135), channel_id=1, source_target_pairs={{0,68},{4,64},{64,0},{68,4},{1,69},{5,65},{65,1},{69,5},{2,70},{6,... | collective-permute-start | bytes 1376264 | tf_op jit(solution)/shard_map/ppermute | solution.py:635
  24.6 9.1 %collective-permute-start.9 = (bf16[2,256,384]{2,1,0:T(8,128)(2,1)S(1)}, bf16[2,256,384]{2,1,0:T(8,128)(2,1)S(1)}, u32[]{:S(2)}, u32[]{:S(2)}) collective-permute-start(bf16[2,256,384]{2,1,0:T(8,128)(2,1)S(1)} %pad_maximum_fusion.2), channel_id=1, source_target_pairs={{0,3},{1,2},{2,1},{3,0},{4,7},{5,6},{6,5},{7,4},{8,11},{9,10},{10,... | collective-permute-start | bytes 1179656 | tf_op jit(solution)/shard_map/ppermute | solution.py:639
  33.7 7.3 %collective-permute-start.10 = (bf16[2,4,8,1792]{3,2,1,0:T(8,128)(2,1)S(1)}, bf16[2,4,8,1792]{3,2,1,0:T(8,128)(2,1)S(1)}, u32[]{:S(2)}, u32[]{:S(2)}) collective-permute-start(bf16[2,4,8,1792]{3,2,1,0:T(8,128)(2,1)S(1)} %slice.18), channel_id=1, source_target_pairs={{0,64},{4,68},{64,4},{68,0},{1,65},{5,69},{65,5},{69,1},{2,66},{6,... | collective-permute-start | bytes 688136 | tf_op jit(solution)/shard_map/ppermute | solution.py:635
  33.8 7.2 %collective-permute-start.11 = (bf16[2,4,8,1792]{3,2,1,0:T(8,128)(2,1)S(1)}, bf16[2,4,8,1792]{3,2,1,0:T(8,128)(2,1)S(1)}, u32[]{:S(2)}, u32[]{:S(2)}) collective-permute-start(bf16[2,4,8,1792]{3,2,1,0:T(8,128)(2,1)S(1)} %slice.19), channel_id=1, source_target_pairs={{0,68},{4,64},{64,0},{68,4},{1,69},{5,65},{65,1},{69,5},{2,70},{6,... | collective-permute-start | bytes 688136 | tf_op jit(solution)/shard_map/ppermute | solution.py:635
  41.3 4.0 %collective-permute-start.12 = (bf16[512,1792]{1,0:T(8,128)(2,1)S(1)}, bf16[512,1792]{1,0:T(8,128)(2,1)S(1)}, u32[]{:S(2)}, u32[]{:S(2)}) collective-permute-start(bf16[512,1792]{1,0:T(8,128)(2,1)S(1)} %bitcast.34), channel_id=1, source_target_pairs={{0,8},{8,0},{1,9},{9,1},{2,10},{10,2},{3,11},{11,3},{4,12},{12,4},... | collective-permute-start | bytes 5505032 | tf_op jit(solution)/shard_map/ppermute | solution.py:626
  57.8 9.3 %collective-permute-start.14 = (bf16[512,1024]{1,0:T(8,128)(2,1)S(1)}, bf16[512,1024]{1,0:T(8,128)(2,1)S(1)}, u32[]{:S(2)}, u32[]{:S(2)}) collective-permute-start(bf16[512,1024]{1,0:T(8,128)(2,1)S(1)} %get-tuple-element.100), channel_id=1, source_target_pairs={{0,8},{8,0},{1,9},{9,1},{2,10},{10,2},{3,11},{11,3},{4,12},{12,4},... | collective-permute-start | bytes 3145736 | tf_op jit(solution)/shard_map/ppermute | solution.py:626
  64.7 2.4 %collective-permute-start.13 = (bf16[512,768]{1,0:T(8,128)(2,1)S(1)}, bf16[512,768]{1,0:T(8,128)(2,1)S(1)}, u32[]{:S(2)}, u32[]{:S(2)}) collective-permute-start(bf16[512,768]{1,0:T(8,128)(2,1)S(1)} %get-tuple-element.98), channel_id=1, source_target_pairs={{0,8},{8,0},{1,9},{9,1},{2,10},{10,2},{3,11},{11,3},{4,12},{12,4},... | collective-permute-start | bytes 2359304 | tf_op jit(solution)/shard_map/ppermute | solution.py:626
  67.5 9.4 %collective-permute-start.15 = (bf16[64,1792]{1,0:T(8,128)(2,1)S(1)}, bf16[64,1792]{1,0:T(8,128)(2,1)S(1)}, u32[]{:S(2)}, u32[]{:S(2)}) collective-permute-start(bf16[64,1792]{1,0:T(8,128)(2,1)S(1)} %get-tuple-element.103), channel_id=1, source_target_pairs={{0,64},{4,68},{64,4},{68,0},{1,65},{5,69},{65,5},{69,1},{2,66},{6,... | collective-permute-start | bytes 688136 | tf_op jit(solution)/shard_map/ppermute | solution.py:635
  67.9 9.1 %collective-permute-start.16 = (bf16[64,1792]{1,0:T(8,128)(2,1)S(1)}, bf16[64,1792]{1,0:T(8,128)(2,1)S(1)}, u32[]{:S(2)}, u32[]{:S(2)}) collective-permute-start(bf16[64,1792]{1,0:T(8,128)(2,1)S(1)} %get-tuple-element.104), channel_id=1, source_target_pairs={{0,68},{4,64},{64,0},{68,4},{1,69},{5,65},{65,1},{69,5},{2,70},{6,... | collective-permute-start | bytes 688136 | tf_op jit(solution)/shard_map/ppermute | solution.py:635
  77.1 16.5 %collective-permute-start.17 = (bf16[128,1792]{1,0:T(8,128)(2,1)S(1)}, bf16[128,1792]{1,0:T(8,128)(2,1)S(1)}, u32[]{:S(2)}, u32[]{:S(2)}) collective-permute-start(bf16[128,1792]{1,0:T(8,128)(2,1)S(1)} %get-tuple-element.105), channel_id=1, source_target_pairs={{0,64},{4,68},{64,4},{68,0},{1,65},{5,69},{65,5},{69,1},{2,66},{6,... | collective-permute-start | bytes 1376264 | tf_op jit(solution)/shard_map/ppermute | solution.py:635
  78.3 15.3 %collective-permute-start.18 = (bf16[128,1792]{1,0:T(8,128)(2,1)S(1)}, bf16[128,1792]{1,0:T(8,128)(2,1)S(1)}, u32[]{:S(2)}, u32[]{:S(2)}) collective-permute-start(bf16[128,1792]{1,0:T(8,128)(2,1)S(1)} %get-tuple-element.106), channel_id=1, source_target_pairs={{0,68},{4,64},{64,0},{68,4},{1,69},{5,65},{65,1},{69,5},{2,70},{6,... | collective-permute-start | bytes 1376264 | tf_op jit(solution)/shard_map/ppermute | solution.py:635
  80.4 8.1 %collective-permute-start.19 = (bf16[272,384]{1,0:T(8,128)(2,1)S(1)}, bf16[272,384]{1,0:T(8,128)(2,1)S(1)}, u32[]{:S(2)}, u32[]{:S(2)}) collective-permute-start(bf16[272,384]{1,0:T(8,128)(2,1)S(1)} %get-tuple-element.108), channel_id=1, source_target_pairs={{0,1},{1,0},{2,3},{3,2},{4,5},{5,4},{6,7},{7,6},{8,9},{9,8},{10,11... | collective-permute-start | bytes 626696 | tf_op jit(solution)/shard_map/ppermute | solution.py:639
  80.4 11.2 %collective-permute-start.20 = (bf16[272,384]{1,0:T(8,128)(2,1)S(1)}, bf16[272,384]{1,0:T(8,128)(2,1)S(1)}, u32[]{:S(2)}, u32[]{:S(2)}) collective-permute-start(bf16[272,384]{1,0:T(8,128)(2,1)S(1)} %get-tuple-element.109), channel_id=1, source_target_pairs={{0,3},{1,2},{2,1},{3,0},{4,7},{5,6},{6,5},{7,4},{8,11},{9,10},{10,... | collective-permute-start | bytes 626696 | tf_op jit(solution)/shard_map/ppermute | solution.py:639
  83.3 10.2 %collective-permute-start.21 = (bf16[272,384]{1,0:T(8,128)(2,1)S(1)}, bf16[272,384]{1,0:T(8,128)(2,1)S(1)}, u32[]{:S(2)}, u32[]{:S(2)}) collective-permute-start(bf16[272,384]{1,0:T(8,128)(2,1)S(1)} %get-tuple-element.110), channel_id=1, source_target_pairs={{0,2},{1,3},{2,0},{3,1},{4,6},{5,7},{6,4},{7,5},{8,10},{9,11},{10,... | collective-permute-start | bytes 626696 | tf_op jit(solution)/shard_map/ppermute | solution.py:639
  94.5 14.8 %all-to-all-start = ((bf16[16,8,1792]{2,1,0:T(8,128)(2,1)}), bf16[16,8,1792]{2,1,0:T(8,128)(2,1)S(1)}, u32[]{:S(2)}, u32[]{:S(2)}) async-start(bf16[16,8,1792]{2,1,0:T(8,128)(2,1)} %shard_map.219), calls=%async_computation | async-start | bytes 917504 | tf_op jit(solution)/shard_map/all_to_all | solution.py:777
  101.1 7.4 %collective-permute-start.22 = (bf16[272,384]{1,0:T(8,128)(2,1)S(1)}, bf16[272,384]{1,0:T(8,128)(2,1)S(1)}, u32[]{:S(2)}, u32[]{:S(2)}) collective-permute-start(bf16[272,384]{1,0:T(8,128)(2,1)S(1)} %get-tuple-element.117), channel_id=1, source_target_pairs={{0,4},{4,0},{1,5},{5,1},{2,6},{6,2},{3,7},{7,3},{8,12},{12,8},{9,1... | collective-permute-start | bytes 626696 | tf_op jit(solution)/shard_map/ppermute | solution.py:626
  (1 other events, 4.3 us)
